TPU v7x, 128 devices: a whole 4x4x4 slice. The times are simulated.
128 devices in a mesh: gy: 8 (over x, core), gz: 16 (over y, z).
Axes of the slice: x: 4, y: 4, z: 4, core: 2. Of those that a mesh axis runs over, the one named last changes fastest.
Arguments:
- velocity: float32 [3, 768, 12288], P(None, 'gy', 'gz'), may hold values from -250 to 250
- strain: bfloat16 [6, 768, 12288], P(None, 'gy', 'gz'), may hold values from -250 to 250
- cell_height: float32 [768], P('gy'), may hold values from 0.5 to 2
- stencil_reach: int32 [2, 768], P(None, 'gy'), may hold values from 1 to 8, as said below
Outputs:
- coefficient: float32 [768], P('gy')
Inputs may be any that keep to these rules, and one draw needn't show every extreme that they name: `stencil_reach`: in every draw some plane reaches 8 planes on both sides; stencils are cut at the walls by the steps.
All inputs are finite; a program needn't handle non-finite values.
Results may differ from a plain program's by a relative error of at most 0.0003.
Values sent between devices are 32-bit elements; how exact they have to be, the bound alone decides.
No kernel may reach another device: no remote copies, remote signals or barrier semaphores. Data moves between devices by JAX's collectives and lax.ppermute only.
A program may use at most 128 MiB of HBM per device.

v0:
```python
import jax
import jax.numpy as jnp
from jax import lax
from jax.sharding import PartitionSpec as P

NX = 8
HMAX = 8


LEAD_INDEX = (0, 1, 2, 0, 0, 1)
TAIL_INDEX = (0, 1, 2, 1, 2, 2)
TENSOR_WEIGHTS = (1.0, 1.0, 1.0, 2.0, 2.0, 2.0)


def extended(cells, sides, width, closed):
    for axis, dim in sides:
        count = lax.axis_size(axis)
        ends = count if closed else count - 1
        head = lax.slice_in_dim(cells, 0, width, axis=dim)
        tail = lax.slice_in_dim(cells, cells.shape[dim] - width, cells.shape[dim], axis=dim)
        cells = jnp.concatenate(
            [
                lax.ppermute(tail, axis, [(i, (i + 1) % count) for i in range(ends)]),
                cells,
                lax.ppermute(head, axis, [((i + 1) % count, i) for i in range(ends)]),
            ],
            axis=dim,
        )
    return cells


def strain_rate(tensor):
    squares = 2.0 * (tensor[0] * tensor[0] + tensor[1] * tensor[1] + tensor[2] * tensor[2])
    squares = squares + 4.0 * (
        tensor[3] * tensor[3] + tensor[4] * tensor[4] + tensor[5] * tensor[5]
    )
    return jnp.sqrt(squares)


def form_fields(velocity, tensor):
    products = jnp.stack(
        [
            velocity[first_index] * velocity[second_index]
            for first_index, second_index in zip(LEAD_INDEX, TAIL_INDEX)
        ]
    )
    magnitude = strain_rate(tensor)
    return jnp.concatenate([velocity, products, tensor, magnitude[None] * tensor], axis=0)


def streamwise_filter(fields):
    length = fields.shape[-1]
    position = jnp.arange(length, dtype=jnp.int32) % NX
    behind = jnp.where(
        position == 0, jnp.roll(fields, 1 - NX, axis=-1), jnp.roll(fields, 1, axis=-1)
    )
    ahead_cells = jnp.where(
        position == NX - 1, jnp.roll(fields, NX - 1, axis=-1), jnp.roll(fields, -1, axis=-1)
    )
    return 0.25 * behind + 0.5 * fields + 0.25 * ahead_cells


def spanwise_filter(widened):
    return (
        0.25 * widened[..., : -2 * NX] + 0.5 * widened[..., NX:-NX] + 0.25 * widened[..., 2 * NX :]
    )


def band_apply(band_matrix, padded):
    flattened = padded.reshape(padded.shape[0], padded.shape[1], -1)
    result = jnp.einsum("jc,fcm->fjm", band_matrix, flattened, precision=lax.Precision.HIGHEST)
    return result.reshape((padded.shape[0], band_matrix.shape[0]) + padded.shape[2:])


def contraction(filtered, sum_axes):
    velocity_bar = filtered[0:3]
    product_bar = filtered[3:9]
    tensor_bar = filtered[9:15]
    model_bar = filtered[15:21]
    rate_bar = strain_rate(tensor_bar)
    numerator = jnp.zeros(filtered.shape[1:], jnp.float32)
    denominator = jnp.zeros(filtered.shape[1:], jnp.float32)
    for component in range(6):
        leonard = (
            product_bar[component]
            - velocity_bar[LEAD_INDEX[component]] * velocity_bar[TAIL_INDEX[component]]
        )
        model_term = model_bar[component] - 4.0 * rate_bar * tensor_bar[component]
        numerator = numerator + TENSOR_WEIGHTS[component] * leonard * model_term
        denominator = denominator + TENSOR_WEIGHTS[component] * model_term * model_term
    return (jnp.sum(numerator, axis=sum_axes), jnp.sum(denominator, axis=sum_axes))


def local(velocity, strain, cell_height, stencil_reach):
    planes = velocity.shape[1]
    cell_count = velocity.shape[2]
    total_planes = lax.axis_size("gy") * planes
    total_cells = lax.axis_size("gz") * cell_count
    heights = extended(cell_height, (("gy", 0),), HMAX, False)
    offset = lax.axis_index("gy") * planes
    rows_global = offset + jnp.arange(planes, dtype=jnp.int32)
    columns_global = offset - HMAX + jnp.arange(planes + 2 * HMAX, dtype=jnp.int32)
    lowest = jnp.maximum(rows_global - stencil_reach[0], 0)
    highest = jnp.minimum(rows_global + stencil_reach[1], total_planes - 1)
    inside = (columns_global[None, :] >= lowest[:, None]) & (
        columns_global[None, :] <= highest[:, None]
    )
    weights = jnp.where(inside, heights[None, :], 0.0)
    band_matrix = weights / jnp.sum(weights, axis=1, keepdims=True)
    raw_inputs = jnp.concatenate([velocity, strain.astype(jnp.float32)], axis=0)
    fields = form_fields(raw_inputs[0:3], raw_inputs[3:9])
    widened = extended(streamwise_filter(fields), (("gz", 2),), NX, True)
    spanwise = spanwise_filter(widened)
    full_band = lax.all_gather(band_matrix, "gy", axis=0, tiled=True)
    block_count = lax.axis_size("gy")
    grouped = spanwise.reshape(spanwise.shape[0], planes, block_count, cell_count // block_count)
    padded = jnp.pad(
        lax.all_to_all(grouped, "gy", split_axis=2, concat_axis=1, tiled=True),
        ((0, 0), (HMAX, HMAX), (0, 0), (0, 0)),
    )
    sections = [
        band_apply(
            full_band[block_index * planes : (block_index + 1) * planes],
            padded[:, block_index * planes : block_index * planes + planes + 2 * HMAX],
        )
        for block_index in range(block_count)
    ]
    filtered = jnp.concatenate(sections, axis=1)
    numerator, denominator = contraction(filtered, 1)
    numerator = jnp.sum(numerator, axis=1)
    denominator = jnp.sum(denominator, axis=1)
    numerator, denominator = lax.psum((numerator, denominator), ("gy", "gz"))
    whole = numerator / total_cells / (denominator / total_cells + 1e-06)
    return lax.dynamic_slice_in_dim(whole, offset, planes)


def solution(mesh):
    in_specs = (P(None, "gy", "gz"), P(None, "gy", "gz"), P("gy"), P(None, "gy"))
    out_specs = P("gy")
    return jax.shard_map(local, mesh=mesh, in_specs=in_specs, out_specs=out_specs, check_vma=False)
```

profile of v0, /device:TPU:1, one launch (start us, length us, event | category | flops | bytes accessed | tf_op | source)
XLA Modules:
  0.0 296.6 jit_solution(2417976112965533351)
XLA Ops:
  0.0 1.6 copy.30
  1.6 1.2 constant_dynamic-update-slice_fusion
  2.8 0.8 multiply_dynamic-update-slice_fusion.6
  3.6 0.8 multiply_dynamic-update-slice_fusion.5
  4.4 0.8 multiply_dynamic-update-slice_fusion.4
  5.1 0.8 multiply_dynamic-update-slice_fusion.3
  6.0 0.8 multiply_dynamic-update-slice_fusion.2
  6.8 0.8 multiply_dynamic-update-slice_fusion.1
  7.6 0.7 copy.29
  8.3 0.2 convert_element_type.5
  8.4 1.7 convert_dynamic-update-slice_fusion
  10.1 0.3 fusion.16
  10.4 1.6 multiply_dynamic-update-slice_fusion
  12.0 9.7 %fusion.62 = (f32[21,96,767]{1,2,0:T(8,128)S(1)}, f32[21,96,767]{1,2,0:T(8,128)}) fusion(f32[21,96,768]{1,2,0:T(8,128)} %multiply_dynamic-update-slice_fusion), kind=kLoop, calls=%fused_computation.136 | loop fusion | bytes 24740352 | tf_op jit(solution)/shard_map/jit(_roll_static)/slice | solution.py:58
  21.7 10.9 %fusion.65 = (f32[21,96,761]{1,2,0:T(8,128)}, f32[21,96,761]{1,2,0:T(8,128)}) fusion(f32[21,96,768]{1,2,0:T(8,128)} %multiply_dynamic-update-slice_fusion), kind=kLoop, calls=%fused_computation.139 | loop fusion | bytes 24546816 | tf_op jit(solution)/shard_map/jit(_roll_static)/slice | solution.py:58
  32.6 0.9 fusion.64
  33.5 0.9 fusion.63
  34.5 15.5 %fusion.6 = f32[21,96,768]{1,2,0:T(8,128)S(1)} fusion(f32[21,96,7]{1,2,0:T(8,128)S(1)} %get-tuple-element.16, f32[21,96,761]{1,2,0:T(8,128)} %get-tuple-element.18, f32[21,96,767]{1,2,0:T(8,128)} %get-tuple-element.12, f32[21,96,1]{1,2,0:T(1,128)S(1)} %get-tuple-element.14, f32[21,96,761]{1,2,0:T(8,128)} %get-tuple-element.17, ...), kind=kLoop, calls=%fused_computation.9 | loop fusion | flops 17031168 | bytes 37160448 | tf_op jit(solution)/shard_map/add | solution.py:60
  50.0 2.5 collective-permute-start
  52.5 4.7 %collective-permute-start.1 = (f32[21,96,8]{1,2,0:T(8,128)S(1)}, f32[21,96,8]{1,2,0:T(8,128)S(1)}, u32[]{:S(2)}, u32[]{:S(2)}) collective-permute-start(f32[21,96,8]{1,2,0:T(8,128)S(1)} %get-tuple-element.10), channel_id=1, source_target_pairs={{1,0},{2,1},{3,2},{4,3},{5,4},{6,5},{7,6},{8,7},{9,8},{10,9},{11,1... | collective-permute-start | bytes 193544 | tf_op jit(solution)/shard_map/ppermute | solution.py:25
  57.2 2.2 collective-permute-done
  59.4 2.4 fusion.1
  61.8 3.9 %copy.31 = f32[21,96,8,96]{1,3,0,2:T(8,128)} copy(f32[21,96,8,96]{1,3,2,0:T(8,128)S(1)} %bitcast.280) | data formatting | bytes 12386304 | tf_op jit(solution)/shard_map/reshape | solution.py:116
  65.7 6.2 %all-to-all-start = ((f32[21,96,8,96]{1,3,0,2:T(8,128)}), f32[21,96,8,96]{1,3,0,2:T(8,128)}, u32[]{:S(2)}, u32[]{:S(2)}) async-start(f32[21,96,8,96]{1,3,0,2:T(8,128)} %copy.31), calls=%async_computation | async-start | bytes 16515072 | tf_op jit(solution)/shard_map/all_to_all | solution.py:118
  71.9 0.1 fusion.66
  72.0 3.5 %collective-permute-start.2 = (f32[8]{0:T(128)S(1)}, f32[8]{0:T(128)S(1)}, u32[]{:S(2)}, u32[]{:S(2)}) collective-permute-start(f32[8]{0:T(128)S(1)} %get-tuple-element.21), channel_id=1, source_target_pairs={{0,16},{16,32},{32,48},{48,64},{64,80},{80,96},{96,112},{1,17},{17... | collective-permute-start | bytes 104 | tf_op jit(solution)/shard_map/ppermute | solution.py:23
  75.5 1.9 collective-permute-start.3
  77.5 83.5 %collective-permute-done.2 = f32[8]{0:T(128)S(1)} collective-permute-done((f32[8]{0:T(128)S(1)}, f32[8]{0:T(128)S(1)}, u32[]{:S(2)}, u32[]{:S(2)}) %collective-permute-start.2) | collective-permute-done | bytes 64 | tf_op jit(solution)/shard_map/ppermute | solution.py:23
  160.9 2.4 collective-permute-done.3
  163.3 0.1 pad_maximum_fusion.2
  163.4 0.2 select_reduce_fusion
  163.6 0.1 select_divide_fusion
  163.7 11.9 %all_gather.3 = f32[768,112]{1,0:T(8,128)S(1)} all-gather(f32[96,112]{1,0:T(8,128)S(1)} %select_divide_fusion), channel_id=1, replica_groups=mesh['gy'=8,'gz'=16] {'gy'}, dimensions={0}, use_global_device_ids=true | all-gather | bytes 387072 | tf_op jit(solution)/shard_map/all_gather | solution.py:114
  175.6 13.4 %copy.32 = f32[21,8,96,1,96]{2,1,4,0,3:T(8,128)} copy(f32[21,8,96,1,96]{2,4,0,1,3:T(8,128)} %bitcast.3) | data formatting | bytes 12386304 | tf_op jit(solution)/shard_map/all_to_all | solution.py:118
  189.0 9.5 %all_to_all.16 = f32[21,768,1,96]{1,3,0,2:T(8,128)} reshape(f32[21,8,96,1,96]{2,1,4,0,3:T(8,128)} %copy.32) | data formatting | bytes 12386304 | tf_op jit(solution)/shard_map/all_to_all | solution.py:118
  198.5 2.4 convolution_bitcast_fusion
  200.9 2.6 convolution_bitcast_fusion.1
  203.5 2.0 convolution_bitcast_fusion.2
  205.5 2.0 convolution_bitcast_fusion.3
  207.5 2.1 convolution_bitcast_fusion.4
  209.5 2.0 convolution_bitcast_fusion.5
  211.5 2.0 convolution_bitcast_fusion.6
  213.5 1.0 convolution_bitcast_fusion.7
  214.6 8.9 %concatenate.40 = f32[21,768,1,96]{1,3,0,2:T(8,128)} concatenate(f32[21,96,1,96]{1,3,0,2:T(8,128)S(1)} %convolution_bitcast_fusion.7, f32[21,96,1,96]{1,3,0,2:T(8,128)} %convolution_bitcast_fusion.6, f32[21,96,1,96]{1,3,0,2:T(8,128)} %convolution_bitcast_fusion.5, f32[21,96,1,96]{1,3,0,2:T(8,128)} %convolution_bitcast_fusion.4, f32[21,96,1,96]{1,3,0,2:T(8,128)} %convolution_bitcast_fusion.3, ...), dimensions={1} | concatenate | bytes 12386304 | tf_op jit(solution)/shard_map/concatenate | solution.py:128
  223.4 3.3 %fusion.30 = (f32[768]{0:T(1024)S(1)}, f32[768,96]{0,1:T(8,128)S(1)}) fusion(f32[21,768,1,96]{1,3,2,0:T(8,128)} %bitcast.278, f32[21,768,1,96]{1,3,0,2:T(8,128)} %concatenate.40), kind=kLoop, calls=%fused_computation.67 | loop fusion | flops 3906816 | bytes 6491136 | tf_op jit(solution)/shard_map/reduce_sum | solution.py:130
  226.7 2.2 fusion.24
  229.0 67.1 %all-reduce.1 = (f32[768]{0:T(1024)S(1)}, f32[768]{0:T(1024)S(1)}) all-reduce(f32[768]{0:T(1024)S(1)} %fusion.24, f32[768]{0:T(1024)S(1)} %get-tuple-element.7), channel_id=1, replica_groups=mesh['gy'=8,'gz'=16] {'gy','gz'}, use_global_device_ids=true, to_apply=%region_4.5 | all-reduce | flops 1536 | bytes 12288 | tf_op jit(solution)/shard_map/psum | solution.py:132
  296.0 0.6 dynamic_slice.3
  (15 shorter events, 0.1 us)
Async XLA Ops:
  0.0 7.5 %copy-start.1 = (bf16[6,96,768]{2,1,0:T(8,128)(2,1)S(1)}, bf16[6,96,768]{2,1,0:T(8,128)(2,1)}, u32[]{:S(2)}) copy-start(bf16[6,96,768]{2,1,0:T(8,128)(2,1)} %param.5) | copy-start | bytes 2654212
  50.0 9.4 %collective-permute-start = (f32[21,96,8]{1,2,0:T(8,128)S(1)}, f32[21,96,8]{1,2,0:T(8,128)S(1)}, u32[]{:S(2)}, u32[]{:S(2)}) collective-permute-start(f32[21,96,8]{1,2,0:T(8,128)S(1)} %get-tuple-element.9), channel_id=1, source_target_pairs={{0,1},{1,2},{2,3},{3,4},{4,5},{5,6},{6,7},{7,8},{8,9},{9,10},{10,1... | collective-permute-start | bytes 193544 | tf_op jit(solution)/shard_map/ppermute | solution.py:23
  52.5 6.8 %collective-permute-start.1 = (f32[21,96,8]{1,2,0:T(8,128)S(1)}, f32[21,96,8]{1,2,0:T(8,128)S(1)}, u32[]{:S(2)}, u32[]{:S(2)}) collective-permute-start(f32[21,96,8]{1,2,0:T(8,128)S(1)} %get-tuple-element.10), channel_id=1, source_target_pairs={{1,0},{2,1},{3,2},{4,3},{5,4},{6,5},{7,6},{8,7},{9,8},{10,9},{11,1... | collective-permute-start | bytes 193544 | tf_op jit(solution)/shard_map/ppermute | solution.py:25
  65.7 6.2 %copy-start.2 = (f32[96]{0:T(128)S(1)}, f32[96]{0:T(128)}, u32[]{:S(2)}) copy-start(f32[96]{0:T(128)} %param.6) | copy-start | bytes 1156
  65.7 11.7 %copy-start.3 = (s32[2,96]{1,0:T(2,128)S(1)}, s32[2,96]{1,0:T(2,128)}, u32[]{:S(2)}) copy-start(s32[2,96]{1,0:T(2,128)} %param.7) | copy-start | bytes 2308
  65.7 109.9 %all-to-all-start = ((f32[21,96,8,96]{1,3,0,2:T(8,128)}), f32[21,96,8,96]{1,3,0,2:T(8,128)}, u32[]{:S(2)}, u32[]{:S(2)}) async-start(f32[21,96,8,96]{1,3,0,2:T(8,128)} %copy.31), calls=%async_computation | async-start | bytes 16515072 | tf_op jit(solution)/shard_map/all_to_all | solution.py:118
  72.0 89.0 %collective-permute-start.2 = (f32[8]{0:T(128)S(1)}, f32[8]{0:T(128)S(1)}, u32[]{:S(2)}, u32[]{:S(2)}) collective-permute-start(f32[8]{0:T(128)S(1)} %get-tuple-element.21), channel_id=1, source_target_pairs={{0,16},{16,32},{32,48},{48,64},{64,80},{80,96},{96,112},{1,17},{17... | collective-permute-start | bytes 104 | tf_op jit(solution)/shard_map/ppermute | solution.py:23
  75.5 87.8 %collective-permute-start.3 = (f32[8]{0:T(128)S(1)}, f32[8]{0:T(128)S(1)}, u32[]{:S(2)}, u32[]{:S(2)}) collective-permute-start(f32[8]{0:T(128)S(1)} %get-tuple-element.22), channel_id=1, source_target_pairs={{16,0},{32,16},{48,32},{64,48},{80,64},{96,80},{112,96},{17,1},{33... | collective-permute-start | bytes 104 | tf_op jit(solution)/shard_map/ppermute | solution.py:25
  198.5 5.0 %copy-start = (f32[21,768,1,96]{1,3,0,2:T(8,128)S(1)}, f32[21,768,1,96]{1,3,0,2:T(8,128)}, u32[]{:S(2)}) copy-start(f32[21,768,1,96]{1,3,0,2:T(8,128)} %all_to_all.16) | copy-start | bytes 18579460
where the time goes:
time: 297 us
  waiting for transfers between devices  88 us (30%)
  blocking collectives  79 us (27%)
  local copies, waits for them, and re-layouts  62.3 us (21%)
  other arithmetic  32.3 us (11%)
  starting transfers between devices  18.8 us (6%)
  matrix products  16 us (5%)
    ppermute x2, waiting for transfers between devices, extended(): lax.ppermute(tail, axis, [(i, (i + 1) % count) for i in range(ends)])  85.6 us
    psum x1, blocking collectives, local(): numerator, denominator = lax.psum((numerator, denominator), ('gy', 'gz'))  67.1 us
    all_to_all x2, local copies, waits for them, and re-layouts, local(): lax.all_to_all(grouped, 'gy', split_axis=2, concat_axis=1, tiled=True)  22.9 us
    dot_general x8, matrix products, band_apply(): jnp.einsum('jc,fcm->fjm', band_matrix, flattened, precision=lax.Precision...  16 us
    add x1, other arithmetic, streamwise_filter(): return 0.25 * behind + 0.5 * fields + 0.25 * ahead_cells  15.5 us
    all_gather x1, blocking collectives, local(): full_band = lax.all_gather(band_matrix, 'gy', axis=0, tiled=True)  11.9 us
    slice x2, local copies, waits for them, and re-layouts, streamwise_filter(): jnp.roll(fields, NX - 1, axis=-1)  11.9 us
    slice x2, local copies, waits for them, and re-layouts, streamwise_filter(): jnp.roll(fields, -1, axis=-1)  10.6 us
  transfers between devices with their start and end apart: 5, of which 3 were waited for; matrix products, arithmetic and copies ran while one was open for 0% of the time, Pallas kernels for 0%

commit v1 on v0

v1 whole, which is shorter than its diff:
```python
import jax
import jax.numpy as jnp
from jax import lax
from jax.experimental import pallas as pl
from jax.experimental.pallas import tpu as pltpu
from jax.sharding import PartitionSpec as P

NX = 8
HMAX = 8
LANES = 128
LEAD_INDEX = (0, 1, 2, 0, 0, 1)
TAIL_INDEX = (0, 1, 2, 1, 2, 2)
TENSOR_WEIGHTS = (1.0, 1.0, 1.0, 2.0, 2.0, 2.0)
F32 = jnp.float32
BF16 = jnp.bfloat16


def strain_rate(s):
    squares = 2.0 * (s[0] * s[0] + s[1] * s[1] + s[2] * s[2])
    squares = squares + 4.0 * (s[3] * s[3] + s[4] * s[4] + s[5] * s[5])
    return jnp.sqrt(squares)


def lane_iota(shape):
    return lax.broadcasted_iota(jnp.int32, shape, len(shape) - 1)


def rot(x, amount):
    amount = amount % LANES
    return pltpu.roll(x, amount, x.ndim - 1) if amount else x


def pack_span_kernel(vl, vr, sl, sr, near_ref, far_ref):
    rows = vl.shape[1]
    lane = lane_iota((rows, LANES))
    left = jnp.zeros((rows, LANES), F32)
    right = jnp.zeros((rows, LANES), F32)
    for f in range(9):
        a = vl[f] if f < 3 else sl[f - 3].astype(F32)
        b = vr[f] if f < 3 else sr[f - 3].astype(F32)
        here = (lane >= NX * f) & (lane < NX * (f + 1))
        left = jnp.where(here, rot(a, NX * f), left)
        right = jnp.where(here, rot(b, NX * f + NX), right)
    odd = lax.axis_index("gz") % 2 == 1
    near_ref[...] = jnp.where(odd, left, right)
    far_ref[...] = jnp.where(odd, right, left)


def pack_span(velocity, strain):
    rows, cells = velocity.shape[1:]
    last = cells // LANES - 1
    return pl.pallas_call(
        pack_span_kernel,
        grid=(1,),
        in_specs=[
            pl.BlockSpec((3, rows, LANES), lambda i: (0, 0, 0)),
            pl.BlockSpec((3, rows, LANES), lambda i: (0, 0, last)),
            pl.BlockSpec((6, rows, LANES), lambda i: (0, 0, 0)),
            pl.BlockSpec((6, rows, LANES), lambda i: (0, 0, last)),
        ],
        out_specs=[pl.BlockSpec((rows, LANES), lambda i: (0, 0))] * 2,
        out_shape=[jax.ShapeDtypeStruct((rows, LANES), F32)] * 2,
    )(velocity, velocity, strain, strain)


def pack_wall_kernel(vlo, vhi, slo, shi, h_ref, znear, zfar, near_ref, far_ref):
    cells = vlo.shape[2]
    rows = znear.shape[0]
    gz_odd = lax.axis_index("gz") % 2 == 1
    gy_odd = lax.axis_index("gy") % 2 == 1
    tail = 9 * cells
    lane = lane_iota((HMAX, LANES))
    row = lax.broadcasted_iota(jnp.int32, (HMAX, LANES), 0)
    stamp = (row == 0) & (lane >= 9 * NX) & (lane < 10 * NX)
    heights = jnp.broadcast_to(jnp.pad(h_ref[...], ((0, 0), (0, LANES - rows))), (HMAX, LANES))

    def emit(ref, high):
        v = vhi if high else vlo
        s = shi if high else slo
        r0 = rows - HMAX if high else 0
        for f in range(3):
            ref[:, f * cells : (f + 1) * cells] = v[f]
        for f in range(6):
            part = s[f].astype(F32)
            ref[:, (3 + f) * cells : (4 + f) * cells] = part[HMAX:] if high else part[:HMAX]
        zn = znear[r0 : r0 + HMAX, :]
        zf = zfar[r0 : r0 + HMAX, :]
        zl = jnp.where(gz_odd, zn, zf)
        zr = jnp.where(gz_odd, zf, zn)
        ref[:, tail : tail + LANES] = jnp.where(stamp, rot(heights, 9 * NX - r0), zl)
        ref[:, tail + LANES : tail + 2 * LANES] = zr

    @pl.when(gy_odd)
    def _():
        emit(near_ref, False)
        emit(far_ref, True)

    @pl.when(jnp.logical_not(gy_odd))
    def _():
        emit(near_ref, True)
        emit(far_ref, False)


def pack_wall(velocity, strain, heights, znear, zfar):
    rows, cells = velocity.shape[1:]
    width = 9 * cells + 2 * LANES
    return pl.pallas_call(
        pack_wall_kernel,
        grid=(1,),
        in_specs=[
            pl.BlockSpec((3, HMAX, cells), lambda i: (0, 0, 0)),
            pl.BlockSpec((3, HMAX, cells), lambda i: (0, rows // HMAX - 1, 0)),
            pl.BlockSpec((6, 2 * HMAX, cells), lambda i: (0, 0, 0)),
            pl.BlockSpec((6, 2 * HMAX, cells), lambda i: (0, rows // (2 * HMAX) - 1, 0)),
            pl.BlockSpec((1, rows), lambda i: (0, 0)),
            pl.BlockSpec((rows, LANES), lambda i: (0, 0)),
            pl.BlockSpec((rows, LANES), lambda i: (0, 0)),
        ],
        out_specs=[pl.BlockSpec((HMAX, width), lambda i: (0, 0))] * 2,
        out_shape=[jax.ShapeDtypeStruct((HMAX, width), F32)] * 2,
    )(velocity, velocity, strain, strain, heights, znear, zfar)


def split2(x):
    hi = x.astype(BF16)
    return hi, (x - hi.astype(F32)).astype(BF16)


def main_kernel(v_ref, s_ref, h_ref, reach_ref, znear, zfar, ynear, yfar, out_ref, raw, stack, filt, acc):
    rows, cells = v_ref.shape[1:]
    tiles = cells // LANES
    ext = rows + 2 * HMAX
    total_planes = lax.axis_size("gy") * rows
    gy = lax.axis_index("gy")
    gz_odd = lax.axis_index("gz") % 2 == 1
    gy_odd = gy % 2 == 1
    offset = gy * rows
    tail = 9 * cells

    ylo = jnp.where(gy_odd, ynear[:, tail:], yfar[:, tail:])
    yhi = jnp.where(gy_odd, yfar[:, tail:], ynear[:, tail:])

    column = lane_iota((rows, LANES))
    place = jnp.where(column < rows, column, jnp.where(column < rows + HMAX, column - rows - HMAX, column - HMAX))
    row = lax.broadcasted_iota(jnp.int32, (rows, LANES), 0)
    hpad = jnp.pad(h_ref[...], ((0, 0), (0, LANES - rows)))
    hrow = lane_iota((1, LANES))
    hext = jnp.where(
        hrow < rows,
        hpad,
        jnp.where(hrow < rows + HMAX, rot(ylo[:, :LANES], rows - 9 * NX)[0:1], rot(yhi[:, :LANES], rows + HMAX - 9 * NX)[0:1]),
    )
    eye = row == column
    reach = jnp.pad(reach_ref[...].astype(F32), ((0, 0), (0, LANES - rows)))
    down = jnp.sum(jnp.where(eye, reach[0:1], 0.0), axis=1, keepdims=True).astype(jnp.int32)
    up = jnp.sum(jnp.where(eye, reach[1:2], 0.0), axis=1, keepdims=True).astype(jnp.int32)
    inside = (place >= row - down) & (place <= row + up) & (place + offset >= 0) & (place + offset < total_planes)
    inside = inside & (column < ext)
    weights = jnp.where(inside, jnp.broadcast_to(hext, (rows, LANES)), 0.0)
    inv = 1.0 / jnp.sum(weights, axis=1, keepdims=True)
    whi, wlo = split2(weights * inv)
    lhs = jnp.concatenate(
        [jnp.concatenate([whi, whi], axis=1), jnp.concatenate([wlo, jnp.zeros_like(wlo)], axis=1)], axis=0
    )

    zl_own = jnp.where(gz_odd, znear[...], zfar[...])
    zr_own = jnp.where(gz_odd, zfar[...], znear[...])
    zl = jnp.concatenate([zl_own, ylo[:, :LANES], yhi[:, :LANES]], axis=0)
    zr = jnp.concatenate([zr_own, ylo[:, LANES:], yhi[:, LANES:]], axis=0)
    elane = lane_iota((ext, LANES))
    for f in range(9):
        raw[f, 0:rows, 0:cells] = v_ref[f] if f < 3 else s_ref[f - 3].astype(F32)
        near = ynear[:, f * cells : (f + 1) * cells]
        far = yfar[:, f * cells : (f + 1) * cells]
        raw[f, rows : rows + HMAX, 0:cells] = jnp.where(gy_odd, near, far)
        raw[f, rows + HMAX : ext, 0:cells] = jnp.where(gy_odd, far, near)
        edge = jnp.where(elane < NX, rot(zl, -NX * f), jnp.where(elane < 2 * NX, rot(zr, NX - NX * f), 0.0))
        raw[f, 0:ext, cells : cells + LANES] = edge
    stack[...] = jnp.zeros_like(stack)

    def tile_step(t, carry):
        at = pl.ds(pl.multiple_of(t * LANES, LANES), LANES)
        for r in range(0, ext, 16):
            u = [raw[f, r : r + 16, at] for f in range(3)]
            s = [raw[f, r : r + 16, at] for f in range(3, 9)]
            rate = strain_rate(s)
            fields = u + [u[a] * u[b] for a, b in zip(LEAD_INDEX, TAIL_INDEX)] + s + [rate * x for x in s]
            for f in range(21):
                hi, lo = split2(fields[f])
                stack[r : r + 16, f * LANES : (f + 1) * LANES] = hi
                stack[LANES + r : LANES + r + 16, f * LANES : (f + 1) * LANES] = lo
        both = jnp.dot(lhs, stack[...], preferred_element_type=F32)
        merged = both[:rows] + both[rows:]
        for f in range(21):
            filt[f, :, at] = merged[:, f * LANES : (f + 1) * LANES]
        return carry

    lax.fori_loop(0, tiles + 1, tile_step, 0)

    lane8 = lane_iota((HMAX, LANES))
    phase = lane8 % NX
    first, last = phase == 0, phase == NX - 1

    def row_step(r, carry):
        rr = pl.ds(pl.multiple_of(r * HMAX, HMAX), HMAX)
        num = jnp.zeros((HMAX, LANES), F32)
        den = jnp.zeros((HMAX, LANES), F32)
        for t in range(tiles):
            g = []
            for f in range(21):
                c = filt[f, rr, t * LANES : (t + 1) * LANES]
                e = filt[f, rr, cells : cells + LANES]
                below = rot(filt[f, rr, (t - 1) * LANES : t * LANES], NX) if t else e
                above = rot(filt[f, rr, (t + 1) * LANES : (t + 2) * LANES], -NX) if t < tiles - 1 else rot(e, -2 * NX)
                below = jnp.where(lane8 < NX, below, rot(c, NX))
                above = jnp.where(lane8 >= LANES - NX, above, rot(c, -NX))
                z = 0.5 * c + 0.25 * (below + above)
                behind = jnp.where(first, rot(z, 1 - NX), rot(z, 1))
                ahead = jnp.where(last, rot(z, NX - 1), rot(z, -1))
                g.append(0.5 * z + 0.25 * (behind + ahead))
            u, p, s, m = g[0:3], g[3:9], g[9:15], g[15:21]
            rate = 4.0 * strain_rate(s)
            for k in range(6):
                leonard = p[k] - u[LEAD_INDEX[k]] * u[TAIL_INDEX[k]]
                model = m[k] - rate * s[k]
                weighted = TENSOR_WEIGHTS[k] * model
                num = num + weighted * leonard
                den = den + weighted * model
        acc[0, rr, :] = num
        acc[1, rr, :] = den
        return carry

    lax.fori_loop(0, rows // HMAX, row_step, 0)
    ones = jnp.ones((HMAX, LANES), F32)
    for k in range(2):
        sums = lax.dot_general(
            ones, acc[k], (((1,), (1,)), ((), ())), precision=lax.Precision.HIGHEST, preferred_element_type=F32
        )
        out_ref[k : k + 1, :] = sums[0:1]


def main_call(velocity, strain, heights, reach, znear, zfar, ynear, yfar):
    rows, cells = velocity.shape[1:]
    ext = rows + 2 * HMAX
    vmem = pl.BlockSpec(memory_space=pltpu.VMEM)
    return pl.pallas_call(
        main_kernel,
        in_specs=[vmem] * 8,
        out_specs=vmem,
        out_shape=jax.ShapeDtypeStruct((2, rows), F32),
        scratch_shapes=[
            pltpu.VMEM((9, ext, cells + LANES), F32),
            pltpu.VMEM((2 * LANES, 21 * LANES), BF16),
            pltpu.VMEM((21, rows, cells + LANES), F32),
            pltpu.VMEM((2, rows, LANES), F32),
        ],
        compiler_params=pltpu.CompilerParams(vmem_limit_bytes=40 * 1024 * 1024),
    )(velocity, strain, heights, reach, znear, zfar, ynear, yfar)


def near_pairs(axis):
    return [(i, i ^ 1) for i in range(lax.axis_size(axis))]


def far_pairs(axis, closed):
    n = lax.axis_size(axis)
    pairs = []
    for i in range(1, n if closed else n - 1, 2):
        pairs += [(i, (i + 1) % n), ((i + 1) % n, i)]
    return pairs


def local(velocity, strain, cell_height, stencil_reach):
    rows, cells = velocity.shape[1:]
    heights = cell_height.reshape(1, rows)
    near, far = pack_span(velocity, strain)
    zfar = lax.ppermute(far, "gz", far_pairs("gz", True))
    znear = lax.ppermute(near, "gz", near_pairs("gz"))
    near, far = pack_wall(velocity, strain, heights, znear, zfar)
    yfar = lax.ppermute(far, "gy", far_pairs("gy", False))
    ynear = lax.ppermute(near, "gy", near_pairs("gy"))
    sums = main_call(velocity, strain, heights, stencil_reach, znear, zfar, ynear, yfar)
    for mask in (1, 3, 4, 12):
        sums = sums + lax.ppermute(sums, "gz", [(i, i ^ mask) for i in range(16)])
    total = lax.axis_size("gz") * cells
    return sums[0] / total / (sums[1] / total + 1e-06)


def solution(mesh):
    in_specs = (P(None, "gy", "gz"), P(None, "gy", "gz"), P("gy"), P(None, "gy"))
    return jax.shard_map(local, mesh=mesh, in_specs=in_specs, out_specs=P("gy"), check_vma=False)
```

time: 297 us -> 141 us (0.47)
  the two profiles are of different devices: /device:TPU:1 before, /device:TPU:2 now
where the time goes in v1:
time: 141 us
  Pallas kernels  104 us (74%)
  waiting for transfers between devices  20.4 us (14%)
  starting transfers between devices  13.4 us (10%)
  local copies, waits for them, and re-layouts  2.22 us (2%)
    pallas_call x1, Pallas kernels, main_call(): pl.pallas_call(main_kernel, in_specs=[vmem] * 8, out_specs=vmem, out_shap...  100 us
    ppermute x4, waiting for transfers between devices, local(): sums = sums + lax.ppermute(sums, 'gz', [(i, i ^ mask) for i in range(16)])  12.7 us
    ppermute x1, waiting for transfers between devices, local(): yfar = lax.ppermute(far, 'gy', far_pairs('gy', False))  5 us
    ppermute x1, starting transfers between devices, local(): zfar = lax.ppermute(far, 'gz', far_pairs('gz', True))  4.97 us
    ppermute x4, starting transfers between devices, local(): sums = sums + lax.ppermute(sums, 'gz', [(i, i ^ mask) for i in range(16)])  3.98 us
  transfers between devices with their start and end apart: 8, of which 6 were waited for; matrix products, arithmetic and copies ran while one was open for 0% of the time, Pallas kernels for 0%

profile of v1, /device:TPU:2, one launch (start us, length us, event | category | flops | bytes accessed | tf_op | source)
XLA Modules:
  0.0 141.0 jit_solution(3904723892280855796)
XLA Ops:
  0.0 2.0 %shard_map.46 = (f32[96,128]{1,0:T(8,128)}, f32[96,128]{1,0:T(8,128)}) custom-call(f32[3,96,768]{2,1,0:T(8,128)} %v_ref.1, f32[3,96,768]{2,1,0:T(8,128)} %v_ref.1, bf16[6,96,768]{2,1,0:T(8,128)(2,1)} %s_ref.1, bf16[6,96,768]{2,1,0:T(8,128)(2,1)} %s_ref.1), custom_call_target="tpu_custom_call" | custom-call | tf_op jit(solution)/shard_map/pallas_call | solution.py:52
  2.0 1.9 %collective-permute-start = (f32[96,128]{1,0:T(8,128)}, f32[96,128]{1,0:T(8,128)S(1)}, u32[]{:S(2)}, u32[]{:S(2)}) collective-permute-start(f32[96,128]{1,0:T(8,128)} %get-tuple-element.9), channel_id=1, source_target_pairs={{0,1},{1,0},{2,3},{3,2},{4,5},{5,4},{6,7},{7,6},{8,9},{9,8},{10,11... | collective-permute-start | bytes 147464 | tf_op jit(solution)/shard_map/ppermute | solution.py:278
  3.9 5.0 %collective-permute-start.1 = (f32[96,128]{1,0:T(8,128)}, f32[96,128]{1,0:T(8,128)S(1)}, u32[]{:S(2)}, u32[]{:S(2)}) collective-permute-start(f32[96,128]{1,0:T(8,128)} %get-tuple-element.10), channel_id=1, source_target_pairs={{1,2},{2,1},{3,4},{4,3},{5,6},{6,5},{7,8},{8,7},{9,10},{10,9},{11,... | collective-permute-start | bytes 147464 | tf_op jit(solution)/shard_map/ppermute | solution.py:277
  8.9 0.0 collective-permute-done.znear
  8.9 0.0 copy-start.2
  8.9 2.6 %collective-permute-done.1.zfar = f32[96,128]{1,0:T(8,128)S(1)} collective-permute-done((f32[96,128]{1,0:T(8,128)}, f32[96,128]{1,0:T(8,128)S(1)}, u32[]{:S(2)}, u32[]{:S(2)}) %collective-permute-start.1) | collective-permute-done | bytes 49184 | tf_op jit(solution)/shard_map/ppermute | solution.py:277
  11.5 0.0 copy-start.4
  11.5 0.0 copy-done.2
  11.5 0.6 copy-done.4
  12.1 0.0 copy-start
  12.1 0.0 copy-start.1
  12.1 2.0 %shard_map.47 = (f32[8,7168]{1,0:T(8,128)}, f32[8,7168]{1,0:T(8,128)}) custom-call(f32[3,96,768]{2,1,0:T(8,128)} %v_ref.1, f32[3,96,768]{2,1,0:T(8,128)} %v_ref.1, bf16[6,96,768]{2,1,0:T(8,128)(2,1)} %s_ref.1, bf16[6,96,768]{2,1,0:T(8,128)(2,1)} %s_ref.1, f32[1,96]{1,0:T(1,128)} %bitcast.3, f32[96,128]{1,0:T(8,128)} %copy-done.2, f32[96,128]{1,0:T(8,128)} %copy-done.4), custom_call_target="tpu_custom_call" | custom-call | tf_op jit(solution)/shard_map/pallas_call | solution.py:107
  14.2 0.0 copy-start.6
  14.2 0.0 copy-start.7
  14.2 0.0 collective-permute-start.2
  14.2 2.5 %collective-permute-start.3 = (f32[8,7168]{1,0:T(8,128)}, f32[8,7168]{1,0:T(8,128)S(1)}, u32[]{:S(2)}, u32[]{:S(2)}) collective-permute-start(f32[8,7168]{1,0:T(8,128)} %get-tuple-element.12), channel_id=1, source_target_pairs={{16,32},{32,16},{48,64},{64,48},{80,96},{96,80},{17,33},{33,17},{4... | collective-permute-start | bytes 688136 | tf_op jit(solution)/shard_map/ppermute | solution.py:280
  16.8 0.0 collective-permute-done.2.ynear
  16.8 5.0 %collective-permute-done.3.yfar = f32[8,7168]{1,0:T(8,128)S(1)} collective-permute-done((f32[8,7168]{1,0:T(8,128)}, f32[8,7168]{1,0:T(8,128)S(1)}, u32[]{:S(2)}, u32[]{:S(2)}) %collective-permute-start.3) | collective-permute-done | bytes 229408 | tf_op jit(solution)/shard_map/ppermute | solution.py:280
  21.8 0.0 copy-done
  21.8 0.0 copy-done.1
  21.8 0.0 copy-done.6
  21.8 0.0 copy-done.7
  21.8 0.0 copy-start.3
  21.8 0.8 copy-done.3
  22.6 0.0 copy-start.5
  22.6 0.8 copy-done.5
  23.4 100.3 %shard_map.48 = f32[2,96]{1,0:T(2,128)S(1)} custom-call(f32[3,96,768]{2,1,0:T(8,128)S(1)} %copy-done, bf16[6,96,768]{2,1,0:T(8,128)(2,1)S(1)} %copy-done.1, f32[1,96]{1,0:T(1,128)S(1)} %bitcast.4, s32[2,96]{1,0:T(2,128)S(1)} %copy-done.7, f32[96,128]{1,0:T(8,128)S(1)} %copy-done.3, f32[96,128]{1,0:T(8,128)S(1)} %copy-done.5, ...), custom_call_target="tpu_custom_call" | custom-call | tf_op jit(solution)/shard_map/pallas_call | solution.py:246
  123.7 0.0 collective-permute-start.4
  123.7 3.6 %collective-permute-done.4 = f32[2,96]{1,0:T(2,128)S(1)} collective-permute-done((f32[2,96]{1,0:T(2,128)S(1)}, f32[2,96]{1,0:T(2,128)S(1)}, u32[]{:S(2)}, u32[]{:S(2)}) %collective-permute-start.4) | collective-permute-done | bytes 800 | tf_op jit(solution)/shard_map/ppermute | solution.py:284
  127.3 1.3 collective-permute-start.5
  128.6 3.5 %collective-permute-done.5 = f32[2,96]{1,0:T(2,128)S(1)} collective-permute-done((f32[2,96]{1,0:T(2,128)S(1)}, f32[2,96]{1,0:T(2,128)S(1)}, u32[]{:S(2)}, u32[]{:S(2)}) %collective-permute-start.5) | collective-permute-done | bytes 800 | tf_op jit(solution)/shard_map/ppermute | solution.py:284
  132.1 0.4 collective-permute-start.6
  132.5 3.2 %collective-permute-done.6 = f32[2,96]{1,0:T(2,128)S(1)} collective-permute-done((f32[2,96]{1,0:T(2,128)S(1)}, f32[2,96]{1,0:T(2,128)S(1)}, u32[]{:S(2)}, u32[]{:S(2)}) %collective-permute-start.6) | collective-permute-done | bytes 800 | tf_op jit(solution)/shard_map/ppermute | solution.py:284
  135.7 2.3 %collective-permute-start.7 = (f32[2,96]{1,0:T(2,128)S(1)}, f32[2,96]{1,0:T(2,128)S(1)}, u32[]{:S(2)}, u32[]{:S(2)}) collective-permute-start(f32[2,96]{1,0:T(2,128)S(1)} %add.21), channel_id=1, source_target_pairs={{0,12},{1,13},{2,14},{3,15},{4,8},{5,9},{6,10},{7,11},{8,4},{9,5},... | collective-permute-start | bytes 2312 | tf_op jit(solution)/shard_map/ppermute | solution.py:284
  138.0 2.5 %collective-permute-done.7 = f32[2,96]{1,0:T(2,128)S(1)} collective-permute-done((f32[2,96]{1,0:T(2,128)S(1)}, f32[2,96]{1,0:T(2,128)S(1)}, u32[]{:S(2)}, u32[]{:S(2)}) %collective-permute-start.7) | collective-permute-done | bytes 800 | tf_op jit(solution)/shard_map/ppermute | solution.py:284
  140.5 0.5 fusion
  (4 shorter events, 0.0 us)
Async XLA Ops:
  2.0 6.9 %collective-permute-start = (f32[96,128]{1,0:T(8,128)}, f32[96,128]{1,0:T(8,128)S(1)}, u32[]{:S(2)}, u32[]{:S(2)}) collective-permute-start(f32[96,128]{1,0:T(8,128)} %get-tuple-element.9), channel_id=1, source_target_pairs={{0,1},{1,0},{2,3},{3,2},{4,5},{5,4},{6,7},{7,6},{8,9},{9,8},{10,11... | collective-permute-start | bytes 147464 | tf_op jit(solution)/shard_map/ppermute | solution.py:278
  3.9 7.6 %collective-permute-start.1 = (f32[96,128]{1,0:T(8,128)}, f32[96,128]{1,0:T(8,128)S(1)}, u32[]{:S(2)}, u32[]{:S(2)}) collective-permute-start(f32[96,128]{1,0:T(8,128)} %get-tuple-element.10), channel_id=1, source_target_pairs={{1,2},{2,1},{3,4},{4,3},{5,6},{6,5},{7,8},{8,7},{9,10},{10,9},{11,... | collective-permute-start | bytes 147464 | tf_op jit(solution)/shard_map/ppermute | solution.py:277
  8.9 2.6 %copy-start.2 = (f32[96,128]{1,0:T(8,128)}, f32[96,128]{1,0:T(8,128)S(1)}, u32[]{:S(2)}) copy-start(f32[96,128]{1,0:T(8,128)S(1)} %collective-permute-done.znear) | copy-start | bytes 147460
  11.5 0.6 copy-start.4
  12.1 9.6 %copy-start = (f32[3,96,768]{2,1,0:T(8,128)S(1)}, f32[3,96,768]{2,1,0:T(8,128)}, u32[]{:S(2)}) copy-start(f32[3,96,768]{2,1,0:T(8,128)} %v_ref.1) | copy-start | bytes 2654212
  12.1 9.6 %copy-start.1 = (bf16[6,96,768]{2,1,0:T(8,128)(2,1)S(1)}, bf16[6,96,768]{2,1,0:T(8,128)(2,1)}, u32[]{:S(2)}) copy-start(bf16[6,96,768]{2,1,0:T(8,128)(2,1)} %s_ref.1) | copy-start | bytes 2654212
  14.2 7.6 %copy-start.6 = (f32[96]{0:T(128)S(1)}, f32[96]{0:T(128)}, u32[]{:S(2)}) copy-start(f32[96]{0:T(128)} %param.6) | copy-start | bytes 1156
  14.2 7.6 %copy-start.7 = (s32[2,96]{1,0:T(2,128)S(1)}, s32[2,96]{1,0:T(2,128)}, u32[]{:S(2)}) copy-start(s32[2,96]{1,0:T(2,128)} %reach_ref.1) | copy-start | bytes 2308
  14.2 2.6 %collective-permute-start.2 = (f32[8,7168]{1,0:T(8,128)}, f32[8,7168]{1,0:T(8,128)S(1)}, u32[]{:S(2)}, u32[]{:S(2)}) collective-permute-start(f32[8,7168]{1,0:T(8,128)} %get-tuple-element.11), channel_id=1, source_target_pairs={{0,16},{16,0},{32,48},{48,32},{64,80},{80,64},{96,112},{112,96},{1... | collective-permute-start | bytes 688136 | tf_op jit(solution)/shard_map/ppermute | solution.py:281
  14.2 7.5 %collective-permute-start.3 = (f32[8,7168]{1,0:T(8,128)}, f32[8,7168]{1,0:T(8,128)S(1)}, u32[]{:S(2)}, u32[]{:S(2)}) collective-permute-start(f32[8,7168]{1,0:T(8,128)} %get-tuple-element.12), channel_id=1, source_target_pairs={{16,32},{32,16},{48,64},{64,48},{80,96},{96,80},{17,33},{33,17},{4... | collective-permute-start | bytes 688136 | tf_op jit(solution)/shard_map/ppermute | solution.py:280
  21.8 0.8 copy-start.3
  22.6 0.8 copy-start.5
  123.7 3.6 %collective-permute-start.4 = (f32[2,96]{1,0:T(2,128)S(1)}, f32[2,96]{1,0:T(2,128)S(1)}, u32[]{:S(2)}, u32[]{:S(2)}) collective-permute-start(f32[2,96]{1,0:T(2,128)S(1)} %shard_map.48), channel_id=1, source_target_pairs={{0,1},{1,0},{2,3},{3,2},{4,5},{5,4},{6,7},{7,6},{8,9},{9,8},{10,11... | collective-permute-start | bytes 2312 | tf_op jit(solution)/shard_map/ppermute | solution.py:284
  127.3 4.8 %collective-permute-start.5 = (f32[2,96]{1,0:T(2,128)S(1)}, f32[2,96]{1,0:T(2,128)S(1)}, u32[]{:S(2)}, u32[]{:S(2)}) collective-permute-start(f32[2,96]{1,0:T(2,128)S(1)} %add.19), channel_id=1, source_target_pairs={{0,3},{1,2},{2,1},{3,0},{4,7},{5,6},{6,5},{7,4},{8,11},{9,10},{10,... | collective-permute-start | bytes 2312 | tf_op jit(solution)/shard_map/ppermute | solution.py:284
  132.1 3.6 %collective-permute-start.6 = (f32[2,96]{1,0:T(2,128)S(1)}, f32[2,96]{1,0:T(2,128)S(1)}, u32[]{:S(2)}, u32[]{:S(2)}) collective-permute-start(f32[2,96]{1,0:T(2,128)S(1)} %add.20), channel_id=1, source_target_pairs={{0,4},{1,5},{2,6},{3,7},{4,0},{5,1},{6,2},{7,3},{8,12},{9,13},{10,... | collective-permute-start | bytes 2312 | tf_op jit(solution)/shard_map/ppermute | solution.py:284
  135.7 4.8 %collective-permute-start.7 = (f32[2,96]{1,0:T(2,128)S(1)}, f32[2,96]{1,0:T(2,128)S(1)}, u32[]{:S(2)}, u32[]{:S(2)}) collective-permute-start(f32[2,96]{1,0:T(2,128)S(1)} %add.21), channel_id=1, source_target_pairs={{0,12},{1,13},{2,14},{3,15},{4,8},{5,9},{6,10},{7,11},{8,4},{9,5},... | collective-permute-start | bytes 2312 | tf_op jit(solution)/shard_map/ppermute | solution.py:284

commit v2 on v1

--- a/solution.py
+++ b/solution.py
@@ -1,5 +1,6 @@
 import jax
 import jax.numpy as jnp
+import numpy as np
 from jax import lax
 from jax.experimental import pallas as pl
 from jax.experimental.pallas import tpu as pltpu
@@ -121,12 +122,22 @@
     )(velocity, velocity, strain, strain, heights, znear, zfar)
 
 
+def plane_filter():
+    k = np.arange(4 * LANES)[:, None]
+    m = np.arange(2 * LANES)[None, :] + LANES
+    turn = (k - m) % NX
+    along = np.where(turn == 0, 0.5, np.where((turn == 1) | (turn == NX - 1), 0.25, 0.0))
+    step = np.abs(k // NX - m // NX)
+    across = np.where(step == 0, 0.5, np.where(step == 1, 0.25, 0.0))
+    return jnp.asarray(along * across, BF16)
+
+
 def split2(x):
     hi = x.astype(BF16)
     return hi, (x - hi.astype(F32)).astype(BF16)
 
 
-def main_kernel(v_ref, s_ref, h_ref, reach_ref, znear, zfar, ynear, yfar, out_ref, raw, stack, filt, acc):
+def main_kernel(v_ref, s_ref, h_ref, reach_ref, znear, zfar, ynear, yfar, plane_ref, out_ref, raw, stack, fh, fl, smooth, acc):
     rows, cells = v_ref.shape[1:]
     tiles = cells // LANES
     ext = rows + 2 * HMAX
@@ -174,12 +185,13 @@
         far = yfar[:, f * cells : (f + 1) * cells]
         raw[f, rows : rows + HMAX, 0:cells] = jnp.where(gy_odd, near, far)
         raw[f, rows + HMAX : ext, 0:cells] = jnp.where(gy_odd, far, near)
-        edge = jnp.where(elane < NX, rot(zl, -NX * f), jnp.where(elane < 2 * NX, rot(zr, NX - NX * f), 0.0))
+        edge = jnp.where(elane < NX, rot(zr, -NX * f), jnp.where(elane >= LANES - NX, rot(zl, -NX * f - NX), 0.0))
         raw[f, 0:ext, cells : cells + LANES] = edge
     stack[...] = jnp.zeros_like(stack)
 
     def tile_step(t, carry):
         at = pl.ds(pl.multiple_of(t * LANES, LANES), LANES)
+        to = pl.ds(pl.multiple_of(t * LANES + LANES, LANES), LANES)
         for r in range(0, ext, 16):
             u = [raw[f, r : r + 16, at] for f in range(3)]
             s = [raw[f, r : r + 16, at] for f in range(3, 9)]
@@ -192,45 +204,42 @@
         both = jnp.dot(lhs, stack[...], preferred_element_type=F32)
         merged = both[:rows] + both[rows:]
         for f in range(21):
-            filt[f, :, at] = merged[:, f * LANES : (f + 1) * LANES]
+            hi, lo = split2(merged[:, f * LANES : (f + 1) * LANES])
+            fh[f, :, to] = hi
+            fl[f, :, to] = lo
         return carry
 
     lax.fori_loop(0, tiles + 1, tile_step, 0)
 
-    lane8 = lane_iota((HMAX, LANES))
-    phase = lane8 % NX
-    first, last = phase == 0, phase == NX - 1
-
-    def row_step(r, carry):
-        rr = pl.ds(pl.multiple_of(r * HMAX, HMAX), HMAX)
-        num = jnp.zeros((HMAX, LANES), F32)
-        den = jnp.zeros((HMAX, LANES), F32)
-        for t in range(tiles):
-            g = []
-            for f in range(21):
-                c = filt[f, rr, t * LANES : (t + 1) * LANES]
-                e = filt[f, rr, cells : cells + LANES]
-                below = rot(filt[f, rr, (t - 1) * LANES : t * LANES], NX) if t else e
-                above = rot(filt[f, rr, (t + 1) * LANES : (t + 2) * LANES], -NX) if t < tiles - 1 else rot(e, -2 * NX)
-                below = jnp.where(lane8 < NX, below, rot(c, NX))
-                above = jnp.where(lane8 >= LANES - NX, above, rot(c, -NX))
-                z = 0.5 * c + 0.25 * (below + above)
-                behind = jnp.where(first, rot(z, 1 - NX), rot(z, 1))
-                ahead = jnp.where(last, rot(z, NX - 1), rot(z, -1))
-                g.append(0.5 * z + 0.25 * (behind + ahead))
-            u, p, s, m = g[0:3], g[3:9], g[9:15], g[15:21]
-            rate = 4.0 * strain_rate(s)
-            for k in range(6):
-                leonard = p[k] - u[LEAD_INDEX[k]] * u[TAIL_INDEX[k]]
-                model = m[k] - rate * s[k]
-                weighted = TENSOR_WEIGHTS[k] * model
-                num = num + weighted * leonard
-                den = den + weighted * model
-        acc[0, rr, :] = num
-        acc[1, rr, :] = den
+    fh[:, :, 0:LANES] = fh[:, :, cells + LANES :]
+    fl[:, :, 0:LANES] = fl[:, :, cells + LANES :]
+    acc[...] = jnp.zeros_like(acc)
+
+    def block_step(n, carry):
+        at = pl.ds(pl.multiple_of(n * 2 * LANES, LANES), 4 * LANES)
+        for f in range(21):
+            hi = jnp.dot(fh[f, :, at], plane_ref[...], preferred_element_type=F32)
+            lo = jnp.dot(fl[f, :, at], plane_ref[...], preferred_element_type=F32)
+            smooth[f] = hi + lo
+        for r in range(0, rows, HMAX):
+            rr = slice(r, r + HMAX)
+            for c in range(2):
+                g = [smooth[f, rr, c * LANES : (c + 1) * LANES] for f in range(21)]
+                u, p, s, m = g[0:3], g[3:9], g[9:15], g[15:21]
+                rate = 4.0 * strain_rate(s)
+                num = acc[0, rr, :]
+                den = acc[1, rr, :]
+                for k in range(6):
+                    leonard = p[k] - u[LEAD_INDEX[k]] * u[TAIL_INDEX[k]]
+                    model = m[k] - rate * s[k]
+                    weighted = TENSOR_WEIGHTS[k] * model
+                    num = num + weighted * leonard
+                    den = den + weighted * model
+                acc[0, rr, :] = num
+                acc[1, rr, :] = den
         return carry
 
-    lax.fori_loop(0, rows // HMAX, row_step, 0)
+    lax.fori_loop(0, tiles // 2, block_step, 0)
     ones = jnp.ones((HMAX, LANES), F32)
     for k in range(2):
         sums = lax.dot_general(
@@ -245,17 +254,19 @@
     vmem = pl.BlockSpec(memory_space=pltpu.VMEM)
     return pl.pallas_call(
         main_kernel,
-        in_specs=[vmem] * 8,
+        in_specs=[vmem] * 9,
         out_specs=vmem,
         out_shape=jax.ShapeDtypeStruct((2, rows), F32),
         scratch_shapes=[
             pltpu.VMEM((9, ext, cells + LANES), F32),
             pltpu.VMEM((2 * LANES, 21 * LANES), BF16),
-            pltpu.VMEM((21, rows, cells + LANES), F32),
+            pltpu.VMEM((21, rows, cells + 2 * LANES), BF16),
+            pltpu.VMEM((21, rows, cells + 2 * LANES), BF16),
+            pltpu.VMEM((21, rows, 2 * LANES), F32),
             pltpu.VMEM((2, rows, LANES), F32),
         ],
         compiler_params=pltpu.CompilerParams(vmem_limit_bytes=40 * 1024 * 1024),
-    )(velocity, strain, heights, reach, znear, zfar, ynear, yfar)
+    )(velocity, strain, heights, reach, znear, zfar, ynear, yfar, plane_filter())
 
 
 def near_pairs(axis):

time: 141 us -> 52.9 us (0.38)
  the two profiles are of different devices: /device:TPU:2 before, /device:TPU:4 now
where the time goes in v2:
time: 52.9 us; the launch traced here: 52.6 us
  waiting for transfers between devices  20.4 us (39%)
  Pallas kernels  16 us (30%)
  starting transfers between devices  13.4 us (25%)
  local copies, waits for them, and re-layouts  2.22 us (4%)
  other arithmetic  0.54 us (1%)
    ppermute x4, waiting for transfers between devices, local(): sums = sums + lax.ppermute(sums, 'gz', [(i, i ^ mask) for i in range(16)])  12.8 us
    pallas_call x1, Pallas kernels, main_call(): pl.pallas_call(main_kernel, in_specs=[vmem] * 9, out_specs=vmem, out_shap...  11.9 us
    ppermute x1, waiting for transfers between devices, local(): yfar = lax.ppermute(far, 'gy', far_pairs('gy', False))  5 us
    ppermute x1, starting transfers between devices, local(): zfar = lax.ppermute(far, 'gz', far_pairs('gz', True))  4.97 us
    ppermute x4, starting transfers between devices, local(): sums = sums + lax.ppermute(sums, 'gz', [(i, i ^ mask) for i in range(16)])  3.96 us
    ppermute x1, waiting for transfers between devices, local(): zfar = lax.ppermute(far, 'gz', far_pairs('gz', True))  2.64 us
    ppermute x1, starting transfers between devices, local(): yfar = lax.ppermute(far, 'gy', far_pairs('gy', False))  2.53 us
    unnamed x18, local copies, waits for them, and re-layouts  2.22 us
  transfers between devices with their start and end apart: 8, of which 6 were waited for; matrix products, arithmetic and copies ran while one was open for 0% of the time, Pallas kernels for 0%

profile of v2, /device:TPU:4, one launch (start us, length us, event | category | flops | bytes accessed | tf_op | source)
XLA Modules:
  0.0 52.6 jit_solution(16787772992362113855)
XLA Ops:
  0.0 2.0 %shard_map.55 = (f32[96,128]{1,0:T(8,128)}, f32[96,128]{1,0:T(8,128)}) custom-call(f32[3,96,768]{2,1,0:T(8,128)} %v_ref.1, f32[3,96,768]{2,1,0:T(8,128)} %v_ref.1, bf16[6,96,768]{2,1,0:T(8,128)(2,1)} %s_ref.1, bf16[6,96,768]{2,1,0:T(8,128)(2,1)} %s_ref.1), custom_call_target="tpu_custom_call" | custom-call | tf_op jit(solution)/shard_map/pallas_call | solution.py:53
  2.0 1.9 %collective-permute-start = (f32[96,128]{1,0:T(8,128)}, f32[96,128]{1,0:T(8,128)S(1)}, u32[]{:S(2)}, u32[]{:S(2)}) collective-permute-start(f32[96,128]{1,0:T(8,128)} %get-tuple-element.9), channel_id=1, source_target_pairs={{0,1},{1,0},{2,3},{3,2},{4,5},{5,4},{6,7},{7,6},{8,9},{9,8},{10,11... | collective-permute-start | bytes 147464 | tf_op jit(solution)/shard_map/ppermute | solution.py:289
  3.9 5.0 %collective-permute-start.1 = (f32[96,128]{1,0:T(8,128)}, f32[96,128]{1,0:T(8,128)S(1)}, u32[]{:S(2)}, u32[]{:S(2)}) collective-permute-start(f32[96,128]{1,0:T(8,128)} %get-tuple-element.10), channel_id=1, source_target_pairs={{1,2},{2,1},{3,4},{4,3},{5,6},{6,5},{7,8},{8,7},{9,10},{10,9},{11,... | collective-permute-start | bytes 147464 | tf_op jit(solution)/shard_map/ppermute | solution.py:288
  8.9 0.0 collective-permute-done.znear
  8.9 0.0 copy-start.3
  8.9 2.6 %collective-permute-done.1.zfar = f32[96,128]{1,0:T(8,128)S(1)} collective-permute-done((f32[96,128]{1,0:T(8,128)}, f32[96,128]{1,0:T(8,128)S(1)}, u32[]{:S(2)}, u32[]{:S(2)}) %collective-permute-start.1) | collective-permute-done | bytes 49184 | tf_op jit(solution)/shard_map/ppermute | solution.py:288
  11.5 0.0 copy-start.5
  11.5 0.0 copy-done.3
  11.5 0.6 %copy-done.5 = f32[96,128]{1,0:T(8,128)} copy-done((f32[96,128]{1,0:T(8,128)}, f32[96,128]{1,0:T(8,128)S(1)}, u32[]{:S(2)}) %copy-start.5) | copy-done | bytes 49176
  12.1 0.0 copy-start
  12.1 0.0 copy-start.1
  12.2 0.0 copy-start.2
  12.2 2.0 %shard_map.56 = (f32[8,7168]{1,0:T(8,128)}, f32[8,7168]{1,0:T(8,128)}) custom-call(f32[3,96,768]{2,1,0:T(8,128)} %v_ref.1, f32[3,96,768]{2,1,0:T(8,128)} %v_ref.1, bf16[6,96,768]{2,1,0:T(8,128)(2,1)} %s_ref.1, bf16[6,96,768]{2,1,0:T(8,128)(2,1)} %s_ref.1, f32[1,96]{1,0:T(1,128)} %bitcast.3, f32[96,128]{1,0:T(8,128)} %copy-done.3, f32[96,128]{1,0:T(8,128)} %copy-done.5), custom_call_target="tpu_custom_call" | custom-call | tf_op jit(solution)/shard_map/pallas_call | solution.py:108
  14.2 0.0 copy-start.7
  14.2 0.0 copy-start.8
  14.2 0.0 collective-permute-start.2
  14.3 2.5 %collective-permute-start.3 = (f32[8,7168]{1,0:T(8,128)}, f32[8,7168]{1,0:T(8,128)S(1)}, u32[]{:S(2)}, u32[]{:S(2)}) collective-permute-start(f32[8,7168]{1,0:T(8,128)} %get-tuple-element.12), channel_id=1, source_target_pairs={{16,32},{32,16},{48,64},{64,48},{80,96},{96,80},{17,33},{33,17},{4... | collective-permute-start | bytes 688136 | tf_op jit(solution)/shard_map/ppermute | solution.py:291
  16.8 0.0 collective-permute-done.2.ynear
  16.8 5.0 %collective-permute-done.3.yfar = f32[8,7168]{1,0:T(8,128)S(1)} collective-permute-done((f32[8,7168]{1,0:T(8,128)}, f32[8,7168]{1,0:T(8,128)S(1)}, u32[]{:S(2)}, u32[]{:S(2)}) %collective-permute-start.3) | collective-permute-done | bytes 229408 | tf_op jit(solution)/shard_map/ppermute | solution.py:291
  21.8 0.0 copy-done
  21.8 0.0 copy-done.1
  21.8 0.0 copy-done.2
  21.8 0.0 copy-done.7
  21.8 0.0 copy-done.8
  21.8 0.0 copy-start.4
  21.8 0.8 %copy-done.4 = f32[96,128]{1,0:T(8,128)S(1)} copy-done((f32[96,128]{1,0:T(8,128)S(1)}, f32[96,128]{1,0:T(8,128)}, u32[]{:S(2)}) %copy-start.4) | copy-done | bytes 49176
  22.6 0.0 copy-start.6
  22.6 0.8 %copy-done.6 = f32[96,128]{1,0:T(8,128)S(1)} copy-done((f32[96,128]{1,0:T(8,128)S(1)}, f32[96,128]{1,0:T(8,128)}, u32[]{:S(2)}) %copy-start.6) | copy-done | bytes 49176
  23.4 11.9 %shard_map.57 = f32[2,96]{1,0:T(2,128)S(1)} custom-call(f32[3,96,768]{2,1,0:T(8,128)S(1)} %copy-done, bf16[6,96,768]{2,1,0:T(8,128)(2,1)S(1)} %copy-done.1, f32[1,96]{1,0:T(1,128)S(1)} %bitcast.4, s32[2,96]{1,0:T(2,128)S(1)} %copy-done.8, f32[96,128]{1,0:T(8,128)S(1)} %copy-done.4, f32[96,128]{1,0:T(8,128)S(1)} %copy-done.6, ...), custom_call_target="tpu_custom_call" | custom-call | tf_op jit(solution)/shard_map/pallas_call | solution.py:255
  35.4 0.0 collective-permute-start.4
  35.4 3.6 %collective-permute-done.4 = f32[2,96]{1,0:T(2,128)S(1)} collective-permute-done((f32[2,96]{1,0:T(2,128)S(1)}, f32[2,96]{1,0:T(2,128)S(1)}, u32[]{:S(2)}, u32[]{:S(2)}) %collective-permute-start.4) | collective-permute-done | bytes 800 | tf_op jit(solution)/shard_map/ppermute | solution.py:295
  39.0 1.3 %collective-permute-start.5 = (f32[2,96]{1,0:T(2,128)S(1)}, f32[2,96]{1,0:T(2,128)S(1)}, u32[]{:S(2)}, u32[]{:S(2)}) collective-permute-start(f32[2,96]{1,0:T(2,128)S(1)} %add.19), channel_id=1, source_target_pairs={{0,3},{1,2},{2,1},{3,0},{4,7},{5,6},{6,5},{7,4},{8,11},{9,10},{10,... | collective-permute-start | bytes 2312 | tf_op jit(solution)/shard_map/ppermute | solution.py:295
  40.3 3.5 %collective-permute-done.5 = f32[2,96]{1,0:T(2,128)S(1)} collective-permute-done((f32[2,96]{1,0:T(2,128)S(1)}, f32[2,96]{1,0:T(2,128)S(1)}, u32[]{:S(2)}, u32[]{:S(2)}) %collective-permute-start.5) | collective-permute-done | bytes 800 | tf_op jit(solution)/shard_map/ppermute | solution.py:295
  43.7 0.4 collective-permute-start.6
  44.1 3.2 %collective-permute-done.6 = f32[2,96]{1,0:T(2,128)S(1)} collective-permute-done((f32[2,96]{1,0:T(2,128)S(1)}, f32[2,96]{1,0:T(2,128)S(1)}, u32[]{:S(2)}, u32[]{:S(2)}) %collective-permute-start.6) | collective-permute-done | bytes 800 | tf_op jit(solution)/shard_map/ppermute | solution.py:295
  47.3 2.3 %collective-permute-start.7 = (f32[2,96]{1,0:T(2,128)S(1)}, f32[2,96]{1,0:T(2,128)S(1)}, u32[]{:S(2)}, u32[]{:S(2)}) collective-permute-start(f32[2,96]{1,0:T(2,128)S(1)} %add.21), channel_id=1, source_target_pairs={{0,12},{1,13},{2,14},{3,15},{4,8},{5,9},{6,10},{7,11},{8,4},{9,5},... | collective-permute-start | bytes 2312 | tf_op jit(solution)/shard_map/ppermute | solution.py:295
  49.6 2.5 %collective-permute-done.7 = f32[2,96]{1,0:T(2,128)S(1)} collective-permute-done((f32[2,96]{1,0:T(2,128)S(1)}, f32[2,96]{1,0:T(2,128)S(1)}, u32[]{:S(2)}, u32[]{:S(2)}) %collective-permute-start.7) | collective-permute-done | bytes 800 | tf_op jit(solution)/shard_map/ppermute | solution.py:295
  52.1 0.5 fusion
  (4 shorter events, 0.0 us)
Async XLA Ops:
  2.0 6.9 %collective-permute-start = (f32[96,128]{1,0:T(8,128)}, f32[96,128]{1,0:T(8,128)S(1)}, u32[]{:S(2)}, u32[]{:S(2)}) collective-permute-start(f32[96,128]{1,0:T(8,128)} %get-tuple-element.9), channel_id=1, source_target_pairs={{0,1},{1,0},{2,3},{3,2},{4,5},{5,4},{6,7},{7,6},{8,9},{9,8},{10,11... | collective-permute-start | bytes 147464 | tf_op jit(solution)/shard_map/ppermute | solution.py:289
  3.9 7.6 %collective-permute-start.1 = (f32[96,128]{1,0:T(8,128)}, f32[96,128]{1,0:T(8,128)S(1)}, u32[]{:S(2)}, u32[]{:S(2)}) collective-permute-start(f32[96,128]{1,0:T(8,128)} %get-tuple-element.10), channel_id=1, source_target_pairs={{1,2},{2,1},{3,4},{4,3},{5,6},{6,5},{7,8},{8,7},{9,10},{10,9},{11,... | collective-permute-start | bytes 147464 | tf_op jit(solution)/shard_map/ppermute | solution.py:288
  8.9 2.6 %copy-start.3 = (f32[96,128]{1,0:T(8,128)}, f32[96,128]{1,0:T(8,128)S(1)}, u32[]{:S(2)}) copy-start(f32[96,128]{1,0:T(8,128)S(1)} %collective-permute-done.znear) | copy-start | bytes 147460
  11.5 0.6 %copy-start.5 = (f32[96,128]{1,0:T(8,128)}, f32[96,128]{1,0:T(8,128)S(1)}, u32[]{:S(2)}) copy-start(f32[96,128]{1,0:T(8,128)S(1)} %collective-permute-done.1.zfar) | copy-start | bytes 147460
  12.1 9.7 %copy-start = (f32[3,96,768]{2,1,0:T(8,128)S(1)}, f32[3,96,768]{2,1,0:T(8,128)}, u32[]{:S(2)}) copy-start(f32[3,96,768]{2,1,0:T(8,128)} %v_ref.1) | copy-start | bytes 2654212
  12.1 9.7 %copy-start.1 = (bf16[6,96,768]{2,1,0:T(8,128)(2,1)S(1)}, bf16[6,96,768]{2,1,0:T(8,128)(2,1)}, u32[]{:S(2)}) copy-start(bf16[6,96,768]{2,1,0:T(8,128)(2,1)} %s_ref.1) | copy-start | bytes 2654212
  12.2 9.7 %copy-start.2 = (bf16[512,256]{1,0:T(8,128)(2,1)S(1)}, bf16[512,256]{1,0:T(8,128)(2,1)}, u32[]{:S(2)}) copy-start(bf16[512,256]{1,0:T(8,128)(2,1)} %constant.8.clone.plane_ref) | copy-start | bytes 786436
  14.2 7.6 %copy-start.7 = (f32[96]{0:T(128)S(1)}, f32[96]{0:T(128)}, u32[]{:S(2)}) copy-start(f32[96]{0:T(128)} %param.7) | copy-start | bytes 1156
  14.2 7.6 %copy-start.8 = (s32[2,96]{1,0:T(2,128)S(1)}, s32[2,96]{1,0:T(2,128)}, u32[]{:S(2)}) copy-start(s32[2,96]{1,0:T(2,128)} %reach_ref.1) | copy-start | bytes 2308
  14.2 2.6 %collective-permute-start.2 = (f32[8,7168]{1,0:T(8,128)}, f32[8,7168]{1,0:T(8,128)S(1)}, u32[]{:S(2)}, u32[]{:S(2)}) collective-permute-start(f32[8,7168]{1,0:T(8,128)} %get-tuple-element.11), channel_id=1, source_target_pairs={{0,16},{16,0},{32,48},{48,32},{64,80},{80,64},{96,112},{112,96},{1... | collective-permute-start | bytes 688136 | tf_op jit(solution)/shard_map/ppermute | solution.py:292
  14.3 7.5 %collective-permute-start.3 = (f32[8,7168]{1,0:T(8,128)}, f32[8,7168]{1,0:T(8,128)S(1)}, u32[]{:S(2)}, u32[]{:S(2)}) collective-permute-start(f32[8,7168]{1,0:T(8,128)} %get-tuple-element.12), channel_id=1, source_target_pairs={{16,32},{32,16},{48,64},{64,48},{80,96},{96,80},{17,33},{33,17},{4... | collective-permute-start | bytes 688136 | tf_op jit(solution)/shard_map/ppermute | solution.py:291
  21.8 0.8 %copy-start.4 = (f32[96,128]{1,0:T(8,128)S(1)}, f32[96,128]{1,0:T(8,128)}, u32[]{:S(2)}) copy-start(f32[96,128]{1,0:T(8,128)} %copy-done.3) | copy-start | bytes 147460
  22.6 0.8 %copy-start.6 = (f32[96,128]{1,0:T(8,128)S(1)}, f32[96,128]{1,0:T(8,128)}, u32[]{:S(2)}) copy-start(f32[96,128]{1,0:T(8,128)} %copy-done.5) | copy-start | bytes 147460
  35.4 3.6 %collective-permute-start.4 = (f32[2,96]{1,0:T(2,128)S(1)}, f32[2,96]{1,0:T(2,128)S(1)}, u32[]{:S(2)}, u32[]{:S(2)}) collective-permute-start(f32[2,96]{1,0:T(2,128)S(1)} %shard_map.57), channel_id=1, source_target_pairs={{0,1},{1,0},{2,3},{3,2},{4,5},{5,4},{6,7},{7,6},{8,9},{9,8},{10,11... | collective-permute-start | bytes 2312 | tf_op jit(solution)/shard_map/ppermute | solution.py:295
  39.0 4.8 %collective-permute-start.5 = (f32[2,96]{1,0:T(2,128)S(1)}, f32[2,96]{1,0:T(2,128)S(1)}, u32[]{:S(2)}, u32[]{:S(2)}) collective-permute-start(f32[2,96]{1,0:T(2,128)S(1)} %add.19), channel_id=1, source_target_pairs={{0,3},{1,2},{2,1},{3,0},{4,7},{5,6},{6,5},{7,4},{8,11},{9,10},{10,... | collective-permute-start | bytes 2312 | tf_op jit(solution)/shard_map/ppermute | solution.py:295
  43.7 3.6 %collective-permute-start.6 = (f32[2,96]{1,0:T(2,128)S(1)}, f32[2,96]{1,0:T(2,128)S(1)}, u32[]{:S(2)}, u32[]{:S(2)}) collective-permute-start(f32[2,96]{1,0:T(2,128)S(1)} %add.20), channel_id=1, source_target_pairs={{0,4},{1,5},{2,6},{3,7},{4,0},{5,1},{6,2},{7,3},{8,12},{9,13},{10,... | collective-permute-start | bytes 2312 | tf_op jit(solution)/shard_map/ppermute | solution.py:295
  47.3 4.8 %collective-permute-start.7 = (f32[2,96]{1,0:T(2,128)S(1)}, f32[2,96]{1,0:T(2,128)S(1)}, u32[]{:S(2)}, u32[]{:S(2)}) collective-permute-start(f32[2,96]{1,0:T(2,128)S(1)} %add.21), channel_id=1, source_target_pairs={{0,12},{1,13},{2,14},{3,15},{4,8},{5,9},{6,10},{7,11},{8,4},{9,5},... | collective-permute-start | bytes 2312 | tf_op jit(solution)/shard_map/ppermute | solution.py:295

commit v3 on v2

--- a/solution.py
+++ b/solution.py
@@ -31,42 +31,35 @@
     return pltpu.roll(x, amount, x.ndim - 1) if amount else x
 
 
-def pack_span_kernel(vl, vr, sl, sr, near_ref, far_ref):
-    rows = vl.shape[1]
+def pack_span_kernel(v_ref, s_ref, near_ref, far_ref):
+    rows, cells = v_ref.shape[1:]
     lane = lane_iota((rows, LANES))
     left = jnp.zeros((rows, LANES), F32)
     right = jnp.zeros((rows, LANES), F32)
     for f in range(9):
-        a = vl[f] if f < 3 else sl[f - 3].astype(F32)
-        b = vr[f] if f < 3 else sr[f - 3].astype(F32)
+        ref, at = (v_ref, f) if f < 3 else (s_ref, f - 3)
         here = (lane >= NX * f) & (lane < NX * (f + 1))
-        left = jnp.where(here, rot(a, NX * f), left)
-        right = jnp.where(here, rot(b, NX * f + NX), right)
+        left = jnp.where(here, rot(ref[at, :, :LANES].astype(F32), NX * f), left)
+        right = jnp.where(here, rot(ref[at, :, cells - LANES :].astype(F32), NX * f + NX), right)
     odd = lax.axis_index("gz") % 2 == 1
     near_ref[...] = jnp.where(odd, left, right)
     far_ref[...] = jnp.where(odd, right, left)
 
 
 def pack_span(velocity, strain):
-    rows, cells = velocity.shape[1:]
-    last = cells // LANES - 1
+    rows = velocity.shape[1]
+    vmem = pl.BlockSpec(memory_space=pltpu.VMEM)
     return pl.pallas_call(
         pack_span_kernel,
-        grid=(1,),
-        in_specs=[
-            pl.BlockSpec((3, rows, LANES), lambda i: (0, 0, 0)),
-            pl.BlockSpec((3, rows, LANES), lambda i: (0, 0, last)),
-            pl.BlockSpec((6, rows, LANES), lambda i: (0, 0, 0)),
-            pl.BlockSpec((6, rows, LANES), lambda i: (0, 0, last)),
-        ],
-        out_specs=[pl.BlockSpec((rows, LANES), lambda i: (0, 0))] * 2,
+        in_specs=[vmem] * 2,
+        out_specs=[vmem] * 2,
         out_shape=[jax.ShapeDtypeStruct((rows, LANES), F32)] * 2,
-    )(velocity, velocity, strain, strain)
-
-
-def pack_wall_kernel(vlo, vhi, slo, shi, h_ref, znear, zfar, near_ref, far_ref):
-    cells = vlo.shape[2]
-    rows = znear.shape[0]
+        compiler_params=pltpu.CompilerParams(vmem_limit_bytes=4 * 1024 * 1024),
+    )(velocity, strain)
+
+
+def pack_wall_kernel(v_ref, s_ref, h_ref, znear, zfar, near_ref, far_ref):
+    rows, cells = v_ref.shape[1:]
     gz_odd = lax.axis_index("gz") % 2 == 1
     gy_odd = lax.axis_index("gy") % 2 == 1
     tail = 9 * cells
@@ -76,13 +69,11 @@
     heights = jnp.broadcast_to(jnp.pad(h_ref[...], ((0, 0), (0, LANES - rows))), (HMAX, LANES))
 
     def emit(ref, high):
-        v = vhi if high else vlo
-        s = shi if high else slo
         r0 = rows - HMAX if high else 0
         for f in range(3):
-            ref[:, f * cells : (f + 1) * cells] = v[f]
+            ref[:, f * cells : (f + 1) * cells] = v_ref[f, r0 : r0 + HMAX, :]
         for f in range(6):
-            part = s[f].astype(F32)
+            part = (s_ref[f, rows - 2 * HMAX :, :] if high else s_ref[f, : 2 * HMAX, :]).astype(F32)
             ref[:, (3 + f) * cells : (4 + f) * cells] = part[HMAX:] if high else part[:HMAX]
         zn = znear[r0 : r0 + HMAX, :]
         zf = zfar[r0 : r0 + HMAX, :]
@@ -105,21 +96,14 @@
 def pack_wall(velocity, strain, heights, znear, zfar):
     rows, cells = velocity.shape[1:]
     width = 9 * cells + 2 * LANES
+    vmem = pl.BlockSpec(memory_space=pltpu.VMEM)
     return pl.pallas_call(
         pack_wall_kernel,
-        grid=(1,),
-        in_specs=[
-            pl.BlockSpec((3, HMAX, cells), lambda i: (0, 0, 0)),
-            pl.BlockSpec((3, HMAX, cells), lambda i: (0, rows // HMAX - 1, 0)),
-            pl.BlockSpec((6, 2 * HMAX, cells), lambda i: (0, 0, 0)),
-            pl.BlockSpec((6, 2 * HMAX, cells), lambda i: (0, rows // (2 * HMAX) - 1, 0)),
-            pl.BlockSpec((1, rows), lambda i: (0, 0)),
-            pl.BlockSpec((rows, LANES), lambda i: (0, 0)),
-            pl.BlockSpec((rows, LANES), lambda i: (0, 0)),
-        ],
-        out_specs=[pl.BlockSpec((HMAX, width), lambda i: (0, 0))] * 2,
+        in_specs=[vmem] * 5,
+        out_specs=[vmem] * 2,
         out_shape=[jax.ShapeDtypeStruct((HMAX, width), F32)] * 2,
-    )(velocity, velocity, strain, strain, heights, znear, zfar)
+        compiler_params=pltpu.CompilerParams(vmem_limit_bytes=4 * 1024 * 1024),
+    )(velocity, strain, heights, znear, zfar)
 
 
 def plane_filter():
@@ -129,7 +113,10 @@
     along = np.where(turn == 0, 0.5, np.where((turn == 1) | (turn == NX - 1), 0.25, 0.0))
     step = np.abs(k // NX - m // NX)
     across = np.where(step == 0, 0.5, np.where(step == 1, 0.25, 0.0))
-    return jnp.asarray(along * across, BF16)
+    full = along * across
+    edge = np.concatenate([full[3 * LANES : 3 * LANES + LANES // 2], full[LANES // 2 : LANES]])
+    middle = full[LANES : 3 * LANES]
+    return jnp.asarray(np.concatenate([middle, edge, edge, middle]), BF16)
 
 
 def split2(x):
@@ -191,7 +178,6 @@
 
     def tile_step(t, carry):
         at = pl.ds(pl.multiple_of(t * LANES, LANES), LANES)
-        to = pl.ds(pl.multiple_of(t * LANES + LANES, LANES), LANES)
         for r in range(0, ext, 16):
             u = [raw[f, r : r + 16, at] for f in range(3)]
             s = [raw[f, r : r + 16, at] for f in range(3, 9)]
@@ -205,22 +191,24 @@
         merged = both[:rows] + both[rows:]
         for f in range(21):
             hi, lo = split2(merged[:, f * LANES : (f + 1) * LANES])
-            fh[f, :, to] = hi
-            fl[f, :, to] = lo
+            fh[f, :, at] = hi
+            fl[f, :, at] = lo
         return carry
 
-    lax.fori_loop(0, tiles + 1, tile_step, 0)
-
-    fh[:, :, 0:LANES] = fh[:, :, cells + LANES :]
-    fl[:, :, 0:LANES] = fl[:, :, cells + LANES :]
+    lax.fori_loop(0, tiles + 1, tile_step, 0, unroll=True)
+
     acc[...] = jnp.zeros_like(acc)
-
-    def block_step(n, carry):
-        at = pl.ds(pl.multiple_of(n * 2 * LANES, LANES), 4 * LANES)
-        for f in range(21):
-            hi = jnp.dot(fh[f, :, at], plane_ref[...], preferred_element_type=F32)
-            lo = jnp.dot(fl[f, :, at], plane_ref[...], preferred_element_type=F32)
-            smooth[f] = hi + lo
+    pick = lane_iota((21, rows, LANES)) < LANES // 2
+
+    for n in range(tiles // 2):
+        at = slice(2 * n * LANES, (2 * n + 2) * LANES)
+        before = (2 * n - 1 if n else tiles) * LANES
+        after = (2 * n + 2) * LANES
+        edge_hi = jnp.where(pick, fh[:, :, after : after + LANES], fh[:, :, before : before + LANES])
+        edge_lo = jnp.where(pick, fl[:, :, after : after + LANES], fl[:, :, before : before + LANES])
+        lhs_plane = jnp.concatenate([fh[:, :, at], edge_hi, edge_lo, fl[:, :, at]], axis=-1)
+        lhs_plane = lhs_plane.reshape(21 * rows, 6 * LANES)
+        smooth[...] = jnp.dot(lhs_plane, plane_ref[...], preferred_element_type=F32).reshape(21, rows, 2 * LANES)
         for r in range(0, rows, HMAX):
             rr = slice(r, r + HMAX)
             for c in range(2):
@@ -237,15 +225,13 @@
                     den = den + weighted * model
                 acc[0, rr, :] = num
                 acc[1, rr, :] = den
-        return carry
-
-    lax.fori_loop(0, tiles // 2, block_step, 0)
+
     ones = jnp.ones((HMAX, LANES), F32)
     for k in range(2):
         sums = lax.dot_general(
             ones, acc[k], (((1,), (1,)), ((), ())), precision=lax.Precision.HIGHEST, preferred_element_type=F32
         )
-        out_ref[k : k + 1, :] = sums[0:1]
+        out_ref[:, k : k + 1, :] = jnp.broadcast_to(sums[0:1][None], (out_ref.shape[0], 1, rows))
 
 
 def main_call(velocity, strain, heights, reach, znear, zfar, ynear, yfar):
@@ -256,16 +242,16 @@
         main_kernel,
         in_specs=[vmem] * 9,
         out_specs=vmem,
-        out_shape=jax.ShapeDtypeStruct((2, rows), F32),
+        out_shape=jax.ShapeDtypeStruct((lax.axis_size("gz"), 2, rows), F32),
         scratch_shapes=[
             pltpu.VMEM((9, ext, cells + LANES), F32),
             pltpu.VMEM((2 * LANES, 21 * LANES), BF16),
-            pltpu.VMEM((21, rows, cells + 2 * LANES), BF16),
-            pltpu.VMEM((21, rows, cells + 2 * LANES), BF16),
+            pltpu.VMEM((21, rows, cells + LANES), BF16),
+            pltpu.VMEM((21, rows, cells + LANES), BF16),
             pltpu.VMEM((21, rows, 2 * LANES), F32),
             pltpu.VMEM((2, rows, LANES), F32),
         ],
-        compiler_params=pltpu.CompilerParams(vmem_limit_bytes=40 * 1024 * 1024),
+        compiler_params=pltpu.CompilerParams(vmem_limit_bytes=32 * 1024 * 1024),
     )(velocity, strain, heights, reach, znear, zfar, ynear, yfar, plane_filter())
 
 
@@ -291,8 +277,7 @@
     yfar = lax.ppermute(far, "gy", far_pairs("gy", False))
     ynear = lax.ppermute(near, "gy", near_pairs("gy"))
     sums = main_call(velocity, strain, heights, stencil_reach, znear, zfar, ynear, yfar)
-    for mask in (1, 3, 4, 12):
-        sums = sums + lax.ppermute(sums, "gz", [(i, i ^ mask) for i in range(16)])
+    sums = jnp.sum(lax.all_to_all(sums, "gz", 0, 0), axis=0)
     total = lax.axis_size("gz") * cells
     return sums[0] / total / (sums[1] / total + 1e-06)
 

time: 52.9 us -> 42.1 us (0.80)
  the two profiles are of different devices: /device:TPU:4 before, /device:TPU:1 now
where the time goes in v3:
time: 42.1 us; the launch traced here: 41.7 us
  starting transfers between devices  12.6 us (30%)
  blocking collectives  12.3 us (29%)
  Pallas kernels  8.16 us (19%)
  waiting for transfers between devices  5.73 us (14%)
  local copies, waits for them, and re-layouts  2.35 us (6%)
  other arithmetic  0.55 us (1%)
    all_to_all x1, blocking collectives, local(): sums = jnp.sum(lax.all_to_all(sums, 'gz', 0, 0), axis=0)  12.3 us
    pallas_call x1, Pallas kernels, main_call(): pl.pallas_call(main_kernel, in_specs=[vmem] * 9, out_specs=vmem, out_shap...  7.87 us
    ppermute x1, starting transfers between devices, local(): zfar = lax.ppermute(far, 'gz', far_pairs('gz', True))  4.69 us
    ppermute x1, waiting for transfers between devices, local(): yfar = lax.ppermute(far, 'gy', far_pairs('gy', False))  4.16 us
    ppermute x1, starting transfers between devices, local(): yfar = lax.ppermute(far, 'gy', far_pairs('gy', False))  3.15 us
    ppermute x1, starting transfers between devices, local(): znear = lax.ppermute(near, 'gz', near_pairs('gz'))  2.55 us
    unnamed x14, local copies, waits for them, and re-layouts  2.35 us
    ppermute x1, starting transfers between devices, local(): ynear = lax.ppermute(near, 'gy', near_pairs('gy'))  2.17 us
  transfers between devices with their start and end apart: 4, of which 2 were waited for; matrix products, arithmetic and copies ran while one was open for 0% of the time, Pallas kernels for 0%

profile of v3, /device:TPU:1, one launch (start us, length us, event | category | flops | bytes accessed | tf_op | source)
XLA Modules:
  0.0 41.7 jit_solution(5631331886412534585)
XLA Ops:
  0.0 0.0 copy-start
  0.0 1.2 %copy-done = f32[3,96,768]{2,1,0:T(8,128)S(1)} copy-done((f32[3,96,768]{2,1,0:T(8,128)S(1)}, f32[3,96,768]{2,1,0:T(8,128)}, u32[]{:S(2)}) %copy-start) | copy-done | bytes 884760
  1.2 0.0 copy-start.2
  1.2 1.2 %copy-done.2 = bf16[6,96,768]{2,1,0:T(8,128)(2,1)S(1)} copy-done((bf16[6,96,768]{2,1,0:T(8,128)(2,1)S(1)}, bf16[6,96,768]{2,1,0:T(8,128)(2,1)}, u32[]{:S(2)}) %copy-start.2) | copy-done | bytes 884760
  2.3 0.0 copy-start.4
  2.3 0.2 shard_map.55
  2.6 2.5 %collective-permute-start = (f32[96,128]{1,0:T(8,128)S(1)}, f32[96,128]{1,0:T(8,128)S(1)}, u32[]{:S(2)}, u32[]{:S(2)}) collective-permute-start(f32[96,128]{1,0:T(8,128)S(1)} %get-tuple-element.9), channel_id=1, source_target_pairs={{0,1},{1,0},{2,3},{3,2},{4,5},{5,4},{6,7},{7,6},{8,9},{9,8},{10,11... | collective-permute-start | bytes 147464 | tf_op jit(solution)/shard_map/ppermute | solution.py:275
  5.1 0.0 copy-start.5
  5.1 4.7 %collective-permute-start.1 = (f32[96,128]{1,0:T(8,128)S(1)}, f32[96,128]{1,0:T(8,128)S(1)}, u32[]{:S(2)}, u32[]{:S(2)}) collective-permute-start(f32[96,128]{1,0:T(8,128)S(1)} %get-tuple-element.10), channel_id=1, source_target_pairs={{1,2},{2,1},{3,4},{4,3},{5,6},{6,5},{7,8},{8,7},{9,10},{10,9},{11,... | collective-permute-start | bytes 147464 | tf_op jit(solution)/shard_map/ppermute | solution.py:274
  9.8 0.0 collective-permute-done.znear
  9.8 1.6 %collective-permute-done.1.zfar = f32[96,128]{1,0:T(8,128)S(1)} collective-permute-done((f32[96,128]{1,0:T(8,128)S(1)}, f32[96,128]{1,0:T(8,128)S(1)}, u32[]{:S(2)}, u32[]{:S(2)}) %collective-permute-start.1) | collective-permute-done | bytes 49184 | tf_op jit(solution)/shard_map/ppermute | solution.py:274
  11.4 0.0 copy-done.5
  11.4 0.0 copy-start.1
  11.4 0.0 copy-start.3
  11.4 0.1 shard_map.56
  11.5 0.0 copy-start.6
  11.5 2.2 %collective-permute-start.2 = (f32[8,7168]{1,0:T(8,128)S(1)}, f32[8,7168]{1,0:T(8,128)S(1)}, u32[]{:S(2)}, u32[]{:S(2)}) collective-permute-start(f32[8,7168]{1,0:T(8,128)S(1)} %get-tuple-element.11), channel_id=1, source_target_pairs={{0,16},{16,0},{32,48},{48,32},{64,80},{80,64},{96,112},{112,96},{1... | collective-permute-start | bytes 688136 | tf_op jit(solution)/shard_map/ppermute | solution.py:278
  13.6 3.1 %collective-permute-start.3 = (f32[8,7168]{1,0:T(8,128)S(1)}, f32[8,7168]{1,0:T(8,128)S(1)}, u32[]{:S(2)}, u32[]{:S(2)}) collective-permute-start(f32[8,7168]{1,0:T(8,128)S(1)} %get-tuple-element.12), channel_id=1, source_target_pairs={{16,32},{32,16},{48,64},{64,48},{80,96},{96,80},{17,33},{33,17},{4... | collective-permute-start | bytes 688136 | tf_op jit(solution)/shard_map/ppermute | solution.py:277
  16.8 0.0 collective-permute-done.2.ynear
  16.8 4.2 %collective-permute-done.3.yfar = f32[8,7168]{1,0:T(8,128)S(1)} collective-permute-done((f32[8,7168]{1,0:T(8,128)S(1)}, f32[8,7168]{1,0:T(8,128)S(1)}, u32[]{:S(2)}, u32[]{:S(2)}) %collective-permute-start.3) | collective-permute-done | bytes 229408 | tf_op jit(solution)/shard_map/ppermute | solution.py:277
  21.0 0.0 copy-done.4
  21.0 0.0 copy-done.1
  21.0 0.0 copy-done.3
  21.0 0.0 copy-done.6
  21.0 7.9 %shard_map.57 = f32[16,2,96]{2,1,0:T(2,128)S(1)} custom-call(f32[3,96,768]{2,1,0:T(8,128)S(1)} %copy-done.1, bf16[6,96,768]{2,1,0:T(8,128)(2,1)S(1)} %copy-done.3, f32[1,96]{1,0:T(1,128)S(1)} %bitcast.4, s32[2,96]{1,0:T(2,128)S(1)} %copy-done.6, f32[96,128]{1,0:T(8,128)S(1)} %collective-permute-done.znear, f32[96,128]{1,0:T(8,128)S(1)} %collective-permute-done.1.zfar, ...), custom_call_target="tpu_custom_call" | custom-call | tf_op jit(solution)/shard_map/pallas_call | solution.py:241
  28.8 12.3 %all_to_all.5 = f32[16,2,96]{2,1,0:T(2,128)S(1)} all-to-all(f32[16,2,96]{2,1,0:T(2,128)S(1)} %shard_map.57), channel_id=1, replica_groups=mesh['gy'=8,'gz'=16] {'gz'}, dimensions={0} | all-to-all | bytes 24576 | tf_op jit(solution)/shard_map/all_to_all | solution.py:280
  41.2 0.5 %fusion = f32[96]{0:T(128)} fusion(f32[2,96]{1,0:T(2,128)S(1)} %reduce_sum.9), kind=kLoop, calls=%fused_computation.1 | loop fusion | flops 384 | bytes 1152 | tf_op jit(solution)/shard_map/div | solution.py:282
  (1 shorter events, 0.0 us)
Async XLA Ops:
  0.0 1.2 %copy-start = (f32[3,96,768]{2,1,0:T(8,128)S(1)}, f32[3,96,768]{2,1,0:T(8,128)}, u32[]{:S(2)}) copy-start(f32[3,96,768]{2,1,0:T(8,128)} %v_ref.5) | copy-start | bytes 2654212
  1.2 1.2 %copy-start.2 = (bf16[6,96,768]{2,1,0:T(8,128)(2,1)S(1)}, bf16[6,96,768]{2,1,0:T(8,128)(2,1)}, u32[]{:S(2)}) copy-start(bf16[6,96,768]{2,1,0:T(8,128)(2,1)} %s_ref.5) | copy-start | bytes 2654212
  2.3 18.6 %copy-start.4 = (bf16[768,256]{1,0:T(8,128)(2,1)S(1)}, bf16[768,256]{1,0:T(8,128)(2,1)}, u32[]{:S(2)}) copy-start(bf16[768,256]{1,0:T(8,128)(2,1)} %constant.10.clone.plane_ref) | copy-start | bytes 1179652
  2.6 7.2 %collective-permute-start = (f32[96,128]{1,0:T(8,128)S(1)}, f32[96,128]{1,0:T(8,128)S(1)}, u32[]{:S(2)}, u32[]{:S(2)}) collective-permute-start(f32[96,128]{1,0:T(8,128)S(1)} %get-tuple-element.9), channel_id=1, source_target_pairs={{0,1},{1,0},{2,3},{3,2},{4,5},{5,4},{6,7},{7,6},{8,9},{9,8},{10,11... | collective-permute-start | bytes 147464 | tf_op jit(solution)/shard_map/ppermute | solution.py:275
  5.1 6.3 %copy-start.5 = (f32[96]{0:T(128)S(1)}, f32[96]{0:T(128)}, u32[]{:S(2)}) copy-start(f32[96]{0:T(128)} %param.7) | copy-start | bytes 1156
  5.1 6.3 %collective-permute-start.1 = (f32[96,128]{1,0:T(8,128)S(1)}, f32[96,128]{1,0:T(8,128)S(1)}, u32[]{:S(2)}, u32[]{:S(2)}) collective-permute-start(f32[96,128]{1,0:T(8,128)S(1)} %get-tuple-element.10), channel_id=1, source_target_pairs={{1,2},{2,1},{3,4},{4,3},{5,6},{6,5},{7,8},{8,7},{9,10},{10,9},{11,... | collective-permute-start | bytes 147464 | tf_op jit(solution)/shard_map/ppermute | solution.py:274
  11.4 9.6 %copy-start.1 = (f32[3,96,768]{2,1,0:T(8,128)S(1)}, f32[3,96,768]{2,1,0:T(8,128)}, u32[]{:S(2)}) copy-start(f32[3,96,768]{2,1,0:T(8,128)} %v_ref.5) | copy-start | bytes 2654212
  11.4 9.6 %copy-start.3 = (bf16[6,96,768]{2,1,0:T(8,128)(2,1)S(1)}, bf16[6,96,768]{2,1,0:T(8,128)(2,1)}, u32[]{:S(2)}) copy-start(bf16[6,96,768]{2,1,0:T(8,128)(2,1)} %s_ref.5) | copy-start | bytes 2654212
  11.5 9.5 %copy-start.6 = (s32[2,96]{1,0:T(2,128)S(1)}, s32[2,96]{1,0:T(2,128)}, u32[]{:S(2)}) copy-start(s32[2,96]{1,0:T(2,128)} %reach_ref.1) | copy-start | bytes 2308
  11.5 5.3 %collective-permute-start.2 = (f32[8,7168]{1,0:T(8,128)S(1)}, f32[8,7168]{1,0:T(8,128)S(1)}, u32[]{:S(2)}, u32[]{:S(2)}) collective-permute-start(f32[8,7168]{1,0:T(8,128)S(1)} %get-tuple-element.11), channel_id=1, source_target_pairs={{0,16},{16,0},{32,48},{48,32},{64,80},{80,64},{96,112},{112,96},{1... | collective-permute-start | bytes 688136 | tf_op jit(solution)/shard_map/ppermute | solution.py:278
  13.6 7.3 %collective-permute-start.3 = (f32[8,7168]{1,0:T(8,128)S(1)}, f32[8,7168]{1,0:T(8,128)S(1)}, u32[]{:S(2)}, u32[]{:S(2)}) collective-permute-start(f32[8,7168]{1,0:T(8,128)S(1)} %get-tuple-element.12), channel_id=1, source_target_pairs={{16,32},{32,16},{48,64},{64,48},{80,96},{96,80},{17,33},{33,17},{4... | collective-permute-start | bytes 688136 | tf_op jit(solution)/shard_map/ppermute | solution.py:277

commit v4 on v3

v4 whole, which is shorter than its diff:
```python
import jax
import jax.numpy as jnp
from jax import lax
from jax.experimental import pallas as pl
from jax.experimental.pallas import tpu as pltpu
from jax.sharding import PartitionSpec as P

NX = 8
HMAX = 8
LANES = 128
FIELDS = 21
WIDE = 15
FIRST_VMEM = 51 * 1024 * 1024
SMALL_VMEM = 24 * 1024 * 1024
LARGE_VMEM = 24 * 1024 * 1024
LEAD_INDEX = (0, 1, 2, 0, 0, 1)
TAIL_INDEX = (0, 1, 2, 1, 2, 2)
TENSOR_WEIGHTS = (1.0, 1.0, 1.0, 2.0, 2.0, 2.0)
F32 = jnp.float32
BF16 = jnp.bfloat16


def strain_rate(s):
    squares = 2.0 * (s[0] * s[0] + s[1] * s[1] + s[2] * s[2])
    squares = squares + 4.0 * (s[3] * s[3] + s[4] * s[4] + s[5] * s[5])
    return jnp.sqrt(squares)


def lane_iota(shape):
    return lax.broadcasted_iota(jnp.int32, shape, len(shape) - 1)


def rot(x, amount):
    amount = amount % LANES
    return pltpu.roll(x, amount, x.ndim - 1) if amount else x


def plane_filter():
    shape = (3 * LANES, 2 * LANES)
    k = lax.broadcasted_iota(jnp.int32, shape, 0)
    m = lane_iota(shape)
    k = jnp.where(k < 5 * LANES // 2, k, k - 3 * LANES)
    turn = (k - m) & (NX - 1)
    along = jnp.where(turn == 0, 0.5, jnp.where((turn == 1) | (turn == NX - 1), 0.25, 0.0))
    step = ((k + LANES) >> 3) - ((m + LANES) >> 3)
    across = jnp.where(step == 0, 0.5, jnp.where((step == 1) | (step == -1), 0.25, 0.0))
    return (along * across).astype(BF16)


def pack_span_kernel(v_ref, s_ref, near_ref, far_ref, v_out, s_out, plane_ref, sems):
    rows, cells = v_ref.shape[1:]
    spans = ((0, LANES), (cells - LANES, LANES), (LANES, cells - 2 * LANES))
    copies = []
    for i, (start, size) in enumerate(spans):
        for j, (ref, out) in enumerate(((v_ref, v_out), (s_ref, s_out))):
            at = pl.ds(start, size)
            copies.append(pltpu.make_async_copy(ref.at[:, :, at], out.at[:, :, at], sems.at[i, j]))
    for copy in copies:
        copy.start()
    once = plane_filter()
    plane_ref[: 3 * LANES] = once
    plane_ref[3 * LANES :] = once
    for copy in copies[:4]:
        copy.wait()
    lane = lane_iota((rows, LANES))
    left = jnp.zeros((rows, LANES), F32)
    right = jnp.zeros((rows, LANES), F32)
    for f in range(9):
        ref, at = (v_out, f) if f < 3 else (s_out, f - 3)
        here = (lane >= NX * f) & (lane < NX * (f + 1))
        left = jnp.where(here, rot(ref[at, :, :LANES].astype(F32), NX * f), left)
        right = jnp.where(here, rot(ref[at, :, cells - LANES :].astype(F32), NX * f + NX), right)
    odd = lax.axis_index("gz") % 2 == 1
    near_ref[...] = jnp.where(odd, left, right)
    far_ref[...] = jnp.where(odd, right, left)
    for copy in copies[4:]:
        copy.wait()


def pack_span(velocity, strain):
    rows = velocity.shape[1]
    hbm = pl.BlockSpec(memory_space=pltpu.HBM)
    vmem = pl.BlockSpec(memory_space=pltpu.VMEM)
    return pl.pallas_call(
        pack_span_kernel,
        in_specs=[hbm] * 2,
        out_specs=[vmem] * 5,
        out_shape=[jax.ShapeDtypeStruct((rows, LANES), F32)] * 2
        + [jax.ShapeDtypeStruct(x.shape, x.dtype) for x in (velocity, strain)]
        + [jax.ShapeDtypeStruct((6 * LANES, 2 * LANES), BF16)],
        scratch_shapes=[pltpu.SemaphoreType.DMA((3, 2))],
        compiler_params=pltpu.CompilerParams(vmem_limit_bytes=FIRST_VMEM),
    )(velocity, strain)


def pack_wall_kernel(v_ref, s_ref, h_ref, znear, zfar, near_ref, far_ref):
    rows, cells = v_ref.shape[1:]
    gz_odd = lax.axis_index("gz") % 2 == 1
    gy_odd = lax.axis_index("gy") % 2 == 1
    tail = 9 * cells
    lane = lane_iota((HMAX, LANES))
    row = lax.broadcasted_iota(jnp.int32, (HMAX, LANES), 0)
    stamp = (row == 0) & (lane >= 9 * NX) & (lane < 10 * NX)
    heights = jnp.broadcast_to(jnp.pad(h_ref[...], ((0, 0), (0, LANES - rows))), (HMAX, LANES))

    def emit(ref, high):
        r0 = rows - HMAX if high else 0
        for f in range(3):
            ref[:, f * cells : (f + 1) * cells] = v_ref[f, r0 : r0 + HMAX, :]
        for f in range(6):
            part = (s_ref[f, rows - 2 * HMAX :, :] if high else s_ref[f, : 2 * HMAX, :]).astype(F32)
            ref[:, (3 + f) * cells : (4 + f) * cells] = part[HMAX:] if high else part[:HMAX]
        zn = znear[r0 : r0 + HMAX, :]
        zf = zfar[r0 : r0 + HMAX, :]
        zl = jnp.where(gz_odd, zn, zf)
        zr = jnp.where(gz_odd, zf, zn)
        ref[:, tail : tail + LANES] = jnp.where(stamp, rot(heights, 9 * NX - r0), zl)
        ref[:, tail + LANES : tail + 2 * LANES] = zr

    @pl.when(gy_odd)
    def _():
        emit(near_ref, False)
        emit(far_ref, True)

    @pl.when(jnp.logical_not(gy_odd))
    def _():
        emit(near_ref, True)
        emit(far_ref, False)


def pack_wall(velocity, strain, heights, znear, zfar):
    rows, cells = velocity.shape[1:]
    width = 9 * cells + 2 * LANES
    vmem = pl.BlockSpec(memory_space=pltpu.VMEM)
    return pl.pallas_call(
        pack_wall_kernel,
        in_specs=[vmem] * 5,
        out_specs=[vmem] * 2,
        out_shape=[jax.ShapeDtypeStruct((HMAX, width), F32)] * 2,
        compiler_params=pltpu.CompilerParams(vmem_limit_bytes=SMALL_VMEM),
    )(velocity, strain, heights, znear, zfar)


def split2(x):
    hi = x.astype(BF16)
    return hi, (x - hi.astype(F32)).astype(BF16)


def store_fields(u, s, put_high, put_low):
    tensor = [x.astype(F32) for x in s]
    rate = strain_rate(tensor)
    wide = u + [u[a] * u[b] for a, b in zip(LEAD_INDEX, TAIL_INDEX)] + [rate * x for x in tensor]
    for f, value in enumerate(wide):
        hi, lo = split2(value)
        put_high(f, hi)
        put_low(f, lo)
    for f, value in enumerate(s):
        put_high(WIDE + f, value.astype(BF16))


def smooth_block(n, tiles, fh, fl, eh, el, plane_ref):
    rows = fh.shape[1]
    at = slice(2 * n * LANES, (2 * n + 2) * LANES)

    def edge(ref, outer, fields):
        before = ref[fields, :, (2 * n - 1) * LANES : 2 * n * LANES] if n else outer[fields]
        after = ref[fields, :, (2 * n + 2) * LANES : (2 * n + 3) * LANES] if 2 * n + 2 < tiles else outer[fields]
        return jnp.where(lane_iota(before.shape) < LANES // 2, after, before)

    wide, narrow = slice(0, WIDE), slice(WIDE, FIELDS)
    lhs = jnp.concatenate([fh[wide, :, at], edge(fh, eh, wide), fl[wide, :, at], edge(fl, el, wide)], axis=-1)
    first = jnp.dot(lhs.reshape(WIDE * rows, 6 * LANES), plane_ref[...], preferred_element_type=F32)
    lhs = jnp.concatenate([fh[narrow, :, at], edge(fh, eh, narrow)], axis=-1)
    second = jnp.dot(
        lhs.reshape((FIELDS - WIDE) * rows, 3 * LANES), plane_ref[: 3 * LANES], preferred_element_type=F32
    )
    return [first[f * rows : (f + 1) * rows] for f in range(WIDE)] + [
        second[f * rows : (f + 1) * rows] for f in range(FIELDS - WIDE)
    ]


def contract(g, num, den):
    u, p, m, s = g[0:3], g[3:9], g[9:15], g[15:21]
    rate = 4.0 * strain_rate(s)
    for k in range(6):
        leonard = p[k] - u[LEAD_INDEX[k]] * u[TAIL_INDEX[k]]
        model = m[k] - rate * s[k]
        weighted = TENSOR_WEIGHTS[k] * model
        num = num + weighted * leonard
        den = den + weighted * model
    return num, den


def wall_inside(reach_ref, rows, offset, total_planes):
    column = lane_iota((rows, LANES))
    place = jnp.where(column < rows, column, jnp.where(column < rows + HMAX, column - rows - HMAX, column - HMAX))
    row = lax.broadcasted_iota(jnp.int32, (rows, LANES), 0)
    eye = row == column
    reach = jnp.pad(reach_ref[...].astype(F32), ((0, 0), (0, LANES - rows)))
    down = jnp.sum(jnp.where(eye, reach[0:1], 0.0), axis=1, keepdims=True).astype(jnp.int32)
    up = jnp.sum(jnp.where(eye, reach[1:2], 0.0), axis=1, keepdims=True).astype(jnp.int32)
    inside = (place >= row - down) & (place <= row + up) & (place + offset >= 0) & (place + offset < total_planes)
    return inside & (column < rows + 2 * HMAX)


def wall_block(g, lhs_ref, stack, acc_ref, part_ref):
    rows = g[0].shape[0]
    width = 2 * LANES
    for f in range(FIELDS):
        hi, lo = split2(g[f])
        stack[0:rows, f * width : (f + 1) * width] = hi
        stack[LANES : LANES + rows, f * width : (f + 1) * width] = lo
    both = jnp.dot(lhs_ref[...], stack[...], preferred_element_type=F32)
    merged = both[:rows] + both[rows:]
    for f in range(FIELDS):
        part_ref[f, 0:HMAX, :] = merged[0:HMAX, f * width : (f + 1) * width]
        part_ref[f, HMAX:, :] = merged[rows - HMAX :, f * width : (f + 1) * width]
    for r in range(HMAX, rows - HMAX, HMAX):
        num = acc_ref[0, r : r + HMAX, :]
        den = acc_ref[1, r : r + HMAX, :]
        for c in range(2):
            parts = [
                merged[r : r + HMAX, f * width + c * LANES : f * width + (c + 1) * LANES] for f in range(FIELDS)
            ]
            num, den = contract(parts, num, den)
        acc_ref[0, r : r + HMAX, :] = num
        acc_ref[1, r : r + HMAX, :] = den


def clear_gaps(stack, rows):
    gap = jnp.zeros((LANES - rows, stack.shape[1]), BF16)
    stack[rows:LANES, :] = gap
    stack[LANES + rows :, :] = gap


def inner_kernel(v_ref, s_ref, h_ref, reach_ref, plane_ref, fh, fl, lhs_ref, acc_ref, part_ref, stack):
    rows, cells = v_ref.shape[1:]
    tiles = cells // LANES
    total_planes = lax.axis_size("gy") * rows
    offset = lax.axis_index("gy") * rows
    column = lane_iota((rows, LANES))
    row = lax.broadcasted_iota(jnp.int32, (rows, LANES), 0)
    inside = wall_inside(reach_ref, rows, offset, total_planes) & (column < rows)
    hpad = jnp.pad(h_ref[...], ((0, 0), (0, LANES - rows)))
    weights = jnp.where(inside, jnp.broadcast_to(hpad, (rows, LANES)), 0.0)
    whole = (row >= HMAX) & (row < rows - HMAX)
    weights = jnp.where(whole, weights / jnp.sum(weights, axis=1, keepdims=True), weights)
    whi, wlo = split2(weights)
    lhs_ref[0:rows, 0:LANES] = whi
    lhs_ref[0:rows, LANES:] = whi
    lhs_ref[rows:, 0:LANES] = wlo
    lhs_ref[rows:, LANES:] = jnp.zeros_like(wlo)
    clear_gaps(stack, rows)
    acc_ref[...] = jnp.zeros_like(acc_ref)
    for t in range(tiles):
        at = slice(t * LANES, (t + 1) * LANES)
        for r in range(0, rows, 16):
            rr = slice(r, r + 16)

            def put_high(f, x):
                fh[f, rr, at] = x

            def put_low(f, x):
                fl[f, rr, at] = x

            store_fields(
                [v_ref[f, rr, at] for f in range(3)], [s_ref[f, rr, at] for f in range(6)], put_high, put_low
            )
    for n in range(1, tiles // 2 - 1):
        g = smooth_block(n, tiles, fh, fl, None, None, plane_ref)
        wall_block(g, lhs_ref, stack, acc_ref, part_ref.at[n - 1])


def outer_kernel(fh, fl, lhs_ref, acc_in, znear, zfar, plane_ref, acc_ref, part_ref, eh, el, stack):
    rows, cells = fh.shape[1:]
    tiles = cells // LANES
    gz_odd = lax.axis_index("gz") % 2 == 1
    clear_gaps(stack, rows)
    acc_ref[...] = acc_in[...]
    edge_fields(jnp.where(gz_odd, znear[...], zfar[...]), jnp.where(gz_odd, zfar[...], znear[...]), eh, el)
    for i, n in enumerate((0, tiles // 2 - 1)):
        g = smooth_block(n, tiles, fh, fl, eh, el, plane_ref)
        wall_block(g, lhs_ref, stack, acc_ref, part_ref.at[i])


def edge_fields(zl, zr, eh, el):
    rows = zl.shape[0]
    lane = lane_iota((16, LANES))
    for r in range(0, rows, 16):
        rr = slice(r, r + 16)
        raw = [
            jnp.where(
                lane < NX, rot(zr[rr], -NX * f), jnp.where(lane >= LANES - NX, rot(zl[rr], -NX * f - NX), 0.0)
            )
            for f in range(9)
        ]

        def put_high(f, x):
            eh[f, rr, :] = x

        def put_low(f, x):
            el[f, rr, :] = x

        store_fields(raw[:3], raw[3:], put_high, put_low)


def last_kernel(h_ref, reach_ref, ynear, yfar, acc_in, part_inner, part_outer, plane_ref, out_ref, fh, fl, eh, el, stack, acc):
    rows = h_ref.shape[1]
    cells = (ynear.shape[1] - 2 * LANES) // 9
    tiles = cells // LANES
    width = 2 * LANES
    total_planes = lax.axis_size("gy") * rows
    gy = lax.axis_index("gy")
    gy_odd = gy % 2 == 1
    tail = 9 * cells
    both_rows = 2 * HMAX

    def halo(at):
        near, far = ynear[:, at], yfar[:, at]
        return jnp.concatenate([jnp.where(gy_odd, near, far), jnp.where(gy_odd, far, near)], axis=0)

    zl = halo(slice(tail, tail + LANES))
    zr = halo(slice(tail + LANES, tail + 2 * LANES))
    hpad = jnp.pad(h_ref[...], ((0, 0), (0, LANES - rows)))
    hrow = lane_iota((1, LANES))
    below = rot(zl[:HMAX], rows - 9 * NX)[0:1]
    above = rot(zl[HMAX:], rows + HMAX - 9 * NX)[0:1]
    hext = jnp.where(hrow < rows, hpad, jnp.where(hrow < rows + HMAX, below, above))
    inside = wall_inside(reach_ref, rows, gy * rows, total_planes)
    weights = jnp.where(inside, jnp.broadcast_to(hext, (rows, LANES)), 0.0)
    weights = jnp.concatenate([weights[:HMAX], weights[rows - HMAX :]], axis=0)
    scale = 1.0 / jnp.sum(weights, axis=1, keepdims=True)
    lane = lane_iota((both_rows, LANES))
    outside = jnp.where(lane < both_rows, rot(weights, -rows), 0.0)
    whi, wlo = split2(outside)
    twice = whi.astype(F32) + rot(whi.astype(F32), both_rows)
    lhs = jnp.concatenate([twice, wlo.astype(F32)], axis=0).astype(BF16)[:, : 2 * both_rows]

    edge_fields(zl, zr, eh, el)
    for t in range(tiles):
        at = slice(t * LANES, (t + 1) * LANES)

        def put_high(f, x):
            fh[f, :, at] = x

        def put_low(f, x):
            fl[f, :, at] = x

        raw = [halo(slice(f * cells + t * LANES, f * cells + (t + 1) * LANES)) for f in range(9)]
        store_fields(raw[:3], raw[3:], put_high, put_low)

    zero = jnp.zeros((HMAX, LANES), F32)
    sums = [[zero, zero], [zero, zero]]
    for n in range(tiles // 2):
        g = smooth_block(n, tiles, fh, fl, eh, el, plane_ref)
        for f in range(FIELDS):
            hi, lo = split2(g[f])
            stack[0:both_rows, f * width : (f + 1) * width] = hi
            stack[both_rows:, f * width : (f + 1) * width] = lo
        both = jnp.dot(lhs, stack[...], preferred_element_type=F32)
        merged = both[:both_rows] + both[both_rows:]
        if n == 0:
            part = part_outer.at[0]
        elif n == tiles // 2 - 1:
            part = part_outer.at[1]
        else:
            part = part_inner.at[n - 1]
        for i in range(2):
            rr = slice(i * HMAX, (i + 1) * HMAX)
            for c in range(2):
                at = slice(c * LANES, (c + 1) * LANES)
                values = [
                    scale[rr] * (part[f, rr, at] + merged[rr, f * width + c * LANES : f * width + (c + 1) * LANES])
                    for f in range(FIELDS)
                ]
                sums[i] = list(contract(values, *sums[i]))
    ones = jnp.ones((HMAX, LANES), F32)
    for k in range(2):
        acc[0:HMAX, :] = sums[0][k]
        acc[HMAX : rows - HMAX, :] = acc_in[k, HMAX : rows - HMAX, :]
        acc[rows - HMAX :, :] = sums[1][k]
        total = lax.dot_general(
            ones, acc[...], (((1,), (1,)), ((), ())), precision=lax.Precision.HIGHEST, preferred_element_type=F32
        )
        out_ref[:, k : k + 1, :] = jnp.broadcast_to(total[0:1][None], (out_ref.shape[0], 1, rows))


def call(kernel, out_shape, scratch, limit, *operands):
    vmem = pl.BlockSpec(memory_space=pltpu.VMEM)
    return pl.pallas_call(
        kernel,
        in_specs=[vmem] * len(operands),
        out_specs=jax.tree.map(lambda _: vmem, out_shape),
        out_shape=out_shape,
        scratch_shapes=scratch,
        compiler_params=pltpu.CompilerParams(vmem_limit_bytes=limit),
        cost_estimate=pl.CostEstimate(flops=4 * 10**9, bytes_accessed=2**20, transcendentals=0),
    )(*operands)


def inner_call(velocity, strain, heights, reach, plane):
    rows, cells = velocity.shape[1:]
    width = 2 * LANES
    shape = jax.ShapeDtypeStruct
    return call(
        inner_kernel,
        [
            shape((FIELDS, rows, cells), BF16),
            shape((WIDE, rows, cells), BF16),
            shape((2 * rows, width), BF16),
            shape((2, rows, LANES), F32),
            shape((cells // width - 2, FIELDS, 2 * HMAX, width), F32),
        ],
        [pltpu.VMEM((width, FIELDS * width), BF16)],
        LARGE_VMEM,
        velocity,
        strain,
        heights,
        reach,
        plane,
    )


def outer_call(fh, fl, lhs, acc, znear, zfar, plane):
    rows = fh.shape[1]
    width = 2 * LANES
    shape = jax.ShapeDtypeStruct
    return call(
        outer_kernel,
        [shape((2, rows, LANES), F32), shape((2, FIELDS, 2 * HMAX, width), F32)],
        [
            pltpu.VMEM((FIELDS, rows, LANES), BF16),
            pltpu.VMEM((WIDE, rows, LANES), BF16),
            pltpu.VMEM((width, FIELDS * width), BF16),
        ],
        LARGE_VMEM,
        fh,
        fl,
        lhs,
        acc,
        znear,
        zfar,
        plane,
    )


def last_call(heights, reach, ynear, yfar, acc, part_inner, part_outer, plane, cells):
    rows = heights.shape[1]
    width = 2 * LANES
    return call(
        last_kernel,
        jax.ShapeDtypeStruct((lax.axis_size("gz"), 2, rows), F32),
        [
            pltpu.VMEM((FIELDS, 2 * HMAX, cells), BF16),
            pltpu.VMEM((WIDE, 2 * HMAX, cells), BF16),
            pltpu.VMEM((FIELDS, 2 * HMAX, LANES), BF16),
            pltpu.VMEM((WIDE, 2 * HMAX, LANES), BF16),
            pltpu.VMEM((4 * HMAX, FIELDS * width), BF16),
            pltpu.VMEM((rows, LANES), F32),
        ],
        LARGE_VMEM,
        heights,
        reach,
        ynear,
        yfar,
        acc,
        part_inner,
        part_outer,
        plane,
    )


def near_pairs(axis):
    return [(i, i ^ 1) for i in range(lax.axis_size(axis))]


def far_pairs(axis, closed):
    n = lax.axis_size(axis)
    pairs = []
    for i in range(1, n if closed else n - 1, 2):
        pairs += [(i, (i + 1) % n), ((i + 1) % n, i)]
    return pairs


def local(velocity, strain, cell_height, stencil_reach):
    rows, cells = velocity.shape[1:]
    heights = cell_height.reshape(1, rows)
    near, far, velocity, strain, plane = pack_span(velocity, strain)
    zfar = lax.ppermute(far, "gz", far_pairs("gz", True))
    znear = lax.ppermute(near, "gz", near_pairs("gz"))
    fh, fl, lhs, acc, part_inner = inner_call(velocity, strain, heights, stencil_reach, plane)
    near, far = pack_wall(velocity, strain, heights, znear, zfar)
    yfar = lax.ppermute(far, "gy", far_pairs("gy", False))
    ynear = lax.ppermute(near, "gy", near_pairs("gy"))
    acc, part_outer = outer_call(fh, fl, lhs, acc, znear, zfar, plane)
    sums = last_call(heights, stencil_reach, ynear, yfar, acc, part_inner, part_outer, plane, cells)
    sums = jnp.sum(lax.all_to_all(sums, "gz", 0, 0), axis=0)
    total = lax.axis_size("gz") * cells
    return sums[0] / total / (sums[1] / total + 1e-06)


def solution(mesh):
    in_specs = (P(None, "gy", "gz"), P(None, "gy", "gz"), P("gy"), P(None, "gy"))
    return jax.shard_map(local, mesh=mesh, in_specs=in_specs, out_specs=P("gy"), check_vma=False)
```

time: 42.1 us -> 34.8 us (0.83)
  waiting for transfers between devices: 5.73 us -> 0.59 us
  Pallas kernels: 8.16 us -> 10.2 us
  blocking collectives: 12.3 us -> 10.3 us
  starting transfers between devices: 12.6 us -> 11.5 us
  local copies, waits for them, and re-layouts: 2.35 us -> 1.34 us
    ppermute x1, waiting for transfers between devices: 4.16 us -> 0.58 us  [local(): yfar = lax.ppermute(far, 'gy', far_pairs('gy', False))]
    all_to_all x1, blocking collectives: 12.3 us -> 10.3 us  [local(): sums = jnp.sum(lax.all_to_all(sums, 'gz', 0, 0), axis=0)]
    pallas_call x2 -> x4, Pallas kernels: 8.08 us -> 10.1 us  [the longest x3 8.48 us: call(): pl.pallas_call(kernel, in_specs=[vmem] * len(operands), out_specs=jax.tre...]
    ppermute x1, waiting for transfers between devices: 1.56 us -> 0.01 us  [local(): zfar = lax.ppermute(far, 'gz', far_pairs('gz', True))]
    unnamed x14 -> x8, local copies, waits for them, and re-layouts: 2.35 us -> 1.34 us
    ppermute x1, starting transfers between devices: 2.17 us -> 1.29 us  [local(): ynear = lax.ppermute(near, 'gy', near_pairs('gy'))]
  transfers between devices with their start and end apart: 4 -> 4, of which waited for: 2 -> 1; matrix products, arithmetic and copies ran while one was open for 0% -> 0% of each run, Pallas kernels for 0% -> 19%
where the time goes in v4:
time: 34.8 us; the launch traced here: 34.6 us
  starting transfers between devices  11.5 us (33%)
  blocking collectives  10.3 us (30%)
  Pallas kernels  10.2 us (29%)
  local copies, waits for them, and re-layouts  1.34 us (4%)
  waiting for transfers between devices  0.59 us (2%)
  other arithmetic  0.55 us (2%)
    all_to_all x1, blocking collectives, local(): sums = jnp.sum(lax.all_to_all(sums, 'gz', 0, 0), axis=0)  10.3 us
    pallas_call x3, Pallas kernels, call(): pl.pallas_call(kernel, in_specs=[vmem] * len(operands), out_specs=jax.tre...  8.48 us
    ppermute x1, starting transfers between devices, local(): zfar = lax.ppermute(far, 'gz', far_pairs('gz', True))  4.69 us
    ppermute x1, starting transfers between devices, local(): yfar = lax.ppermute(far, 'gy', far_pairs('gy', False))  3.02 us
    ppermute x1, starting transfers between devices, local(): znear = lax.ppermute(near, 'gz', near_pairs('gz'))  2.55 us
    pallas_call x1, Pallas kernels, pack_span(): pl.pallas_call(pack_span_kernel, in_specs=[hbm] * 2, out_specs=[vmem] * 5...  1.61 us
    unnamed x8, local copies, waits for them, and re-layouts  1.34 us
    ppermute x1, starting transfers between devices, local(): ynear = lax.ppermute(near, 'gy', near_pairs('gy'))  1.29 us
  transfers between devices with their start and end apart: 4, of which 1 were waited for; matrix products, arithmetic and copies ran while one was open for 0% of the time, Pallas kernels for 19%

profile of v4, /device:TPU:1, one launch (start us, length us, event | category | flops | bytes accessed | tf_op | source)
XLA Modules:
  0.0 34.6 jit_solution(151576224380942763)
XLA Ops:
  0.0 1.6 %shard_map.46 = (f32[96,128]{1,0:T(8,128)S(1)}, f32[96,128]{1,0:T(8,128)S(1)}, f32[3,96,768]{2,1,0:T(8,128)S(1)}, bf16[6,96,768]{2,1,0:T(8,128)(2,1)S(1)}, bf16[768,256]{1,0:T(8,128)(2,1)S(1)}) custom-call(f32[3,96,768]{2,1,0:T(8,128)} %v_ref.1, bf16[6,96,768]{2,1,0:T(8,128)(2,1)} %s_ref.1), custom_call_target="tpu_custom_call" | custom-call | tf_op jit(solution)/shard_map/pallas_call | solution.py:84
  1.6 2.5 %collective-permute-start = (f32[96,128]{1,0:T(8,128)S(1)}, f32[96,128]{1,0:T(8,128)S(1)}, u32[]{:S(2)}, u32[]{:S(2)}) collective-permute-start(f32[96,128]{1,0:T(8,128)S(1)} %get-tuple-element.21), channel_id=1, source_target_pairs={{0,1},{1,0},{2,3},{3,2},{4,5},{5,4},{6,7},{7,6},{8,9},{9,8},{10,11... | collective-permute-start | bytes 147464 | tf_op jit(solution)/shard_map/ppermute | solution.py:490
  4.2 4.7 %collective-permute-start.1 = (f32[96,128]{1,0:T(8,128)S(1)}, f32[96,128]{1,0:T(8,128)S(1)}, u32[]{:S(2)}, u32[]{:S(2)}) collective-permute-start(f32[96,128]{1,0:T(8,128)S(1)} %get-tuple-element.22), channel_id=1, source_target_pairs={{1,2},{2,1},{3,4},{4,3},{5,6},{6,5},{7,8},{8,7},{9,10},{10,9},{11,... | collective-permute-start | bytes 147464 | tf_op jit(solution)/shard_map/ppermute | solution.py:489
  8.9 0.0 copy-start
  8.9 0.7 %copy-done = f32[96]{0:T(128)S(1)} copy-done((f32[96]{0:T(128)S(1)}, f32[96]{0:T(128)}, u32[]{:S(2)}) %copy-start) | copy-done | bytes 408
  9.5 0.0 copy-start.2
  9.5 0.7 %copy-done.2 = s32[2,96]{1,0:T(2,128)S(1)} copy-done((s32[2,96]{1,0:T(2,128)S(1)}, s32[2,96]{1,0:T(2,128)}, u32[]{:S(2)}) %copy-start.2) | copy-done | bytes 792
  10.2 0.0 copy-start.1
  10.2 3.0 %shard_map.48 = (bf16[21,96,768]{2,1,0:T(8,128)(2,1)S(1)}, bf16[15,96,768]{2,1,0:T(8,128)(2,1)S(1)}, bf16[192,256]{1,0:T(8,128)(2,1)S(1)}, f32[2,96,128]{2,1,0:T(8,128)S(1)}, f32[1,21,16,256]{3,2,1,0:T(8,128)S(1)}) custom-call(f32[3,96,768]{2,1,0:T(8,128)S(1)} %get-tuple-element.19.v_ref, bf16[6,96,768]{2,1,0:T(8,128)(2,1)S(1)} %get-tuple-element.20.s_ref, ...), custom_call_target="tpu_custom_call" | custom-call | flops 4000000000 | bytes 1048576 | tf_op jit(solution)/shard_map/pallas_call | solution.py:390
  13.2 0.0 collective-permute-done.znear
  13.2 0.0 collective-permute-done.1.zfar
  13.3 0.0 copy-done.1
  13.3 0.1 shard_map.47
  13.4 1.3 %collective-permute-start.2 = (f32[8,7168]{1,0:T(8,128)S(1)}, f32[8,7168]{1,0:T(8,128)S(1)}, u32[]{:S(2)}, u32[]{:S(2)}) collective-permute-start(f32[8,7168]{1,0:T(8,128)S(1)} %get-tuple-element.23), channel_id=1, source_target_pairs={{0,16},{16,0},{32,48},{48,32},{64,80},{80,64},{96,112},{112,96},{1... | collective-permute-start | bytes 688136 | tf_op jit(solution)/shard_map/ppermute | solution.py:494
  14.7 3.0 %collective-permute-start.3 = (f32[8,7168]{1,0:T(8,128)S(1)}, f32[8,7168]{1,0:T(8,128)S(1)}, u32[]{:S(2)}, u32[]{:S(2)}) collective-permute-start(f32[8,7168]{1,0:T(8,128)S(1)} %get-tuple-element.24), channel_id=1, source_target_pairs={{16,32},{32,16},{48,64},{64,48},{80,96},{96,80},{17,33},{33,17},{4... | collective-permute-start | bytes 688136 | tf_op jit(solution)/shard_map/ppermute | solution.py:493
  17.7 0.0 copy-start.3
  17.7 3.7 %shard_map.49 = (f32[2,96,128]{2,1,0:T(8,128)S(1)}, f32[2,21,16,256]{3,2,1,0:T(8,128)S(1)}) custom-call(bf16[21,96,768]{2,1,0:T(8,128)(2,1)S(1)} %get-tuple-element.26.fh, bf16[15,96,768]{2,1,0:T(8,128)(2,1)S(1)} %get-tuple-element.27.fl, bf16[192,256]{1,0:T(8,128)(2,1)S(1)} %get-tuple-element.28.lhs_ref, f32[2,96,128]{2,1,0:T(8,128)S(1)} %get-tuple-element.29.acc_in, ...), custom_call_target="tpu_custom_call" | custom-call | flops 4000000000 | bytes 1048576 | tf_op jit(solution)/shard_map/pallas_call | solution.py:390
  21.4 0.0 collective-permute-done.2.ynear
  21.4 0.6 %collective-permute-done.3.yfar = f32[8,7168]{1,0:T(8,128)S(1)} collective-permute-done((f32[8,7168]{1,0:T(8,128)S(1)}, f32[8,7168]{1,0:T(8,128)S(1)}, u32[]{:S(2)}, u32[]{:S(2)}) %collective-permute-start.3) | collective-permute-done | bytes 229408 | tf_op jit(solution)/shard_map/ppermute | solution.py:493
  22.0 0.0 copy-done.3
  22.0 1.7 %shard_map.50 = f32[16,2,96]{2,1,0:T(2,128)S(1)} custom-call(f32[1,96]{1,0:T(1,128)S(1)} %bitcast.5, s32[2,96]{1,0:T(2,128)S(1)} %copy-done.3, f32[8,7168]{1,0:T(8,128)S(1)} %collective-permute-done.2.ynear, f32[8,7168]{1,0:T(8,128)S(1)} %collective-permute-done.3.yfar, f32[2,96,128]{2,1,0:T(8,128)S(1)} %get-tuple-element.30.acc_in, ...), custom_call_target="tpu_custom_call" | custom-call | flops 4000000000 | bytes 1048576 | tf_op jit(solution)/shard_map/pallas_call | solution.py:390
  23.7 10.3 %all_to_all.5 = f32[16,2,96]{2,1,0:T(2,128)S(1)} all-to-all(f32[16,2,96]{2,1,0:T(2,128)S(1)} %shard_map.50), channel_id=1, replica_groups=mesh['gy'=8,'gz'=16] {'gz'}, dimensions={0} | all-to-all | bytes 24576 | tf_op jit(solution)/shard_map/all_to_all | solution.py:497
  34.1 0.5 %fusion = f32[96]{0:T(128)} fusion(f32[2,96]{1,0:T(2,128)S(1)} %reduce_sum.9), kind=kLoop, calls=%fused_computation.1 | loop fusion | flops 384 | bytes 1152 | tf_op jit(solution)/shard_map/div | solution.py:499
  (1 shorter events, 0.0 us)
Async XLA Ops:
  1.6 11.6 %collective-permute-start = (f32[96,128]{1,0:T(8,128)S(1)}, f32[96,128]{1,0:T(8,128)S(1)}, u32[]{:S(2)}, u32[]{:S(2)}) collective-permute-start(f32[96,128]{1,0:T(8,128)S(1)} %get-tuple-element.21), channel_id=1, source_target_pairs={{0,1},{1,0},{2,3},{3,2},{4,5},{5,4},{6,7},{7,6},{8,9},{9,8},{10,11... | collective-permute-start | bytes 147464 | tf_op jit(solution)/shard_map/ppermute | solution.py:490
  4.2 9.1 %collective-permute-start.1 = (f32[96,128]{1,0:T(8,128)S(1)}, f32[96,128]{1,0:T(8,128)S(1)}, u32[]{:S(2)}, u32[]{:S(2)}) collective-permute-start(f32[96,128]{1,0:T(8,128)S(1)} %get-tuple-element.22), channel_id=1, source_target_pairs={{1,2},{2,1},{3,4},{4,3},{5,6},{6,5},{7,8},{8,7},{9,10},{10,9},{11,... | collective-permute-start | bytes 147464 | tf_op jit(solution)/shard_map/ppermute | solution.py:489
  8.9 0.7 %copy-start = (f32[96]{0:T(128)S(1)}, f32[96]{0:T(128)}, u32[]{:S(2)}) copy-start(f32[96]{0:T(128)} %param.6) | copy-start | bytes 1156
  9.5 0.7 %copy-start.2 = (s32[2,96]{1,0:T(2,128)S(1)}, s32[2,96]{1,0:T(2,128)}, u32[]{:S(2)}) copy-start(s32[2,96]{1,0:T(2,128)} %reach_ref.3) | copy-start | bytes 2308
  10.2 3.1 %copy-start.1 = (f32[96]{0:T(128)S(1)}, f32[96]{0:T(128)}, u32[]{:S(2)}) copy-start(f32[96]{0:T(128)} %param.6) | copy-start | bytes 1156
  13.4 8.0 %collective-permute-start.2 = (f32[8,7168]{1,0:T(8,128)S(1)}, f32[8,7168]{1,0:T(8,128)S(1)}, u32[]{:S(2)}, u32[]{:S(2)}) collective-permute-start(f32[8,7168]{1,0:T(8,128)S(1)} %get-tuple-element.23), channel_id=1, source_target_pairs={{0,16},{16,0},{32,48},{48,32},{64,80},{80,64},{96,112},{112,96},{1... | collective-permute-start | bytes 688136 | tf_op jit(solution)/shard_map/ppermute | solution.py:494
  14.7 7.3 %collective-permute-start.3 = (f32[8,7168]{1,0:T(8,128)S(1)}, f32[8,7168]{1,0:T(8,128)S(1)}, u32[]{:S(2)}, u32[]{:S(2)}) collective-permute-start(f32[8,7168]{1,0:T(8,128)S(1)} %get-tuple-element.24), channel_id=1, source_target_pairs={{16,32},{32,16},{48,64},{64,48},{80,96},{96,80},{17,33},{33,17},{4... | collective-permute-start | bytes 688136 | tf_op jit(solution)/shard_map/ppermute | solution.py:493
  17.7 4.3 %copy-start.3 = (s32[2,96]{1,0:T(2,128)S(1)}, s32[2,96]{1,0:T(2,128)}, u32[]{:S(2)}) copy-start(s32[2,96]{1,0:T(2,128)} %reach_ref.3) | copy-start | bytes 2308

commit v5 on v4

--- a/solution.py
+++ b/solution.py
@@ -179,11 +179,12 @@
     ]
 
 
-def contract(g, num, den):
+def contract(g, inv, num, den):
     u, p, m, s = g[0:3], g[3:9], g[9:15], g[15:21]
-    rate = 4.0 * strain_rate(s)
+    rate = 4.0 * inv * strain_rate(s)
+    scaled = [inv * x for x in u]
     for k in range(6):
-        leonard = p[k] - u[LEAD_INDEX[k]] * u[TAIL_INDEX[k]]
+        leonard = p[k] - scaled[LEAD_INDEX[k]] * u[TAIL_INDEX[k]]
         model = m[k] - rate * s[k]
         weighted = TENSOR_WEIGHTS[k] * model
         num = num + weighted * leonard
@@ -191,67 +192,54 @@
     return num, den
 
 
-def wall_inside(reach_ref, rows, offset, total_planes):
-    column = lane_iota((rows, LANES))
-    place = jnp.where(column < rows, column, jnp.where(column < rows + HMAX, column - rows - HMAX, column - HMAX))
-    row = lax.broadcasted_iota(jnp.int32, (rows, LANES), 0)
-    eye = row == column
-    reach = jnp.pad(reach_ref[...].astype(F32), ((0, 0), (0, LANES - rows)))
-    down = jnp.sum(jnp.where(eye, reach[0:1], 0.0), axis=1, keepdims=True).astype(jnp.int32)
-    up = jnp.sum(jnp.where(eye, reach[1:2], 0.0), axis=1, keepdims=True).astype(jnp.int32)
-    inside = (place >= row - down) & (place <= row + up) & (place + offset >= 0) & (place + offset < total_planes)
-    return inside & (column < rows + 2 * HMAX)
-
-
-def wall_block(g, lhs_ref, stack, acc_ref, part_ref):
+def to_column(row_vector, size):
+    shape = (size, LANES)
+    eye = lax.broadcasted_iota(jnp.int32, shape, 0) == lane_iota(shape)
+    return jnp.sum(jnp.where(eye, jnp.broadcast_to(row_vector, shape), 0.0), axis=1, keepdims=True)
+
+
+def pad_lanes(x):
+    return jnp.pad(x, ((0, 0), (0, LANES - x.shape[1])))
+
+
+def wall_inside(reach_ref, place, rows):
+    gy = lax.axis_index("gy")
+    reach = pad_lanes(reach_ref[...].astype(F32))
+    down = to_column(reach[0:1], rows).astype(jnp.int32)
+    up = to_column(reach[1:2], rows).astype(jnp.int32)
+    row = lax.broadcasted_iota(jnp.int32, place.shape, 0)
+    lowest = jnp.maximum(row - down, -gy * rows)
+    highest = jnp.minimum(row + up, (lax.axis_size("gy") - gy) * rows - 1)
+    return (place >= lowest) & (place <= highest)
+
+
+def wall_block(g, mask, height, inv, stack, acc_ref, part_ref):
     rows = g[0].shape[0]
     width = 2 * LANES
     for f in range(FIELDS):
-        hi, lo = split2(g[f])
+        hi, lo = split2(g[f] * height)
         stack[0:rows, f * width : (f + 1) * width] = hi
-        stack[LANES : LANES + rows, f * width : (f + 1) * width] = lo
-    both = jnp.dot(lhs_ref[...], stack[...], preferred_element_type=F32)
-    merged = both[:rows] + both[rows:]
+        stack[rows:, f * width : (f + 1) * width] = lo
+    merged = jnp.dot(mask, stack[...], preferred_element_type=F32)
     for f in range(FIELDS):
         part_ref[f, 0:HMAX, :] = merged[0:HMAX, f * width : (f + 1) * width]
         part_ref[f, HMAX:, :] = merged[rows - HMAX :, f * width : (f + 1) * width]
     for r in range(HMAX, rows - HMAX, HMAX):
         num = acc_ref[0, r : r + HMAX, :]
         den = acc_ref[1, r : r + HMAX, :]
+        scale = jnp.broadcast_to(inv[r : r + HMAX], (HMAX, LANES))
         for c in range(2):
             parts = [
                 merged[r : r + HMAX, f * width + c * LANES : f * width + (c + 1) * LANES] for f in range(FIELDS)
             ]
-            num, den = contract(parts, num, den)
+            num, den = contract(parts, scale, num, den)
         acc_ref[0, r : r + HMAX, :] = num
         acc_ref[1, r : r + HMAX, :] = den
 
 
-def clear_gaps(stack, rows):
-    gap = jnp.zeros((LANES - rows, stack.shape[1]), BF16)
-    stack[rows:LANES, :] = gap
-    stack[LANES + rows :, :] = gap
-
-
-def inner_kernel(v_ref, s_ref, h_ref, reach_ref, plane_ref, fh, fl, lhs_ref, acc_ref, part_ref, stack):
+def inner_kernel(v_ref, s_ref, plane_ref, fh, fl, smooth):
     rows, cells = v_ref.shape[1:]
     tiles = cells // LANES
-    total_planes = lax.axis_size("gy") * rows
-    offset = lax.axis_index("gy") * rows
-    column = lane_iota((rows, LANES))
-    row = lax.broadcasted_iota(jnp.int32, (rows, LANES), 0)
-    inside = wall_inside(reach_ref, rows, offset, total_planes) & (column < rows)
-    hpad = jnp.pad(h_ref[...], ((0, 0), (0, LANES - rows)))
-    weights = jnp.where(inside, jnp.broadcast_to(hpad, (rows, LANES)), 0.0)
-    whole = (row >= HMAX) & (row < rows - HMAX)
-    weights = jnp.where(whole, weights / jnp.sum(weights, axis=1, keepdims=True), weights)
-    whi, wlo = split2(weights)
-    lhs_ref[0:rows, 0:LANES] = whi
-    lhs_ref[0:rows, LANES:] = whi
-    lhs_ref[rows:, 0:LANES] = wlo
-    lhs_ref[rows:, LANES:] = jnp.zeros_like(wlo)
-    clear_gaps(stack, rows)
-    acc_ref[...] = jnp.zeros_like(acc_ref)
     for t in range(tiles):
         at = slice(t * LANES, (t + 1) * LANES)
         for r in range(0, rows, 16):
@@ -268,19 +256,31 @@
             )
     for n in range(1, tiles // 2 - 1):
         g = smooth_block(n, tiles, fh, fl, None, None, plane_ref)
-        wall_block(g, lhs_ref, stack, acc_ref, part_ref.at[n - 1])
-
-
-def outer_kernel(fh, fl, lhs_ref, acc_in, znear, zfar, plane_ref, acc_ref, part_ref, eh, el, stack):
+        for f in range(FIELDS):
+            smooth[n - 1, f] = g[f]
+
+
+def outer_kernel(h_ref, reach_ref, fh, fl, smooth, znear, zfar, plane_ref, acc_ref, part_ref, eh, el, stack):
     rows, cells = fh.shape[1:]
     tiles = cells // LANES
     gz_odd = lax.axis_index("gz") % 2 == 1
-    clear_gaps(stack, rows)
-    acc_ref[...] = acc_in[...]
+    column = lane_iota((rows, 2 * LANES))
+    place = jnp.where(column < rows, column, column - rows)
+    inside = wall_inside(reach_ref, place, rows)
+    mask = jnp.where(inside, 1.0, 0.0)[:, : 2 * rows].astype(BF16)
+    heights = pad_lanes(h_ref[...])
+    height = to_column(heights, rows)
+    first = (column < rows) & inside
+    total = jnp.sum(jnp.where(first, jnp.pad(heights, ((0, 0), (0, LANES))), 0.0), axis=1, keepdims=True)
+    inv = 1.0 / total
+    acc_ref[...] = jnp.zeros_like(acc_ref)
     edge_fields(jnp.where(gz_odd, znear[...], zfar[...]), jnp.where(gz_odd, zfar[...], znear[...]), eh, el)
-    for i, n in enumerate((0, tiles // 2 - 1)):
-        g = smooth_block(n, tiles, fh, fl, eh, el, plane_ref)
-        wall_block(g, lhs_ref, stack, acc_ref, part_ref.at[i])
+    for n in range(tiles // 2):
+        if 0 < n < tiles // 2 - 1:
+            g = [smooth[n - 1, f] for f in range(FIELDS)]
+        else:
+            g = smooth_block(n, tiles, fh, fl, eh, el, plane_ref)
+        wall_block(g, mask, height, inv, stack.at[n], acc_ref, part_ref.at[n])
 
 
 def edge_fields(zl, zr, eh, el):
@@ -304,14 +304,12 @@
         store_fields(raw[:3], raw[3:], put_high, put_low)
 
 
-def last_kernel(h_ref, reach_ref, ynear, yfar, acc_in, part_inner, part_outer, plane_ref, out_ref, fh, fl, eh, el, stack, acc):
+def last_kernel(h_ref, reach_ref, ynear, yfar, acc_in, part, plane_ref, out_ref, fh, fl, eh, el, stack, acc):
     rows = h_ref.shape[1]
     cells = (ynear.shape[1] - 2 * LANES) // 9
     tiles = cells // LANES
     width = 2 * LANES
-    total_planes = lax.axis_size("gy") * rows
-    gy = lax.axis_index("gy")
-    gy_odd = gy % 2 == 1
+    gy_odd = lax.axis_index("gy") % 2 == 1
     tail = 9 * cells
     both_rows = 2 * HMAX
 
@@ -321,20 +319,22 @@
 
     zl = halo(slice(tail, tail + LANES))
     zr = halo(slice(tail + LANES, tail + 2 * LANES))
-    hpad = jnp.pad(h_ref[...], ((0, 0), (0, LANES - rows)))
+    below = rot(zl[:HMAX], -9 * NX)[0:1]
+    above = rot(zl[HMAX:], -9 * NX)[0:1]
+    height = jnp.concatenate([to_column(below, HMAX), to_column(above, HMAX)], axis=0)
+    column = lane_iota((rows, LANES))
+    place = jnp.where(column < rows, column, jnp.where(column < rows + HMAX, column - rows - HMAX, column - HMAX))
     hrow = lane_iota((1, LANES))
-    below = rot(zl[:HMAX], rows - 9 * NX)[0:1]
-    above = rot(zl[HMAX:], rows + HMAX - 9 * NX)[0:1]
-    hext = jnp.where(hrow < rows, hpad, jnp.where(hrow < rows + HMAX, below, above))
-    inside = wall_inside(reach_ref, rows, gy * rows, total_planes)
-    weights = jnp.where(inside, jnp.broadcast_to(hext, (rows, LANES)), 0.0)
-    weights = jnp.concatenate([weights[:HMAX], weights[rows - HMAX :]], axis=0)
-    scale = 1.0 / jnp.sum(weights, axis=1, keepdims=True)
+    heights = jnp.where(
+        hrow < rows, pad_lanes(h_ref[...]), jnp.where(hrow < rows + HMAX, rot(below, rows), rot(above, rows + HMAX))
+    )
+    inside = wall_inside(reach_ref, place, rows) & (column < rows + both_rows)
+    inv = 1.0 / jnp.sum(jnp.where(inside, jnp.broadcast_to(heights, (rows, LANES)), 0.0), axis=1, keepdims=True)
+    scale = [jnp.broadcast_to(inv[r : r + HMAX], (HMAX, LANES)) for r in (0, rows - HMAX)]
+    mask = jnp.where(inside, 1.0, 0.0)
+    mask = rot(jnp.concatenate([mask[:HMAX], mask[rows - HMAX :]], axis=0), -rows)
     lane = lane_iota((both_rows, LANES))
-    outside = jnp.where(lane < both_rows, rot(weights, -rows), 0.0)
-    whi, wlo = split2(outside)
-    twice = whi.astype(F32) + rot(whi.astype(F32), both_rows)
-    lhs = jnp.concatenate([twice, wlo.astype(F32)], axis=0).astype(BF16)[:, : 2 * both_rows]
+    mask = jnp.where(lane < both_rows, mask, rot(mask, both_rows))[:, : 2 * both_rows].astype(BF16)
 
     edge_fields(zl, zr, eh, el)
     for t in range(tiles):
@@ -354,33 +354,26 @@
     for n in range(tiles // 2):
         g = smooth_block(n, tiles, fh, fl, eh, el, plane_ref)
         for f in range(FIELDS):
-            hi, lo = split2(g[f])
+            hi, lo = split2(g[f] * height)
             stack[0:both_rows, f * width : (f + 1) * width] = hi
             stack[both_rows:, f * width : (f + 1) * width] = lo
-        both = jnp.dot(lhs, stack[...], preferred_element_type=F32)
-        merged = both[:both_rows] + both[both_rows:]
-        if n == 0:
-            part = part_outer.at[0]
-        elif n == tiles // 2 - 1:
-            part = part_outer.at[1]
-        else:
-            part = part_inner.at[n - 1]
+        merged = jnp.dot(mask, stack[...], preferred_element_type=F32)
         for i in range(2):
             rr = slice(i * HMAX, (i + 1) * HMAX)
             for c in range(2):
                 at = slice(c * LANES, (c + 1) * LANES)
                 values = [
-                    scale[rr] * (part[f, rr, at] + merged[rr, f * width + c * LANES : f * width + (c + 1) * LANES])
+                    part[n, f, rr, at] + merged[rr, f * width + c * LANES : f * width + (c + 1) * LANES]
                     for f in range(FIELDS)
                 ]
-                sums[i] = list(contract(values, *sums[i]))
+                sums[i] = list(contract(values, scale[i], *sums[i]))
     ones = jnp.ones((HMAX, LANES), F32)
     for k in range(2):
         acc[0:HMAX, :] = sums[0][k]
         acc[HMAX : rows - HMAX, :] = acc_in[k, HMAX : rows - HMAX, :]
         acc[rows - HMAX :, :] = sums[1][k]
         total = lax.dot_general(
-            ones, acc[...], (((1,), (1,)), ((), ())), precision=lax.Precision.HIGHEST, preferred_element_type=F32
+            ones, acc[...] * (inv * inv), (((1,), (1,)), ((), ())), precision=lax.Precision.HIGHEST, preferred_element_type=F32
         )
         out_ref[:, k : k + 1, :] = jnp.broadcast_to(total[0:1][None], (out_ref.shape[0], 1, rows))
 
@@ -398,7 +391,7 @@
     )(*operands)
 
 
-def inner_call(velocity, strain, heights, reach, plane):
+def inner_call(velocity, strain, plane):
     rows, cells = velocity.shape[1:]
     width = 2 * LANES
     shape = jax.ShapeDtypeStruct
@@ -407,44 +400,41 @@
         [
             shape((FIELDS, rows, cells), BF16),
             shape((WIDE, rows, cells), BF16),
-            shape((2 * rows, width), BF16),
-            shape((2, rows, LANES), F32),
-            shape((cells // width - 2, FIELDS, 2 * HMAX, width), F32),
+            shape((cells // width - 2, FIELDS, rows, width), F32),
         ],
-        [pltpu.VMEM((width, FIELDS * width), BF16)],
+        [],
         LARGE_VMEM,
         velocity,
         strain,
-        heights,
-        reach,
         plane,
     )
 
 
-def outer_call(fh, fl, lhs, acc, znear, zfar, plane):
-    rows = fh.shape[1]
+def outer_call(heights, reach, fh, fl, smooth, znear, zfar, plane):
+    rows, cells = fh.shape[1:]
     width = 2 * LANES
     shape = jax.ShapeDtypeStruct
     return call(
         outer_kernel,
-        [shape((2, rows, LANES), F32), shape((2, FIELDS, 2 * HMAX, width), F32)],
+        [shape((2, rows, LANES), F32), shape((cells // width, FIELDS, 2 * HMAX, width), F32)],
         [
             pltpu.VMEM((FIELDS, rows, LANES), BF16),
             pltpu.VMEM((WIDE, rows, LANES), BF16),
-            pltpu.VMEM((width, FIELDS * width), BF16),
+            pltpu.VMEM((cells // width, 2 * rows, FIELDS * width), BF16),
         ],
         LARGE_VMEM,
+        heights,
+        reach,
         fh,
         fl,
-        lhs,
-        acc,
+        smooth,
         znear,
         zfar,
         plane,
     )
 
 
-def last_call(heights, reach, ynear, yfar, acc, part_inner, part_outer, plane, cells):
+def last_call(heights, reach, ynear, yfar, acc, part, plane, cells):
     rows = heights.shape[1]
     width = 2 * LANES
     return call(
@@ -464,8 +454,7 @@
         ynear,
         yfar,
         acc,
-        part_inner,
-        part_outer,
+        part,
         plane,
     )
 
@@ -488,12 +477,12 @@
     near, far, velocity, strain, plane = pack_span(velocity, strain)
     zfar = lax.ppermute(far, "gz", far_pairs("gz", True))
     znear = lax.ppermute(near, "gz", near_pairs("gz"))
-    fh, fl, lhs, acc, part_inner = inner_call(velocity, strain, heights, stencil_reach, plane)
+    fh, fl, smooth = inner_call(velocity, strain, plane)
     near, far = pack_wall(velocity, strain, heights, znear, zfar)
     yfar = lax.ppermute(far, "gy", far_pairs("gy", False))
     ynear = lax.ppermute(near, "gy", near_pairs("gy"))
-    acc, part_outer = outer_call(fh, fl, lhs, acc, znear, zfar, plane)
-    sums = last_call(heights, stencil_reach, ynear, yfar, acc, part_inner, part_outer, plane, cells)
+    acc, part = outer_call(heights, stencil_reach, fh, fl, smooth, znear, zfar, plane)
+    sums = last_call(heights, stencil_reach, ynear, yfar, acc, part, plane, cells)
     sums = jnp.sum(lax.all_to_all(sums, "gz", 0, 0), axis=0)
     total = lax.axis_size("gz") * cells
     return sums[0] / total / (sums[1] / total + 1e-06)

time: 34.8 us -> 34.7 us (level)
  blocking collectives: 10.3 us -> 12.3 us
  local copies, waits for them, and re-layouts: 1.34 us -> 0.01 us
  Pallas kernels: 10.2 us -> 9.17 us
  starting transfers between devices: 11.5 us -> 12 us
    all_to_all x1, blocking collectives: 10.3 us -> 12.3 us  [local(): sums = jnp.sum(lax.all_to_all(sums, 'gz', 0, 0), axis=0)]
    unnamed x8 -> x4, local copies, waits for them, and re-layouts: 1.34 us -> 0.01 us
    pallas_call x3, Pallas kernels: 8.48 us -> 7.47 us  [call(): pl.pallas_call(kernel, in_specs=[vmem] * len(operands), out_specs=jax.tre...]
    ppermute x1, starting transfers between devices: 1.29 us -> 1.76 us  [local(): ynear = lax.ppermute(near, 'gy', near_pairs('gy'))]
  transfers between devices with their start and end apart: 4 -> 4, of which waited for: 1 -> 1; matrix products, arithmetic and copies ran while one was open for 0% -> 0% of each run, Pallas kernels for 19% -> 17%
where the time goes in v5:
time: 34.7 us; the launch traced here: 34.5 us
  blocking collectives  12.3 us (35%)
  starting transfers between devices  12 us (35%)
  Pallas kernels  9.17 us (26%)
  other arithmetic  0.55 us (2%)
  waiting for transfers between devices  0.36 us (1%)
    all_to_all x1, blocking collectives, local(): sums = jnp.sum(lax.all_to_all(sums, 'gz', 0, 0), axis=0)  12.3 us
    pallas_call x3, Pallas kernels, call(): pl.pallas_call(kernel, in_specs=[vmem] * len(operands), out_specs=jax.tre...  7.47 us
    ppermute x1, starting transfers between devices, local(): zfar = lax.ppermute(far, 'gz', far_pairs('gz', True))  4.69 us
    ppermute x1, starting transfers between devices, local(): yfar = lax.ppermute(far, 'gy', far_pairs('gy', False))  3.02 us
    ppermute x1, starting transfers between devices, local(): znear = lax.ppermute(near, 'gz', near_pairs('gz'))  2.55 us
    ppermute x1, starting transfers between devices, local(): ynear = lax.ppermute(near, 'gy', near_pairs('gy'))  1.76 us
    pallas_call x1, Pallas kernels, pack_span(): pl.pallas_call(pack_span_kernel, in_specs=[hbm] * 2, out_specs=[vmem] * 5...  1.61 us
  transfers between devices with their start and end apart: 4, of which 1 were waited for; matrix products, arithmetic and copies ran while one was open for 0% of the time, Pallas kernels for 17%

profile of v5, /device:TPU:1, one launch (start us, length us, event | category | flops | bytes accessed | tf_op | source)
XLA Modules:
  0.0 34.5 jit_solution(5339757911728754092)
XLA Ops:
  0.0 1.6 %shard_map.46 = (f32[96,128]{1,0:T(8,128)S(1)}, f32[96,128]{1,0:T(8,128)S(1)}, f32[3,96,768]{2,1,0:T(8,128)S(1)}, bf16[6,96,768]{2,1,0:T(8,128)(2,1)S(1)}, bf16[768,256]{1,0:T(8,128)(2,1)S(1)}) custom-call(f32[3,96,768]{2,1,0:T(8,128)} %v_ref.1, bf16[6,96,768]{2,1,0:T(8,128)(2,1)} %s_ref.1), custom_call_target="tpu_custom_call" | custom-call | tf_op jit(solution)/shard_map/pallas_call | solution.py:84
  1.6 2.5 %collective-permute-start = (f32[96,128]{1,0:T(8,128)S(1)}, f32[96,128]{1,0:T(8,128)S(1)}, u32[]{:S(2)}, u32[]{:S(2)}) collective-permute-start(f32[96,128]{1,0:T(8,128)S(1)} %get-tuple-element.19), channel_id=1, source_target_pairs={{0,1},{1,0},{2,3},{3,2},{4,5},{5,4},{6,7},{7,6},{8,9},{9,8},{10,11... | collective-permute-start | bytes 147464 | tf_op jit(solution)/shard_map/ppermute | solution.py:479
  4.2 4.7 %collective-permute-start.1 = (f32[96,128]{1,0:T(8,128)S(1)}, f32[96,128]{1,0:T(8,128)S(1)}, u32[]{:S(2)}, u32[]{:S(2)}) collective-permute-start(f32[96,128]{1,0:T(8,128)S(1)} %get-tuple-element.20), channel_id=1, source_target_pairs={{1,2},{2,1},{3,4},{4,3},{5,6},{6,5},{7,8},{8,7},{9,10},{10,9},{11,... | collective-permute-start | bytes 147464 | tf_op jit(solution)/shard_map/ppermute | solution.py:478
  8.9 0.0 copy-start
  8.9 0.0 copy-start.1
  8.9 1.9 %shard_map.48 = (bf16[21,96,768]{2,1,0:T(8,128)(2,1)S(1)}, bf16[15,96,768]{2,1,0:T(8,128)(2,1)S(1)}, f32[1,21,96,256]{3,2,1,0:T(8,128)S(1)}) custom-call(f32[3,96,768]{2,1,0:T(8,128)S(1)} %get-tuple-element.17.v_ref, bf16[6,96,768]{2,1,0:T(8,128)(2,1)S(1)} %get-tuple-element.18.s_ref, bf16[768,256]{1,0:T(8,128)(2,1)S(1)} %get-tuple-element.23.plane_ref), custom_call_target="tpu_custom_call" | custom-call | flops 4000000000 | bytes 1048576 | tf_op jit(solution)/shard_map/pallas_call | solution.py:383
  10.8 0.0 collective-permute-done.znear
  10.8 0.0 collective-permute-done.1.zfar
  10.8 0.0 copy-done
  10.8 0.1 shard_map.47
  10.9 1.8 %collective-permute-start.2 = (f32[8,7168]{1,0:T(8,128)S(1)}, f32[8,7168]{1,0:T(8,128)S(1)}, u32[]{:S(2)}, u32[]{:S(2)}) collective-permute-start(f32[8,7168]{1,0:T(8,128)S(1)} %get-tuple-element.21), channel_id=1, source_target_pairs={{0,16},{16,0},{32,48},{48,32},{64,80},{80,64},{96,112},{112,96},{1... | collective-permute-start | bytes 688136 | tf_op jit(solution)/shard_map/ppermute | solution.py:483
  12.7 3.0 %collective-permute-start.3 = (f32[8,7168]{1,0:T(8,128)S(1)}, f32[8,7168]{1,0:T(8,128)S(1)}, u32[]{:S(2)}, u32[]{:S(2)}) collective-permute-start(f32[8,7168]{1,0:T(8,128)S(1)} %get-tuple-element.22), channel_id=1, source_target_pairs={{16,32},{32,16},{48,64},{64,48},{80,96},{96,80},{17,33},{33,17},{4... | collective-permute-start | bytes 688136 | tf_op jit(solution)/shard_map/ppermute | solution.py:482
  15.7 0.0 copy-done.1
  15.7 3.9 %shard_map.49 = (f32[2,96,128]{2,1,0:T(8,128)S(1)}, f32[3,21,16,256]{3,2,1,0:T(8,128)S(1)}) custom-call(f32[1,96]{1,0:T(1,128)S(1)} %bitcast.4, s32[2,96]{1,0:T(2,128)S(1)} %copy-done.1, bf16[21,96,768]{2,1,0:T(8,128)(2,1)S(1)} %get-tuple-element.24.fh, bf16[15,96,768]{2,1,0:T(8,128)(2,1)S(1)} %get-tuple-element.25.fl, ...), custom_call_target="tpu_custom_call" | custom-call | flops 4000000000 | bytes 1048576 | tf_op jit(solution)/shard_map/pallas_call | solution.py:383
  19.6 0.0 collective-permute-done.2.ynear
  19.6 0.4 %collective-permute-done.3.yfar = f32[8,7168]{1,0:T(8,128)S(1)} collective-permute-done((f32[8,7168]{1,0:T(8,128)S(1)}, f32[8,7168]{1,0:T(8,128)S(1)}, u32[]{:S(2)}, u32[]{:S(2)}) %collective-permute-start.3) | collective-permute-done | bytes 229408 | tf_op jit(solution)/shard_map/ppermute | solution.py:482
  20.0 1.6 %shard_map.50 = f32[16,2,96]{2,1,0:T(2,128)S(1)} custom-call(f32[1,96]{1,0:T(1,128)S(1)} %bitcast.5, s32[2,96]{1,0:T(2,128)S(1)} %copy-done.1, f32[8,7168]{1,0:T(8,128)S(1)} %collective-permute-done.2.ynear, f32[8,7168]{1,0:T(8,128)S(1)} %collective-permute-done.3.yfar, f32[2,96,128]{2,1,0:T(8,128)S(1)} %get-tuple-element.27.acc_in, ...), custom_call_target="tpu_custom_call" | custom-call | flops 4000000000 | bytes 1048576 | tf_op jit(solution)/shard_map/pallas_call | solution.py:383
  21.6 12.3 %all_to_all.5 = f32[16,2,96]{2,1,0:T(2,128)S(1)} all-to-all(f32[16,2,96]{2,1,0:T(2,128)S(1)} %shard_map.50), channel_id=1, replica_groups=mesh['gy'=8,'gz'=16] {'gz'}, dimensions={0} | all-to-all | bytes 24576 | tf_op jit(solution)/shard_map/all_to_all | solution.py:486
  34.0 0.5 %fusion = f32[96]{0:T(128)} fusion(f32[2,96]{1,0:T(2,128)S(1)} %reduce_sum.9), kind=kLoop, calls=%fused_computation.1 | loop fusion | flops 384 | bytes 1152 | tf_op jit(solution)/shard_map/div | solution.py:488
  (1 shorter events, 0.0 us)
Async XLA Ops:
  1.6 9.2 %collective-permute-start = (f32[96,128]{1,0:T(8,128)S(1)}, f32[96,128]{1,0:T(8,128)S(1)}, u32[]{:S(2)}, u32[]{:S(2)}) collective-permute-start(f32[96,128]{1,0:T(8,128)S(1)} %get-tuple-element.19), channel_id=1, source_target_pairs={{0,1},{1,0},{2,3},{3,2},{4,5},{5,4},{6,7},{7,6},{8,9},{9,8},{10,11... | collective-permute-start | bytes 147464 | tf_op jit(solution)/shard_map/ppermute | solution.py:479
  4.2 6.6 %collective-permute-start.1 = (f32[96,128]{1,0:T(8,128)S(1)}, f32[96,128]{1,0:T(8,128)S(1)}, u32[]{:S(2)}, u32[]{:S(2)}) collective-permute-start(f32[96,128]{1,0:T(8,128)S(1)} %get-tuple-element.20), channel_id=1, source_target_pairs={{1,2},{2,1},{3,4},{4,3},{5,6},{6,5},{7,8},{8,7},{9,10},{10,9},{11,... | collective-permute-start | bytes 147464 | tf_op jit(solution)/shard_map/ppermute | solution.py:478
  8.9 1.9 %copy-start = (f32[96]{0:T(128)S(1)}, f32[96]{0:T(128)}, u32[]{:S(2)}) copy-start(f32[96]{0:T(128)} %param.6) | copy-start | bytes 1156
  8.9 6.8 %copy-start.1 = (s32[2,96]{1,0:T(2,128)S(1)}, s32[2,96]{1,0:T(2,128)}, u32[]{:S(2)}) copy-start(s32[2,96]{1,0:T(2,128)} %reach_ref.3) | copy-start | bytes 2308
  10.9 8.7 %collective-permute-start.2 = (f32[8,7168]{1,0:T(8,128)S(1)}, f32[8,7168]{1,0:T(8,128)S(1)}, u32[]{:S(2)}, u32[]{:S(2)}) collective-permute-start(f32[8,7168]{1,0:T(8,128)S(1)} %get-tuple-element.21), channel_id=1, source_target_pairs={{0,16},{16,0},{32,48},{48,32},{64,80},{80,64},{96,112},{112,96},{1... | collective-permute-start | bytes 688136 | tf_op jit(solution)/shard_map/ppermute | solution.py:483
  12.7 7.3 %collective-permute-start.3 = (f32[8,7168]{1,0:T(8,128)S(1)}, f32[8,7168]{1,0:T(8,128)S(1)}, u32[]{:S(2)}, u32[]{:S(2)}) collective-permute-start(f32[8,7168]{1,0:T(8,128)S(1)} %get-tuple-element.22), channel_id=1, source_target_pairs={{16,32},{32,16},{48,64},{64,48},{80,96},{96,80},{17,33},{33,17},{4... | collective-permute-start | bytes 688136 | tf_op jit(solution)/shard_map/ppermute | solution.py:482

commit v6 on v5

v6 whole, which is shorter than its diff:
```python
import jax
import jax.numpy as jnp
from jax import lax
from jax.experimental import pallas as pl
from jax.experimental.pallas import tpu as pltpu
from jax.sharding import PartitionSpec as P

NX = 8
HMAX = 8
LANES = 128
FIELDS = 21
WIDE = 15
FIRST_VMEM = 51 * 1024 * 1024
SMALL_VMEM = 24 * 1024 * 1024
LARGE_VMEM = 24 * 1024 * 1024
LEAD_INDEX = (0, 1, 2, 0, 0, 1)
TAIL_INDEX = (0, 1, 2, 1, 2, 2)
TENSOR_WEIGHTS = (1.0, 1.0, 1.0, 2.0, 2.0, 2.0)
F32 = jnp.float32
BF16 = jnp.bfloat16


def strain_rate(s):
    squares = 2.0 * (s[0] * s[0] + s[1] * s[1] + s[2] * s[2])
    squares = squares + 4.0 * (s[3] * s[3] + s[4] * s[4] + s[5] * s[5])
    return jnp.sqrt(squares)


def lane_iota(shape):
    return lax.broadcasted_iota(jnp.int32, shape, len(shape) - 1)


def rot(x, amount):
    amount = amount % LANES
    return pltpu.roll(x, amount, x.ndim - 1) if amount else x


def cell_weights(source, target):
    turn = (source - target) & (NX - 1)
    along = jnp.where(turn == 0, 0.5, jnp.where((turn == 1) | (turn == NX - 1), 0.25, 0.0))
    step = ((source + LANES) >> 3) - ((target + LANES) >> 3)
    across = jnp.where(step == 0, 0.5, jnp.where((step == 1) | (step == -1), 0.25, 0.0))
    return along * across


def pair_filter():
    shape = (3 * LANES, 2 * LANES)
    k = lax.broadcasted_iota(jnp.int32, shape, 0)
    return cell_weights(jnp.where(k < 5 * LANES // 2, k, k - 3 * LANES), lane_iota(shape)).astype(BF16)


def ends_filter():
    shape = (4 * LANES, 2 * LANES)
    k = lax.broadcasted_iota(jnp.int32, shape, 0)
    m = lane_iota(shape)
    place = k & (LANES - 1)
    outer = k >= 2 * LANES
    source = jnp.where(outer, jnp.where(place < LANES // 2, place + LANES, place - LANES), place)
    same = ((k >> 7) & 1) == (m >> 7)
    return jnp.where(same, cell_weights(source, m & (LANES - 1)), 0.0).astype(BF16)


def first_kernel(v_ref, s_ref, near_ref, far_ref, wall_near, wall_far, v_out, s_out, pair_ref, ends_ref, sems):
    rows, cells = v_ref.shape[1:]
    spans = ((0, LANES), (cells - LANES, LANES), (LANES, cells - 2 * LANES))
    copies = []
    for i, (start, size) in enumerate(spans):
        for j, (ref, out) in enumerate(((v_ref, v_out), (s_ref, s_out))):
            at = pl.ds(start, size)
            copies.append(pltpu.make_async_copy(ref.at[:, :, at], out.at[:, :, at], sems.at[i, j]))
    for copy in copies:
        copy.start()
    pair_ref[...] = pair_filter()
    ends_ref[...] = ends_filter()
    for copy in copies[:4]:
        copy.wait()
    lane = lane_iota((rows, LANES))
    left = jnp.zeros((rows, LANES), F32)
    right = jnp.zeros((rows, LANES), F32)
    for f in range(9):
        ref, at = (v_out, f) if f < 3 else (s_out, f - 3)
        here = (lane >= NX * f) & (lane < NX * (f + 1))
        left = jnp.where(here, rot(ref[at, :, :LANES].astype(F32), NX * f), left)
        right = jnp.where(here, rot(ref[at, :, cells - LANES :].astype(F32), NX * f + NX), right)
    odd = lax.axis_index("gz") % 2 == 1
    near_ref[...] = jnp.where(odd, left, right)
    far_ref[...] = jnp.where(odd, right, left)
    for copy in copies[4:]:
        copy.wait()
    gy_odd = lax.axis_index("gy") % 2 == 1
    for f in range(9):
        at = slice(f * cells, (f + 1) * cells)
        if f < 3:
            low, high = v_out[f, :HMAX, :], v_out[f, rows - HMAX :, :]
        else:
            low = s_out[f - 3, : 2 * HMAX, :].astype(F32)[:HMAX]
            high = s_out[f - 3, rows - 2 * HMAX :, :].astype(F32)[HMAX:]
        wall_near[:, at] = jnp.where(gy_odd, low, high)
        wall_far[:, at] = jnp.where(gy_odd, high, low)


def first_call(velocity, strain):
    rows, cells = velocity.shape[1:]
    hbm = pl.BlockSpec(memory_space=pltpu.HBM)
    vmem = pl.BlockSpec(memory_space=pltpu.VMEM)
    shape = jax.ShapeDtypeStruct
    return pl.pallas_call(
        first_kernel,
        in_specs=[hbm] * 2,
        out_specs=[vmem] * 8,
        out_shape=[shape((rows, LANES), F32)] * 2
        + [shape((HMAX, 9 * cells), F32)] * 2
        + [shape(x.shape, x.dtype) for x in (velocity, strain)]
        + [shape((3 * LANES, 2 * LANES), BF16), shape((4 * LANES, 2 * LANES), BF16)],
        scratch_shapes=[pltpu.SemaphoreType.DMA((3, 2))],
        compiler_params=pltpu.CompilerParams(vmem_limit_bytes=FIRST_VMEM),
    )(velocity, strain)


def corner_kernel(h_ref, znear, zfar, near_ref, far_ref):
    rows = znear.shape[0]
    gz_odd = lax.axis_index("gz") % 2 == 1
    gy_odd = lax.axis_index("gy") % 2 == 1
    lane = lane_iota((HMAX, LANES))
    row = lax.broadcasted_iota(jnp.int32, (HMAX, LANES), 0)
    stamp = (row == 0) & (lane >= 9 * NX) & (lane < 10 * NX)
    heights = jnp.broadcast_to(jnp.pad(h_ref[...], ((0, 0), (0, LANES - rows))), (HMAX, LANES))
    sides = []
    for r0 in (0, rows - HMAX):
        zn = znear[r0 : r0 + HMAX, :]
        zf = zfar[r0 : r0 + HMAX, :]
        zl = jnp.where(stamp, rot(heights, 9 * NX - r0), jnp.where(gz_odd, zn, zf))
        sides.append((zl, jnp.where(gz_odd, zf, zn)))
    (low_left, low_right), (high_left, high_right) = sides
    near_ref[:, :LANES] = jnp.where(gy_odd, low_left, high_left)
    near_ref[:, LANES:] = jnp.where(gy_odd, low_right, high_right)
    far_ref[:, :LANES] = jnp.where(gy_odd, high_left, low_left)
    far_ref[:, LANES:] = jnp.where(gy_odd, high_right, low_right)


def corner_call(heights, znear, zfar):
    vmem = pl.BlockSpec(memory_space=pltpu.VMEM)
    return pl.pallas_call(
        corner_kernel,
        in_specs=[vmem] * 3,
        out_specs=[vmem] * 2,
        out_shape=[jax.ShapeDtypeStruct((HMAX, 2 * LANES), F32)] * 2,
        compiler_params=pltpu.CompilerParams(vmem_limit_bytes=SMALL_VMEM),
    )(heights, znear, zfar)


def split2(x):
    hi = x.astype(BF16)
    return hi, (x - hi.astype(F32)).astype(BF16)


def store_fields(u, s, put_high, put_low):
    tensor = [x.astype(F32) for x in s]
    rate = strain_rate(tensor)
    wide = u + [u[a] * u[b] for a, b in zip(LEAD_INDEX, TAIL_INDEX)] + [rate * x for x in tensor]
    for f, value in enumerate(wide):
        hi, lo = split2(value)
        put_high(f, hi)
        put_low(f, lo)
    for f, value in enumerate(s):
        put_high(WIDE + f, value.astype(BF16))


def smooth(rows, operand, matrix_ref):
    wide, narrow = slice(0, WIDE), slice(WIDE, FIELDS)
    lhs = jnp.concatenate([operand(True, wide), operand(False, wide)], axis=-1).reshape(WIDE * rows, -1)
    matrix = matrix_ref[...]
    first = jnp.dot(lhs, jnp.concatenate([matrix, matrix], axis=0), preferred_element_type=F32)
    lhs = operand(True, narrow).reshape((FIELDS - WIDE) * rows, -1)
    second = jnp.dot(lhs, matrix, preferred_element_type=F32)
    return [first[f * rows : (f + 1) * rows] for f in range(WIDE)] + [
        second[f * rows : (f + 1) * rows] for f in range(FIELDS - WIDE)
    ]


def pick(after, before):
    return jnp.where(lane_iota(after.shape) < LANES // 2, after, before)


def smooth_pair(n, fh, fl, pair_ref):
    def operand(high, fields):
        ref = fh if high else fl
        tile = [ref[fields, :, (2 * n + i) * LANES : (2 * n + i + 1) * LANES] for i in range(4)]
        return jnp.concatenate([tile[1], tile[2], pick(tile[3], tile[0])], axis=-1)

    return smooth(fh.shape[1], operand, pair_ref)


def smooth_ends(fh, fl, eh, el, ends_ref):
    cells = fh.shape[2]

    def operand(high, fields):
        ref, outer = (fh, eh) if high else (fl, el)
        head, second = ref[fields, :, :LANES], ref[fields, :, LANES : 2 * LANES]
        ahead, last = ref[fields, :, cells - 2 * LANES : cells - LANES], ref[fields, :, cells - LANES :]
        edge = outer[fields]
        return jnp.concatenate([head, last, pick(second, edge), pick(edge, ahead)], axis=-1)

    return smooth(fh.shape[1], operand, ends_ref)


def contract(g, inv, num, den):
    u, p, m, s = g[0:3], g[3:9], g[9:15], g[15:21]
    rate = 4.0 * inv * strain_rate(s)
    scaled = [inv * x for x in u]
    for k in range(6):
        leonard = p[k] - scaled[LEAD_INDEX[k]] * u[TAIL_INDEX[k]]
        model = m[k] - rate * s[k]
        weighted = TENSOR_WEIGHTS[k] * model
        num = num + weighted * leonard
        den = den + weighted * model
    return num, den


def to_column(row_vector, size):
    shape = (size, LANES)
    eye = lax.broadcasted_iota(jnp.int32, shape, 0) == lane_iota(shape)
    return jnp.sum(jnp.where(eye, jnp.broadcast_to(row_vector, shape), 0.0), axis=1, keepdims=True)


def pad_lanes(x):
    return jnp.pad(x, ((0, 0), (0, LANES - x.shape[1])))


def wall_inside(reach_ref, place, rows):
    gy = lax.axis_index("gy")
    reach = pad_lanes(reach_ref[...].astype(F32))
    down = to_column(reach[0:1], rows).astype(jnp.int32)
    up = to_column(reach[1:2], rows).astype(jnp.int32)
    row = lax.broadcasted_iota(jnp.int32, place.shape, 0)
    lowest = jnp.maximum(row - down, -gy * rows)
    highest = jnp.minimum(row + up, (lax.axis_size("gy") - gy) * rows - 1)
    return (place >= lowest) & (place <= highest)


def wall_block(g, mask, height, inv, stack, acc_ref, part_ref):
    rows = g[0].shape[0]
    width = 2 * LANES
    for f in range(FIELDS):
        hi, lo = split2(g[f] * height)
        stack[0:rows, f * width : (f + 1) * width] = hi
        stack[rows:, f * width : (f + 1) * width] = lo
    merged = jnp.dot(mask, stack[...], preferred_element_type=F32)
    for f in range(FIELDS):
        part_ref[f, 0:HMAX, :] = merged[0:HMAX, f * width : (f + 1) * width]
        part_ref[f, HMAX:, :] = merged[rows - HMAX :, f * width : (f + 1) * width]
    for r in range(HMAX, rows - HMAX, HMAX):
        num = acc_ref[0, r : r + HMAX, :]
        den = acc_ref[1, r : r + HMAX, :]
        scale = jnp.broadcast_to(inv[r : r + HMAX], (HMAX, LANES))
        for c in range(2):
            parts = [
                merged[r : r + HMAX, f * width + c * LANES : f * width + (c + 1) * LANES] for f in range(FIELDS)
            ]
            num, den = contract(parts, scale, num, den)
        acc_ref[0, r : r + HMAX, :] = num
        acc_ref[1, r : r + HMAX, :] = den


def inner_kernel(v_ref, s_ref, pair_ref, fh, fl, inner):
    rows, cells = v_ref.shape[1:]
    for t in range(cells // LANES):
        at = slice(t * LANES, (t + 1) * LANES)
        for r in range(0, rows, 16):
            rr = slice(r, r + 16)

            def put_high(f, x):
                fh[f, rr, at] = x

            def put_low(f, x):
                fl[f, rr, at] = x

            store_fields(
                [v_ref[f, rr, at] for f in range(3)], [s_ref[f, rr, at] for f in range(6)], put_high, put_low
            )
    for n in range(inner.shape[0]):
        g = smooth_pair(n, fh, fl, pair_ref)
        for f in range(FIELDS):
            inner[n, f] = g[f]


def outer_kernel(
    h_ref, reach_ref, fh, fl, inner, znear, zfar, ynear, yfar, pair_ref, ends_ref,
    acc_ref, part_ref, hh, hl, halo_inner, eh, el, stack,
):
    rows, cells = fh.shape[1:]
    blocks = inner.shape[0]
    gz_odd = lax.axis_index("gz") % 2 == 1
    gy_odd = lax.axis_index("gy") % 2 == 1
    column = lane_iota((rows, 2 * LANES))
    place = jnp.where(column < rows, column, column - rows)
    inside = wall_inside(reach_ref, place, rows)
    mask = jnp.where(inside, 1.0, 0.0)[:, : 2 * rows].astype(BF16)
    heights = pad_lanes(h_ref[...])
    height = to_column(heights, rows)
    first = (column < rows) & inside
    total = jnp.sum(jnp.where(first, jnp.pad(heights, ((0, 0), (0, LANES))), 0.0), axis=1, keepdims=True)
    inv = 1.0 / total
    acc_ref[...] = jnp.zeros_like(acc_ref)
    edge_fields(jnp.where(gz_odd, znear[...], zfar[...]), jnp.where(gz_odd, zfar[...], znear[...]), eh, el)
    for n in range(blocks + 1):
        if n < blocks:
            g = [inner[n, f] for f in range(FIELDS)]
        else:
            g = smooth_ends(fh, fl, eh, el, ends_ref)
        wall_block(g, mask, height, inv, stack.at[n], acc_ref, part_ref.at[n])
    for t in range(cells // LANES):
        at = slice(t * LANES, (t + 1) * LANES)

        def put_high(f, x):
            hh[f, :, at] = x

        def put_low(f, x):
            hl[f, :, at] = x

        raw = []
        for f in range(9):
            span = slice(f * cells + t * LANES, f * cells + (t + 1) * LANES)
            near, far = ynear[:, span], yfar[:, span]
            raw.append(jnp.concatenate([jnp.where(gy_odd, near, far), jnp.where(gy_odd, far, near)], axis=0))
        store_fields(raw[:3], raw[3:], put_high, put_low)
    for n in range(blocks):
        g = smooth_pair(n, hh, hl, pair_ref)
        for f in range(FIELDS):
            halo_inner[n, f] = g[f]


def edge_fields(zl, zr, eh, el):
    rows = zl.shape[0]
    lane = lane_iota((16, LANES))
    for r in range(0, rows, 16):
        rr = slice(r, r + 16)
        raw = [
            jnp.where(
                lane < NX, rot(zr[rr], -NX * f), jnp.where(lane >= LANES - NX, rot(zl[rr], -NX * f - NX), 0.0)
            )
            for f in range(9)
        ]

        def put_high(f, x):
            eh[f, rr, :] = x

        def put_low(f, x):
            el[f, rr, :] = x

        store_fields(raw[:3], raw[3:], put_high, put_low)


def last_kernel(h_ref, reach_ref, near_ref, far_ref, acc_in, part, hh, hl, halo_inner, ends_ref, out_ref, eh, el, stack, acc):
    rows = h_ref.shape[1]
    width = 2 * LANES
    gy_odd = lax.axis_index("gy") % 2 == 1
    both_rows = 2 * HMAX

    def halo(at):
        near, far = near_ref[:, at], far_ref[:, at]
        return jnp.concatenate([jnp.where(gy_odd, near, far), jnp.where(gy_odd, far, near)], axis=0)

    zl = halo(slice(0, LANES))
    zr = halo(slice(LANES, 2 * LANES))
    below = rot(zl[:HMAX], -9 * NX)[0:1]
    above = rot(zl[HMAX:], -9 * NX)[0:1]
    height = jnp.concatenate([to_column(below, HMAX), to_column(above, HMAX)], axis=0)
    column = lane_iota((rows, LANES))
    place = jnp.where(column < rows, column, jnp.where(column < rows + HMAX, column - rows - HMAX, column - HMAX))
    hrow = lane_iota((1, LANES))
    heights = jnp.where(
        hrow < rows, pad_lanes(h_ref[...]), jnp.where(hrow < rows + HMAX, rot(below, rows), rot(above, rows + HMAX))
    )
    inside = wall_inside(reach_ref, place, rows) & (column < rows + both_rows)
    inv = 1.0 / jnp.sum(jnp.where(inside, jnp.broadcast_to(heights, (rows, LANES)), 0.0), axis=1, keepdims=True)
    scale = [jnp.broadcast_to(inv[r : r + HMAX], (HMAX, LANES)) for r in (0, rows - HMAX)]
    mask = jnp.where(inside, 1.0, 0.0)
    mask = rot(jnp.concatenate([mask[:HMAX], mask[rows - HMAX :]], axis=0), -rows)
    lane = lane_iota((both_rows, LANES))
    mask = jnp.where(lane < both_rows, mask, rot(mask, both_rows))[:, : 2 * both_rows].astype(BF16)

    edge_fields(zl, zr, eh, el)
    zero = jnp.zeros((HMAX, LANES), F32)
    sums = [[zero, zero], [zero, zero]]
    blocks = halo_inner.shape[0]
    for n in range(blocks + 1):
        if n < blocks:
            g = [halo_inner[n, f] for f in range(FIELDS)]
        else:
            g = smooth_ends(hh, hl, eh, el, ends_ref)
        for f in range(FIELDS):
            hi, lo = split2(g[f] * height)
            stack[n, 0:both_rows, f * width : (f + 1) * width] = hi
            stack[n, both_rows:, f * width : (f + 1) * width] = lo
        merged = jnp.dot(mask, stack[n], preferred_element_type=F32)
        for i in range(2):
            rr = slice(i * HMAX, (i + 1) * HMAX)
            for c in range(2):
                at = slice(c * LANES, (c + 1) * LANES)
                values = [
                    part[n, f, rr, at] + merged[rr, f * width + c * LANES : f * width + (c + 1) * LANES]
                    for f in range(FIELDS)
                ]
                sums[i] = list(contract(values, scale[i], *sums[i]))
    ones = jnp.ones((HMAX, LANES), F32)
    for k in range(2):
        acc[0:HMAX, :] = sums[0][k]
        acc[HMAX : rows - HMAX, :] = acc_in[k, HMAX : rows - HMAX, :]
        acc[rows - HMAX :, :] = sums[1][k]
        total = lax.dot_general(
            ones, acc[...] * (inv * inv), (((1,), (1,)), ((), ())), precision=lax.Precision.HIGHEST, preferred_element_type=F32
        )
        out_ref[:, k : k + 1, :] = jnp.broadcast_to(total[0:1][None], (out_ref.shape[0], 1, rows))


def call(kernel, out_shape, scratch, limit, *operands):
    vmem = pl.BlockSpec(memory_space=pltpu.VMEM)
    return pl.pallas_call(
        kernel,
        in_specs=[vmem] * len(operands),
        out_specs=jax.tree.map(lambda _: vmem, out_shape),
        out_shape=out_shape,
        scratch_shapes=scratch,
        compiler_params=pltpu.CompilerParams(vmem_limit_bytes=limit),
        cost_estimate=pl.CostEstimate(flops=4 * 10**9, bytes_accessed=2**20, transcendentals=0),
    )(*operands)


def local(velocity, strain, cell_height, stencil_reach):
    rows, cells = velocity.shape[1:]
    width = 2 * LANES
    blocks = cells // width - 1
    ends = 2 * HMAX
    shape = jax.ShapeDtypeStruct
    heights = cell_height.reshape(1, rows)
    near, far, wall_near, wall_far, velocity, strain, pair, both_ends = first_call(velocity, strain)
    zfar = lax.ppermute(far, "gz", far_pairs("gz", True))
    znear = lax.ppermute(near, "gz", near_pairs("gz"))
    yfar = lax.ppermute(wall_far, "gy", far_pairs("gy", False))
    ynear = lax.ppermute(wall_near, "gy", near_pairs("gy"))
    fh, fl, inner = call(
        inner_kernel,
        [
            shape((FIELDS, rows, cells), BF16),
            shape((WIDE, rows, cells), BF16),
            shape((blocks, FIELDS, rows, width), F32),
        ],
        [],
        LARGE_VMEM,
        velocity,
        strain,
        pair,
    )
    near, far = corner_call(heights, znear, zfar)
    corner_far = lax.ppermute(far, "gy", far_pairs("gy", False))
    corner_near = lax.ppermute(near, "gy", near_pairs("gy"))
    acc, part, hh, hl, halo_inner = call(
        outer_kernel,
        [
            shape((2, rows, LANES), F32),
            shape((blocks + 1, FIELDS, ends, width), F32),
            shape((FIELDS, ends, cells), BF16),
            shape((WIDE, ends, cells), BF16),
            shape((blocks, FIELDS, ends, width), F32),
        ],
        [
            pltpu.VMEM((FIELDS, rows, LANES), BF16),
            pltpu.VMEM((WIDE, rows, LANES), BF16),
            pltpu.VMEM((blocks + 1, 2 * rows, FIELDS * width), BF16),
        ],
        LARGE_VMEM,
        heights,
        stencil_reach,
        fh,
        fl,
        inner,
        znear,
        zfar,
        ynear,
        yfar,
        pair,
        both_ends,
    )
    sums = call(
        last_kernel,
        shape((lax.axis_size("gz"), 2, rows), F32),
        [
            pltpu.VMEM((FIELDS, ends, LANES), BF16),
            pltpu.VMEM((WIDE, ends, LANES), BF16),
            pltpu.VMEM((blocks + 1, 2 * ends, FIELDS * width), BF16),
            pltpu.VMEM((rows, LANES), F32),
        ],
        LARGE_VMEM,
        heights,
        stencil_reach,
        corner_near,
        corner_far,
        acc,
        part,
        hh,
        hl,
        halo_inner,
        both_ends,
    )
    sums = jnp.sum(lax.all_to_all(sums, "gz", 0, 0), axis=0)
    total = lax.axis_size("gz") * cells
    return sums[0] / total / (sums[1] / total + 1e-06)


def near_pairs(axis):
    return [(i, i ^ 1) for i in range(lax.axis_size(axis))]


def far_pairs(axis, closed):
    n = lax.axis_size(axis)
    pairs = []
    for i in range(1, n if closed else n - 1, 2):
        pairs += [(i, (i + 1) % n), ((i + 1) % n, i)]
    return pairs


def solution(mesh):
    in_specs = (P(None, "gy", "gz"), P(None, "gy", "gz"), P("gy"), P(None, "gy"))
    return jax.shard_map(local, mesh=mesh, in_specs=in_specs, out_specs=P("gy"), check_vma=False)
```

time: 34.7 us -> 34.4 us (level)
  blocking collectives: 12.3 us -> 9.06 us
  starting transfers between devices: 12 us -> 15 us
    all_to_all x1, blocking collectives: 12.3 us -> 9.06 us  [local(): sums = jnp.sum(lax.all_to_all(sums, 'gz', 0, 0), axis=0)]
    ppermute x2 -> x4, starting transfers between devices: 4.78 us -> 7.76 us  [the longest x1 3.49 us: local(): corner_far = lax.ppermute(far, 'gy', far_pairs('gy', False))]
  transfers between devices with their start and end apart: 4 -> 6, of which waited for: 1 -> 0; matrix products, arithmetic and copies ran while one was open for 0% -> 0% of each run, Pallas kernels for 17% -> 19%
where the time goes in v6:
time: 34.4 us; the launch traced here: 34.3 us
  starting transfers between devices  15 us (44%)
  Pallas kernels  9.48 us (28%)
  blocking collectives  9.06 us (26%)
  other arithmetic  0.55 us (2%)
    all_to_all x1, blocking collectives, local(): sums = jnp.sum(lax.all_to_all(sums, 'gz', 0, 0), axis=0)  9.06 us
    pallas_call x3, Pallas kernels, call(): pl.pallas_call(kernel, in_specs=[vmem] * len(operands), out_specs=jax.tre...  7.77 us
    ppermute x1, starting transfers between devices, local(): zfar = lax.ppermute(far, 'gz', far_pairs('gz', True))  4.69 us
    ppermute x1, starting transfers between devices, local(): corner_far = lax.ppermute(far, 'gy', far_pairs('gy', False))  3.49 us
    ppermute x1, starting transfers between devices, local(): yfar = lax.ppermute(wall_far, 'gy', far_pairs('gy', False))  3 us
    ppermute x1, starting transfers between devices, local(): znear = lax.ppermute(near, 'gz', near_pairs('gz'))  2.55 us
    pallas_call x1, Pallas kernels, first_call(): pl.pallas_call(first_kernel, in_specs=[hbm] * 2, out_specs=[vmem] * 8, ou...  1.64 us
    ppermute x1, starting transfers between devices, local(): ynear = lax.ppermute(wall_near, 'gy', near_pairs('gy'))  1.24 us
  transfers between devices with their start and end apart: 6, of which 0 were waited for; matrix products, arithmetic and copies ran while one was open for 0% of the time, Pallas kernels for 19%

profile of v6, /device:TPU:1, one launch (start us, length us, event | category | flops | bytes accessed | tf_op | source)
XLA Modules:
  0.0 34.3 jit_solution(18374269074837148860)
XLA Ops:
  0.0 1.6 %shard_map.46 = (f32[96,128]{1,0:T(8,128)S(1)}, f32[96,128]{1,0:T(8,128)S(1)}, f32[8,6912]{1,0:T(8,128)S(1)}, f32[8,6912]{1,0:T(8,128)S(1)}, f32[3,96,768]{2,1,0...) custom-call(f32[3,96,768]{2,1,0:T(8,128)} %v_ref.1, ...), custom_call_target="tpu_custom_call" | custom-call | tf_op jit(solution)/shard_map/pallas_call | solution.py:107
  1.7 2.5 %collective-permute-start = (f32[96,128]{1,0:T(8,128)S(1)}, f32[96,128]{1,0:T(8,128)S(1)}, u32[]{:S(2)}, u32[]{:S(2)}) collective-permute-start(f32[96,128]{1,0:T(8,128)S(1)} %get-tuple-element.23), channel_id=1, source_target_pairs={{0,1},{1,0},{2,3},{3,2},{4,5},{5,4},{6,7},{7,6},{8,9},{9,8},{10,11... | collective-permute-start | bytes 147464 | tf_op jit(solution)/shard_map/ppermute | solution.py:439
  4.2 4.7 %collective-permute-start.1 = (f32[96,128]{1,0:T(8,128)S(1)}, f32[96,128]{1,0:T(8,128)S(1)}, u32[]{:S(2)}, u32[]{:S(2)}) collective-permute-start(f32[96,128]{1,0:T(8,128)S(1)} %get-tuple-element.24), channel_id=1, source_target_pairs={{1,2},{2,1},{3,4},{4,3},{5,6},{6,5},{7,8},{8,7},{9,10},{10,9},{11,... | collective-permute-start | bytes 147464 | tf_op jit(solution)/shard_map/ppermute | solution.py:438
  8.9 1.2 %collective-permute-start.4 = (f32[8,6912]{1,0:T(8,128)S(1)}, f32[8,6912]{1,0:T(8,128)S(1)}, u32[]{:S(2)}, u32[]{:S(2)}) collective-permute-start(f32[8,6912]{1,0:T(8,128)S(1)} %get-tuple-element.33), channel_id=1, source_target_pairs={{0,16},{16,0},{32,48},{48,32},{64,80},{80,64},{96,112},{112,96},{1... | collective-permute-start | bytes 663560 | tf_op jit(solution)/shard_map/ppermute | solution.py:441
  10.1 3.0 %collective-permute-start.5 = (f32[8,6912]{1,0:T(8,128)S(1)}, f32[8,6912]{1,0:T(8,128)S(1)}, u32[]{:S(2)}, u32[]{:S(2)}) collective-permute-start(f32[8,6912]{1,0:T(8,128)S(1)} %get-tuple-element.34), channel_id=1, source_target_pairs={{16,32},{32,16},{48,64},{64,48},{80,96},{96,80},{17,33},{33,17},{4... | collective-permute-start | bytes 663560 | tf_op jit(solution)/shard_map/ppermute | solution.py:440
  13.1 0.0 copy-start
  13.1 0.0 copy-start.1
  13.2 2.1 %shard_map.48 = (bf16[21,96,768]{2,1,0:T(8,128)(2,1)S(1)}, bf16[15,96,768]{2,1,0:T(8,128)(2,1)S(1)}, f32[2,21,96,256]{3,2,1,0:T(8,128)S(1)}) custom-call(f32[3,96,768]{2,1,0:T(8,128)S(1)} %get-tuple-element.27.v_ref, bf16[6,96,768]{2,1,0:T(8,128)(2,1)S(1)} %get-tuple-element.28.s_ref, bf16[384,256]{1,0:T(8,128)(2,1)S(1)} %get-tuple-element.29.pair_ref), custom_call_target="tpu_custom_call" | custom-call | flops 4000000000 | bytes 1048576 | tf_op jit(solution)/shard_map/pallas_call | solution.py:419
  15.3 0.0 collective-permute-done.znear
  15.3 0.0 collective-permute-done.1.zfar
  15.3 0.0 copy-done
  15.3 0.1 shard_map.47
  15.4 0.0 collective-permute-start.2
  15.5 3.5 %collective-permute-start.3 = (f32[8,256]{1,0:T(8,128)S(1)}, f32[8,256]{1,0:T(8,128)S(1)}, u32[]{:S(2)}, u32[]{:S(2)}) collective-permute-start(f32[8,256]{1,0:T(8,128)S(1)} %get-tuple-element.26), channel_id=1, source_target_pairs={{16,32},{32,16},{48,64},{64,48},{80,96},{96,80},{17,33},{33,17},{4... | collective-permute-start | bytes 24584 | tf_op jit(solution)/shard_map/ppermute | solution.py:456
  19.0 0.0 collective-permute-done.4.ynear
  19.0 0.0 collective-permute-done.5.yfar
  19.0 0.0 copy-done.1
  19.0 4.3 %shard_map.49 = (f32[2,96,128]{2,1,0:T(8,128)S(1)}, f32[3,21,16,256]{3,2,1,0:T(8,128)S(1)}, bf16[21,16,768]{2,1,0:T(8,128)(2,1)S(1)}, bf16[15,16,768]{2,1,0:T(8,128)(2,1)S(1)}, f32[2,21,16,256]{3,2,1,0:T(8,128)S(1)}) custom-call(f32[1,96]{1,0:T(1,128)S(1)} %bitcast.4, s32[2,96]{1,0:T(2,128)S(1)} %copy-done.1, bf16[21,96,768]{2,1,0:T(8,128)(2,1)S(1)} %get-tuple-element.30.fh, ...), custom_call_target="tpu_custom_call" | custom-call | flops 4000000000 | bytes 1048576 | tf_op jit(solution)/shard_map/pallas_call | solution.py:419
  23.3 0.0 collective-permute-done.2.near_ref
  23.3 0.0 collective-permute-done.3.far_ref
  23.3 1.4 %shard_map.50 = f32[16,2,96]{2,1,0:T(2,128)S(1)} custom-call(f32[1,96]{1,0:T(1,128)S(1)} %bitcast.5, s32[2,96]{1,0:T(2,128)S(1)} %copy-done.1, f32[8,256]{1,0:T(8,128)S(1)} %collective-permute-done.2.near_ref, f32[8,256]{1,0:T(8,128)S(1)} %collective-permute-done.3.far_ref, f32[2,96,128]{2,1,0:T(8,128)S(1)} %get-tuple-element.36.acc_in, ...), custom_call_target="tpu_custom_call" | custom-call | flops 4000000000 | bytes 1048576 | tf_op jit(solution)/shard_map/pallas_call | solution.py:419
  24.6 9.1 %all_to_all.5 = f32[16,2,96]{2,1,0:T(2,128)S(1)} all-to-all(f32[16,2,96]{2,1,0:T(2,128)S(1)} %shard_map.50), channel_id=1, replica_groups=mesh['gy'=8,'gz'=16] {'gz'}, dimensions={0} | all-to-all | bytes 24576 | tf_op jit(solution)/shard_map/all_to_all | solution.py:506
  33.7 0.5 %fusion = f32[96]{0:T(128)} fusion(f32[2,96]{1,0:T(2,128)S(1)} %reduce_sum.9), kind=kLoop, calls=%fused_computation.1 | loop fusion | flops 384 | bytes 1152 | tf_op jit(solution)/shard_map/div | solution.py:508
  (1 shorter events, 0.0 us)
Async XLA Ops:
  1.7 13.7 %collective-permute-start = (f32[96,128]{1,0:T(8,128)S(1)}, f32[96,128]{1,0:T(8,128)S(1)}, u32[]{:S(2)}, u32[]{:S(2)}) collective-permute-start(f32[96,128]{1,0:T(8,128)S(1)} %get-tuple-element.23), channel_id=1, source_target_pairs={{0,1},{1,0},{2,3},{3,2},{4,5},{5,4},{6,7},{7,6},{8,9},{9,8},{10,11... | collective-permute-start | bytes 147464 | tf_op jit(solution)/shard_map/ppermute | solution.py:439
  4.2 11.1 %collective-permute-start.1 = (f32[96,128]{1,0:T(8,128)S(1)}, f32[96,128]{1,0:T(8,128)S(1)}, u32[]{:S(2)}, u32[]{:S(2)}) collective-permute-start(f32[96,128]{1,0:T(8,128)S(1)} %get-tuple-element.24), channel_id=1, source_target_pairs={{1,2},{2,1},{3,4},{4,3},{5,6},{6,5},{7,8},{8,7},{9,10},{10,9},{11,... | collective-permute-start | bytes 147464 | tf_op jit(solution)/shard_map/ppermute | solution.py:438
  8.9 10.1 %collective-permute-start.4 = (f32[8,6912]{1,0:T(8,128)S(1)}, f32[8,6912]{1,0:T(8,128)S(1)}, u32[]{:S(2)}, u32[]{:S(2)}) collective-permute-start(f32[8,6912]{1,0:T(8,128)S(1)} %get-tuple-element.33), channel_id=1, source_target_pairs={{0,16},{16,0},{32,48},{48,32},{64,80},{80,64},{96,112},{112,96},{1... | collective-permute-start | bytes 663560 | tf_op jit(solution)/shard_map/ppermute | solution.py:441
  10.1 8.8 %collective-permute-start.5 = (f32[8,6912]{1,0:T(8,128)S(1)}, f32[8,6912]{1,0:T(8,128)S(1)}, u32[]{:S(2)}, u32[]{:S(2)}) collective-permute-start(f32[8,6912]{1,0:T(8,128)S(1)} %get-tuple-element.34), channel_id=1, source_target_pairs={{16,32},{32,16},{48,64},{64,48},{80,96},{96,80},{17,33},{33,17},{4... | collective-permute-start | bytes 663560 | tf_op jit(solution)/shard_map/ppermute | solution.py:440
  13.1 2.2 %copy-start = (f32[96]{0:T(128)S(1)}, f32[96]{0:T(128)}, u32[]{:S(2)}) copy-start(f32[96]{0:T(128)} %param.6) | copy-start | bytes 1156
  13.1 5.8 %copy-start.1 = (s32[2,96]{1,0:T(2,128)S(1)}, s32[2,96]{1,0:T(2,128)}, u32[]{:S(2)}) copy-start(s32[2,96]{1,0:T(2,128)} %reach_ref.3) | copy-start | bytes 2308
  15.4 7.8 %collective-permute-start.2 = (f32[8,256]{1,0:T(8,128)S(1)}, f32[8,256]{1,0:T(8,128)S(1)}, u32[]{:S(2)}, u32[]{:S(2)}) collective-permute-start(f32[8,256]{1,0:T(8,128)S(1)} %get-tuple-element.25), channel_id=1, source_target_pairs={{0,16},{16,0},{32,48},{48,32},{64,80},{80,64},{96,112},{112,96},{1... | collective-permute-start | bytes 24584 | tf_op jit(solution)/shard_map/ppermute | solution.py:457
  15.5 7.8 %collective-permute-start.3 = (f32[8,256]{1,0:T(8,128)S(1)}, f32[8,256]{1,0:T(8,128)S(1)}, u32[]{:S(2)}, u32[]{:S(2)}) collective-permute-start(f32[8,256]{1,0:T(8,128)S(1)} %get-tuple-element.26), channel_id=1, source_target_pairs={{16,32},{32,16},{48,64},{64,48},{80,96},{96,80},{17,33},{33,17},{4... | collective-permute-start | bytes 24584 | tf_op jit(solution)/shard_map/ppermute | solution.py:456

commit v7 on v6

--- a/solution.py
+++ b/solution.py
@@ -50,14 +50,21 @@
 
 
 def ends_filter():
-    shape = (4 * LANES, 2 * LANES)
+    shape = (3 * LANES, 2 * LANES)
     k = lax.broadcasted_iota(jnp.int32, shape, 0)
     m = lane_iota(shape)
     place = k & (LANES - 1)
+    middle = LANES // 2
     outer = k >= 2 * LANES
-    source = jnp.where(outer, jnp.where(place < LANES // 2, place + LANES, place - LANES), place)
-    same = ((k >> 7) & 1) == (m >> 7)
-    return jnp.where(same, cell_weights(source, m & (LANES - 1)), 0.0).astype(BF16)
+    last = place >= LANES - NX
+    after = (place >= middle - NX) & (place < middle)
+    before = (place >= middle) & (place < middle + NX)
+    used = (place < NX) | last | after | before
+    shift = jnp.where(last, -LANES, jnp.where(after, LANES - middle + NX, jnp.where(before, -middle - NX, LANES)))
+    source = jnp.where(outer, place + shift, place)
+    tile = jnp.where(outer, jnp.where(last | after, 1, 0), k >> 7)
+    fits = (tile == (m >> 7)) & (used | (k < 2 * LANES))
+    return jnp.where(fits, cell_weights(source, m & (LANES - 1)), 0.0).astype(BF16)
 
 
 def first_kernel(v_ref, s_ref, near_ref, far_ref, wall_near, wall_far, v_out, s_out, pair_ref, ends_ref, sems):
@@ -111,7 +118,7 @@
         out_shape=[shape((rows, LANES), F32)] * 2
         + [shape((HMAX, 9 * cells), F32)] * 2
         + [shape(x.shape, x.dtype) for x in (velocity, strain)]
-        + [shape((3 * LANES, 2 * LANES), BF16), shape((4 * LANES, 2 * LANES), BF16)],
+        + [shape((3 * LANES, 2 * LANES), BF16)] * 2,
         scratch_shapes=[pltpu.SemaphoreType.DMA((3, 2))],
         compiler_params=pltpu.CompilerParams(vmem_limit_bytes=FIRST_VMEM),
     )(velocity, strain)
@@ -196,10 +203,11 @@
 
     def operand(high, fields):
         ref, outer = (fh, eh) if high else (fl, el)
-        head, second = ref[fields, :, :LANES], ref[fields, :, LANES : 2 * LANES]
-        ahead, last = ref[fields, :, cells - 2 * LANES : cells - LANES], ref[fields, :, cells - LANES :]
-        edge = outer[fields]
-        return jnp.concatenate([head, last, pick(second, edge), pick(edge, ahead)], axis=-1)
+        second = ref[fields, :, LANES : 2 * LANES]
+        ahead = ref[fields, :, cells - 2 * LANES : cells - LANES]
+        lane = lane_iota(second.shape)
+        edge = jnp.where(lane < NX, second, jnp.where(lane >= LANES - NX, ahead, outer[fields]))
+        return jnp.concatenate([ref[fields, :, :LANES], ref[fields, :, cells - LANES :], edge], axis=-1)
 
     return smooth(fh.shape[1], operand, ends_ref)
 
@@ -223,19 +231,23 @@
     return jnp.sum(jnp.where(eye, jnp.broadcast_to(row_vector, shape), 0.0), axis=1, keepdims=True)
 
 
+def to_row(column_vector, row):
+    return jnp.sum(jnp.where(row == lane_iota(row.shape), column_vector, 0.0), axis=0, keepdims=True)
+
+
 def pad_lanes(x):
     return jnp.pad(x, ((0, 0), (0, LANES - x.shape[1])))
 
 
-def wall_inside(reach_ref, place, rows):
+def stencil_holds(place, row, down, up, rows):
     gy = lax.axis_index("gy")
-    reach = pad_lanes(reach_ref[...].astype(F32))
-    down = to_column(reach[0:1], rows).astype(jnp.int32)
-    up = to_column(reach[1:2], rows).astype(jnp.int32)
-    row = lax.broadcasted_iota(jnp.int32, place.shape, 0)
     lowest = jnp.maximum(row - down, -gy * rows)
     highest = jnp.minimum(row + up, (lax.axis_size("gy") - gy) * rows - 1)
     return (place >= lowest) & (place <= highest)
+
+
+def end_rows(x):
+    return jnp.concatenate([x[:HMAX], x[x.shape[0] - HMAX :]], axis=0)
 
 
 def wall_block(g, mask, height, inv, stack, acc_ref, part_ref):
@@ -286,21 +298,34 @@
 
 def outer_kernel(
     h_ref, reach_ref, fh, fl, inner, znear, zfar, ynear, yfar, pair_ref, ends_ref,
-    acc_ref, part_ref, hh, hl, halo_inner, eh, el, stack,
+    sums_ref, part_ref, mask_ref, total_ref, hh, hl, halo_inner, eh, el, stack, acc_ref,
 ):
     rows, cells = fh.shape[1:]
     blocks = inner.shape[0]
+    ends = 2 * HMAX
     gz_odd = lax.axis_index("gz") % 2 == 1
     gy_odd = lax.axis_index("gy") % 2 == 1
+    reach = pad_lanes(reach_ref[...].astype(F32))
+    down = to_column(reach[0:1], rows).astype(jnp.int32)
+    up = to_column(reach[1:2], rows).astype(jnp.int32)
     column = lane_iota((rows, 2 * LANES))
+    row = lax.broadcasted_iota(jnp.int32, (rows, 2 * LANES), 0)
     place = jnp.where(column < rows, column, column - rows)
-    inside = wall_inside(reach_ref, place, rows)
+    inside = stencil_holds(place, row, down, up, rows)
     mask = jnp.where(inside, 1.0, 0.0)[:, : 2 * rows].astype(BF16)
     heights = pad_lanes(h_ref[...])
     height = to_column(heights, rows)
-    first = (column < rows) & inside
-    total = jnp.sum(jnp.where(first, jnp.pad(heights, ((0, 0), (0, LANES))), 0.0), axis=1, keepdims=True)
+    own = inside[:, :LANES] & (column[:, :LANES] < rows)
+    total = jnp.sum(jnp.where(own, jnp.broadcast_to(heights, (rows, LANES)), 0.0), axis=1, keepdims=True)
     inv = 1.0 / total
+    total_ref[...] = jnp.broadcast_to(end_rows(total), (ends, LANES))
+    column = lane_iota((ends, LANES))
+    row = lax.broadcasted_iota(jnp.int32, (ends, LANES), 0)
+    turn = column & (ends - 1)
+    place = jnp.where(turn < HMAX, turn - HMAX, turn - HMAX + rows)
+    row = jnp.where(row < HMAX, row, row + rows - ends)
+    inside = stencil_holds(place, row, end_rows(down), end_rows(up), rows) & (column < 2 * ends)
+    mask_ref[...] = jnp.where(inside, 1.0, 0.0)
     acc_ref[...] = jnp.zeros_like(acc_ref)
     edge_fields(jnp.where(gz_odd, znear[...], zfar[...]), jnp.where(gz_odd, zfar[...], znear[...]), eh, el)
     for n in range(blocks + 1):
@@ -328,16 +353,24 @@
         g = smooth_pair(n, hh, hl, pair_ref)
         for f in range(FIELDS):
             halo_inner[n, f] = g[f]
+    for k in range(2):
+        plane_sums = jnp.sum(acc_ref[k] * (inv * inv), axis=1, keepdims=True)
+        sums_ref[k : k + 1, :] = to_row(plane_sums, lax.broadcasted_iota(jnp.int32, (rows, LANES), 0))
 
 
 def edge_fields(zl, zr, eh, el):
     rows = zl.shape[0]
     lane = lane_iota((16, LANES))
+    middle = LANES // 2
+    follows = (lane >= middle - NX) & (lane < middle)
+    precedes = (lane >= middle) & (lane < middle + NX)
     for r in range(0, rows, 16):
         rr = slice(r, r + 16)
         raw = [
             jnp.where(
-                lane < NX, rot(zr[rr], -NX * f), jnp.where(lane >= LANES - NX, rot(zl[rr], -NX * f - NX), 0.0)
+                follows,
+                rot(zr[rr], middle - NX - NX * f),
+                jnp.where(precedes, rot(zl[rr], middle - NX * f), 0.0),
             )
             for f in range(9)
         ]
@@ -351,8 +384,8 @@
         store_fields(raw[:3], raw[3:], put_high, put_low)
 
 
-def last_kernel(h_ref, reach_ref, near_ref, far_ref, acc_in, part, hh, hl, halo_inner, ends_ref, out_ref, eh, el, stack, acc):
-    rows = h_ref.shape[1]
+def last_kernel(near_ref, far_ref, sums_in, part, mask_ref, total_ref, hh, hl, halo_inner, ends_ref, out_ref, eh, el, stack):
+    rows = out_ref.shape[2]
     width = 2 * LANES
     gy_odd = lax.axis_index("gy") % 2 == 1
     both_rows = 2 * HMAX
@@ -366,19 +399,12 @@
     below = rot(zl[:HMAX], -9 * NX)[0:1]
     above = rot(zl[HMAX:], -9 * NX)[0:1]
     height = jnp.concatenate([to_column(below, HMAX), to_column(above, HMAX)], axis=0)
-    column = lane_iota((rows, LANES))
-    place = jnp.where(column < rows, column, jnp.where(column < rows + HMAX, column - rows - HMAX, column - HMAX))
-    hrow = lane_iota((1, LANES))
-    heights = jnp.where(
-        hrow < rows, pad_lanes(h_ref[...]), jnp.where(hrow < rows + HMAX, rot(below, rows), rot(above, rows + HMAX))
-    )
-    inside = wall_inside(reach_ref, place, rows) & (column < rows + both_rows)
-    inv = 1.0 / jnp.sum(jnp.where(inside, jnp.broadcast_to(heights, (rows, LANES)), 0.0), axis=1, keepdims=True)
-    scale = [jnp.broadcast_to(inv[r : r + HMAX], (HMAX, LANES)) for r in (0, rows - HMAX)]
-    mask = jnp.where(inside, 1.0, 0.0)
-    mask = rot(jnp.concatenate([mask[:HMAX], mask[rows - HMAX :]], axis=0), -rows)
     lane = lane_iota((both_rows, LANES))
-    mask = jnp.where(lane < both_rows, mask, rot(mask, both_rows))[:, : 2 * both_rows].astype(BF16)
+    heights = jnp.where(lane[0:1] < HMAX, below, rot(above, HMAX))
+    outside = jnp.where(lane < both_rows, mask_ref[...] * heights, 0.0)
+    inv = 1.0 / (total_ref[...] + jnp.sum(outside, axis=1, keepdims=True))
+    scale = [inv[:HMAX], inv[HMAX:]]
+    mask = mask_ref[:, : 2 * both_rows].astype(BF16)
 
     edge_fields(zl, zr, eh, el)
     zero = jnp.zeros((HMAX, LANES), F32)
@@ -403,15 +429,12 @@
                     for f in range(FIELDS)
                 ]
                 sums[i] = list(contract(values, scale[i], *sums[i]))
-    ones = jnp.ones((HMAX, LANES), F32)
+    row = lax.broadcasted_iota(jnp.int32, (both_rows, LANES), 0)
+    row = jnp.where(row < HMAX, row, row + rows - both_rows)
     for k in range(2):
-        acc[0:HMAX, :] = sums[0][k]
-        acc[HMAX : rows - HMAX, :] = acc_in[k, HMAX : rows - HMAX, :]
-        acc[rows - HMAX :, :] = sums[1][k]
-        total = lax.dot_general(
-            ones, acc[...] * (inv * inv), (((1,), (1,)), ((), ())), precision=lax.Precision.HIGHEST, preferred_element_type=F32
-        )
-        out_ref[:, k : k + 1, :] = jnp.broadcast_to(total[0:1][None], (out_ref.shape[0], 1, rows))
+        values = jnp.concatenate([sums[0][k], sums[1][k]], axis=0) * (inv * inv)
+        total = sums_in[k : k + 1, :] + to_row(jnp.sum(values, axis=1, keepdims=True), row)
+        out_ref[:, k : k + 1, :] = jnp.broadcast_to(total[None, :, :rows], (out_ref.shape[0], 1, rows))
 
 
 def call(kernel, out_shape, scratch, limit, *operands):
@@ -455,11 +478,13 @@
     near, far = corner_call(heights, znear, zfar)
     corner_far = lax.ppermute(far, "gy", far_pairs("gy", False))
     corner_near = lax.ppermute(near, "gy", near_pairs("gy"))
-    acc, part, hh, hl, halo_inner = call(
+    sums, part, mask, totals, hh, hl, halo_inner = call(
         outer_kernel,
         [
-            shape((2, rows, LANES), F32),
+            shape((2, LANES), F32),
             shape((blocks + 1, FIELDS, ends, width), F32),
+            shape((ends, LANES), F32),
+            shape((ends, LANES), F32),
             shape((FIELDS, ends, cells), BF16),
             shape((WIDE, ends, cells), BF16),
             shape((blocks, FIELDS, ends, width), F32),
@@ -468,6 +493,7 @@
             pltpu.VMEM((FIELDS, rows, LANES), BF16),
             pltpu.VMEM((WIDE, rows, LANES), BF16),
             pltpu.VMEM((blocks + 1, 2 * rows, FIELDS * width), BF16),
+            pltpu.VMEM((2, rows, LANES), F32),
         ],
         LARGE_VMEM,
         heights,
@@ -489,15 +515,14 @@
             pltpu.VMEM((FIELDS, ends, LANES), BF16),
             pltpu.VMEM((WIDE, ends, LANES), BF16),
             pltpu.VMEM((blocks + 1, 2 * ends, FIELDS * width), BF16),
-            pltpu.VMEM((rows, LANES), F32),
         ],
         LARGE_VMEM,
-        heights,
-        stencil_reach,
         corner_near,
         corner_far,
-        acc,
+        sums,
         part,
+        mask,
+        totals,
         hh,
         hl,
         halo_inner,

time: 34.4 us -> 33.7 us (0.980)
  Pallas kernels: 9.48 us -> 8.77 us
    pallas_call x3, Pallas kernels: 7.77 us -> 7.06 us  [call(): pl.pallas_call(kernel, in_specs=[vmem] * len(operands), out_specs=jax.tre...]
  transfers between devices with their start and end apart: 6 -> 6, of which waited for: 0 -> 0; matrix products, arithmetic and copies ran while one was open for 0% -> 0% of each run, Pallas kernels for 19% -> 18%
where the time goes in v7:
time: 33.7 us; the launch traced here: 33.5 us
  starting transfers between devices  15 us (45%)
  blocking collectives  8.99 us (27%)
  Pallas kernels  8.77 us (26%)
  other arithmetic  0.55 us (2%)
    all_to_all x1, blocking collectives, local(): sums = jnp.sum(lax.all_to_all(sums, 'gz', 0, 0), axis=0)  8.99 us
    pallas_call x3, Pallas kernels, call(): pl.pallas_call(kernel, in_specs=[vmem] * len(operands), out_specs=jax.tre...  7.06 us
    ppermute x1, starting transfers between devices, local(): zfar = lax.ppermute(far, 'gz', far_pairs('gz', True))  4.69 us
    ppermute x1, starting transfers between devices, local(): corner_far = lax.ppermute(far, 'gy', far_pairs('gy', False))  3.49 us
    ppermute x1, starting transfers between devices, local(): yfar = lax.ppermute(wall_far, 'gy', far_pairs('gy', False))  3 us
    ppermute x1, starting transfers between devices, local(): znear = lax.ppermute(near, 'gz', near_pairs('gz'))  2.55 us
    pallas_call x1, Pallas kernels, first_call(): pl.pallas_call(first_kernel, in_specs=[hbm] * 2, out_specs=[vmem] * 8, ou...  1.64 us
    ppermute x1, starting transfers between devices, local(): ynear = lax.ppermute(wall_near, 'gy', near_pairs('gy'))  1.24 us
  transfers between devices with their start and end apart: 6, of which 0 were waited for; matrix products, arithmetic and copies ran while one was open for 0% of the time, Pallas kernels for 18%

profile of v7, /device:TPU:1, one launch (start us, length us, event | category | flops | bytes accessed | tf_op | source)
XLA Modules:
  0.0 33.5 jit_solution(8971452930222408535)
XLA Ops:
  0.0 1.6 %shard_map.46 = (f32[96,128]{1,0:T(8,128)S(1)}, f32[96,128]{1,0:T(8,128)S(1)}, f32[8,6912]{1,0:T(8,128)S(1)}, f32[8,6912]{1,0:T(8,128)S(1)}, f32[3,96,768]{2,1,0...) custom-call(f32[3,96,768]{2,1,0:T(8,128)} %v_ref.1, ...), custom_call_target="tpu_custom_call" | custom-call | tf_op jit(solution)/shard_map/pallas_call | solution.py:114
  1.7 2.5 %collective-permute-start = (f32[96,128]{1,0:T(8,128)S(1)}, f32[96,128]{1,0:T(8,128)S(1)}, u32[]{:S(2)}, u32[]{:S(2)}) collective-permute-start(f32[96,128]{1,0:T(8,128)S(1)} %get-tuple-element.25), channel_id=1, source_target_pairs={{0,1},{1,0},{2,3},{3,2},{4,5},{5,4},{6,7},{7,6},{8,9},{9,8},{10,11... | collective-permute-start | bytes 147464 | tf_op jit(solution)/shard_map/ppermute | solution.py:462
  4.2 4.7 %collective-permute-start.1 = (f32[96,128]{1,0:T(8,128)S(1)}, f32[96,128]{1,0:T(8,128)S(1)}, u32[]{:S(2)}, u32[]{:S(2)}) collective-permute-start(f32[96,128]{1,0:T(8,128)S(1)} %get-tuple-element.26), channel_id=1, source_target_pairs={{1,2},{2,1},{3,4},{4,3},{5,6},{6,5},{7,8},{8,7},{9,10},{10,9},{11,... | collective-permute-start | bytes 147464 | tf_op jit(solution)/shard_map/ppermute | solution.py:461
  8.9 1.2 %collective-permute-start.4 = (f32[8,6912]{1,0:T(8,128)S(1)}, f32[8,6912]{1,0:T(8,128)S(1)}, u32[]{:S(2)}, u32[]{:S(2)}) collective-permute-start(f32[8,6912]{1,0:T(8,128)S(1)} %get-tuple-element.35), channel_id=1, source_target_pairs={{0,16},{16,0},{32,48},{48,32},{64,80},{80,64},{96,112},{112,96},{1... | collective-permute-start | bytes 663560 | tf_op jit(solution)/shard_map/ppermute | solution.py:464
  10.1 3.0 %collective-permute-start.5 = (f32[8,6912]{1,0:T(8,128)S(1)}, f32[8,6912]{1,0:T(8,128)S(1)}, u32[]{:S(2)}, u32[]{:S(2)}) collective-permute-start(f32[8,6912]{1,0:T(8,128)S(1)} %get-tuple-element.36), channel_id=1, source_target_pairs={{16,32},{32,16},{48,64},{64,48},{80,96},{96,80},{17,33},{33,17},{4... | collective-permute-start | bytes 663560 | tf_op jit(solution)/shard_map/ppermute | solution.py:463
  13.1 0.0 copy-start
  13.1 0.0 copy-start.1
  13.2 2.2 %shard_map.48 = (bf16[21,96,768]{2,1,0:T(8,128)(2,1)S(1)}, bf16[15,96,768]{2,1,0:T(8,128)(2,1)S(1)}, f32[2,21,96,256]{3,2,1,0:T(8,128)S(1)}) custom-call(f32[3,96,768]{2,1,0:T(8,128)S(1)} %get-tuple-element.29.v_ref, bf16[6,96,768]{2,1,0:T(8,128)(2,1)S(1)} %get-tuple-element.30.s_ref, bf16[384,256]{1,0:T(8,128)(2,1)S(1)} %get-tuple-element.31.pair_ref), custom_call_target="tpu_custom_call" | custom-call | flops 4000000000 | bytes 1048576 | tf_op jit(solution)/shard_map/pallas_call | solution.py:442
  15.4 0.0 collective-permute-done.znear
  15.4 0.0 collective-permute-done.1.zfar
  15.4 0.0 copy-done
  15.4 0.1 shard_map.47
  15.5 0.0 collective-permute-start.2
  15.5 3.5 %collective-permute-start.3 = (f32[8,256]{1,0:T(8,128)S(1)}, f32[8,256]{1,0:T(8,128)S(1)}, u32[]{:S(2)}, u32[]{:S(2)}) collective-permute-start(f32[8,256]{1,0:T(8,128)S(1)} %get-tuple-element.28), channel_id=1, source_target_pairs={{16,32},{32,16},{48,64},{64,48},{80,96},{96,80},{17,33},{33,17},{4... | collective-permute-start | bytes 24584 | tf_op jit(solution)/shard_map/ppermute | solution.py:479
  19.0 0.0 collective-permute-done.4.ynear
  19.1 0.0 collective-permute-done.5.yfar
  19.1 0.0 copy-done.1
  19.1 3.8 %shard_map.49 = (f32[2,128]{1,0:T(2,128)S(1)}, f32[3,21,16,256]{3,2,1,0:T(8,128)S(1)}, f32[16,128]{1,0:T(8,128)S(1)}, f32[16,128]{1,0:T(8,128)S(1)}, bf16[21,16,...) custom-call(f32[1,96]{1,0:T(1,128)S(1)} %bitcast.4, ...), custom_call_target="tpu_custom_call" | custom-call | flops 4000000000 | bytes 1048576 | tf_op jit(solution)/shard_map/pallas_call | solution.py:442
  22.9 0.0 collective-permute-done.2.near_ref
  22.9 0.0 collective-permute-done.3.far_ref
  22.9 1.0 %shard_map.50 = f32[16,2,96]{2,1,0:T(2,128)S(1)} custom-call(f32[8,256]{1,0:T(8,128)S(1)} %collective-permute-done.2.near_ref, f32[8,256]{1,0:T(8,128)S(1)} %collective-permute-done.3.far_ref, f32[2,128]{1,0:T(2,128)S(1)} %get-tuple-element.38.sums_in, f32[3,21,16,256]{3,2,1,0:T(8,128)S(1)} %get-tuple-element.39.part, ...), custom_call_target="tpu_custom_call" | custom-call | flops 4000000000 | bytes 1048576 | tf_op jit(solution)/shard_map/pallas_call | solution.py:442
  23.9 9.0 %all_to_all.5 = f32[16,2,96]{2,1,0:T(2,128)S(1)} all-to-all(f32[16,2,96]{2,1,0:T(2,128)S(1)} %shard_map.50), channel_id=1, replica_groups=mesh['gy'=8,'gz'=16] {'gz'}, dimensions={0} | all-to-all | bytes 24576 | tf_op jit(solution)/shard_map/all_to_all | solution.py:531
  33.0 0.5 %fusion = f32[96]{0:T(128)} fusion(f32[2,96]{1,0:T(2,128)S(1)} %reduce_sum.9), kind=kLoop, calls=%fused_computation.1 | loop fusion | flops 384 | bytes 1152 | tf_op jit(solution)/shard_map/div | solution.py:533
  (1 shorter events, 0.0 us)
Async XLA Ops:
  1.7 13.7 %collective-permute-start = (f32[96,128]{1,0:T(8,128)S(1)}, f32[96,128]{1,0:T(8,128)S(1)}, u32[]{:S(2)}, u32[]{:S(2)}) collective-permute-start(f32[96,128]{1,0:T(8,128)S(1)} %get-tuple-element.25), channel_id=1, source_target_pairs={{0,1},{1,0},{2,3},{3,2},{4,5},{5,4},{6,7},{7,6},{8,9},{9,8},{10,11... | collective-permute-start | bytes 147464 | tf_op jit(solution)/shard_map/ppermute | solution.py:462
  4.2 11.2 %collective-permute-start.1 = (f32[96,128]{1,0:T(8,128)S(1)}, f32[96,128]{1,0:T(8,128)S(1)}, u32[]{:S(2)}, u32[]{:S(2)}) collective-permute-start(f32[96,128]{1,0:T(8,128)S(1)} %get-tuple-element.26), channel_id=1, source_target_pairs={{1,2},{2,1},{3,4},{4,3},{5,6},{6,5},{7,8},{8,7},{9,10},{10,9},{11,... | collective-permute-start | bytes 147464 | tf_op jit(solution)/shard_map/ppermute | solution.py:461
  8.9 10.2 %collective-permute-start.4 = (f32[8,6912]{1,0:T(8,128)S(1)}, f32[8,6912]{1,0:T(8,128)S(1)}, u32[]{:S(2)}, u32[]{:S(2)}) collective-permute-start(f32[8,6912]{1,0:T(8,128)S(1)} %get-tuple-element.35), channel_id=1, source_target_pairs={{0,16},{16,0},{32,48},{48,32},{64,80},{80,64},{96,112},{112,96},{1... | collective-permute-start | bytes 663560 | tf_op jit(solution)/shard_map/ppermute | solution.py:464
  10.1 8.9 %collective-permute-start.5 = (f32[8,6912]{1,0:T(8,128)S(1)}, f32[8,6912]{1,0:T(8,128)S(1)}, u32[]{:S(2)}, u32[]{:S(2)}) collective-permute-start(f32[8,6912]{1,0:T(8,128)S(1)} %get-tuple-element.36), channel_id=1, source_target_pairs={{16,32},{32,16},{48,64},{64,48},{80,96},{96,80},{17,33},{33,17},{4... | collective-permute-start | bytes 663560 | tf_op jit(solution)/shard_map/ppermute | solution.py:463
  13.1 2.3 %copy-start = (f32[96]{0:T(128)S(1)}, f32[96]{0:T(128)}, u32[]{:S(2)}) copy-start(f32[96]{0:T(128)} %param.6) | copy-start | bytes 1156
  13.1 5.9 %copy-start.1 = (s32[2,96]{1,0:T(2,128)S(1)}, s32[2,96]{1,0:T(2,128)}, u32[]{:S(2)}) copy-start(s32[2,96]{1,0:T(2,128)} %reach_ref.1) | copy-start | bytes 2308
  15.5 7.4 %collective-permute-start.2 = (f32[8,256]{1,0:T(8,128)S(1)}, f32[8,256]{1,0:T(8,128)S(1)}, u32[]{:S(2)}, u32[]{:S(2)}) collective-permute-start(f32[8,256]{1,0:T(8,128)S(1)} %get-tuple-element.27), channel_id=1, source_target_pairs={{0,16},{16,0},{32,48},{48,32},{64,80},{80,64},{96,112},{112,96},{1... | collective-permute-start | bytes 24584 | tf_op jit(solution)/shard_map/ppermute | solution.py:480
  15.5 7.4 %collective-permute-start.3 = (f32[8,256]{1,0:T(8,128)S(1)}, f32[8,256]{1,0:T(8,128)S(1)}, u32[]{:S(2)}, u32[]{:S(2)}) collective-permute-start(f32[8,256]{1,0:T(8,128)S(1)} %get-tuple-element.28), channel_id=1, source_target_pairs={{16,32},{32,16},{48,64},{64,48},{80,96},{96,80},{17,33},{33,17},{4... | collective-permute-start | bytes 24584 | tf_op jit(solution)/shard_map/ppermute | solution.py:479

commit v8 on v7

--- a/solution.py
+++ b/solution.py
@@ -250,9 +250,11 @@
     return jnp.concatenate([x[:HMAX], x[x.shape[0] - HMAX :]], axis=0)
 
 
-def wall_block(g, mask, height, inv, stack, acc_ref, part_ref):
+def wall_block(g, own_ref, height_ref, inv_ref, stack, acc_ref, part_ref):
     rows = g[0].shape[0]
     width = 2 * LANES
+    height = jnp.concatenate([height_ref[...], height_ref[...]], axis=1)
+    mask = own_ref[:, : 2 * rows]
     for f in range(FIELDS):
         hi, lo = split2(g[f] * height)
         stack[0:rows, f * width : (f + 1) * width] = hi
@@ -264,7 +266,7 @@
     for r in range(HMAX, rows - HMAX, HMAX):
         num = acc_ref[0, r : r + HMAX, :]
         den = acc_ref[1, r : r + HMAX, :]
-        scale = jnp.broadcast_to(inv[r : r + HMAX], (HMAX, LANES))
+        scale = inv_ref[r : r + HMAX, :]
         for c in range(2):
             parts = [
                 merged[r : r + HMAX, f * width + c * LANES : f * width + (c + 1) * LANES] for f in range(FIELDS)
@@ -274,7 +276,13 @@
         acc_ref[1, r : r + HMAX, :] = den
 
 
-def inner_kernel(v_ref, s_ref, pair_ref, fh, fl, inner):
+def leaves_early():
+    gz = lax.axis_index("gz")
+    y, z = gz // 4, gz % 4
+    return (z == 0) | ((z == 1) & (y <= 1))
+
+
+def inner_work(v_ref, s_ref, pair_ref, fh, fl, inner):
     rows, cells = v_ref.shape[1:]
     for t in range(cells // LANES):
         at = slice(t * LANES, (t + 1) * LANES)
@@ -296,15 +304,23 @@
             inner[n, f] = g[f]
 
 
-def outer_kernel(
-    h_ref, reach_ref, fh, fl, inner, znear, zfar, ynear, yfar, pair_ref, ends_ref,
-    sums_ref, part_ref, mask_ref, total_ref, hh, hl, halo_inner, eh, el, stack, acc_ref,
+def early_kernel(v_ref, s_ref, pair_ref, a, b, c, d, fh, fl, inner, *same):
+    @pl.when(leaves_early())
+    def _():
+        inner_work(v_ref, s_ref, pair_ref, fh, fl, inner)
+
+
+def late_kernel(v_ref, s_ref, pair_ref, a, b, c, fh, fl, inner):
+    @pl.when(jnp.logical_not(leaves_early()))
+    def _():
+        inner_work(v_ref, s_ref, pair_ref, fh, fl, inner)
+
+
+def wall_kernel(
+    h_ref, reach_ref, inner, acc_ref, part_ref, own_ref, height_ref, inv_ref, mask_ref, total_ref, stack
 ):
-    rows, cells = fh.shape[1:]
-    blocks = inner.shape[0]
+    rows = h_ref.shape[1]
     ends = 2 * HMAX
-    gz_odd = lax.axis_index("gz") % 2 == 1
-    gy_odd = lax.axis_index("gy") % 2 == 1
     reach = pad_lanes(reach_ref[...].astype(F32))
     down = to_column(reach[0:1], rows).astype(jnp.int32)
     up = to_column(reach[1:2], rows).astype(jnp.int32)
@@ -312,12 +328,12 @@
     row = lax.broadcasted_iota(jnp.int32, (rows, 2 * LANES), 0)
     place = jnp.where(column < rows, column, column - rows)
     inside = stencil_holds(place, row, down, up, rows)
-    mask = jnp.where(inside, 1.0, 0.0)[:, : 2 * rows].astype(BF16)
+    own_ref[...] = jnp.where(inside, 1.0, 0.0).astype(BF16)
     heights = pad_lanes(h_ref[...])
-    height = to_column(heights, rows)
+    height_ref[...] = jnp.broadcast_to(to_column(heights, rows), (rows, LANES))
     own = inside[:, :LANES] & (column[:, :LANES] < rows)
     total = jnp.sum(jnp.where(own, jnp.broadcast_to(heights, (rows, LANES)), 0.0), axis=1, keepdims=True)
-    inv = 1.0 / total
+    inv_ref[...] = jnp.broadcast_to(1.0 / total, (rows, LANES))
     total_ref[...] = jnp.broadcast_to(end_rows(total), (ends, LANES))
     column = lane_iota((ends, LANES))
     row = lax.broadcasted_iota(jnp.int32, (ends, LANES), 0)
@@ -327,13 +343,22 @@
     inside = stencil_holds(place, row, end_rows(down), end_rows(up), rows) & (column < 2 * ends)
     mask_ref[...] = jnp.where(inside, 1.0, 0.0)
     acc_ref[...] = jnp.zeros_like(acc_ref)
+    for n in range(inner.shape[0]):
+        g = [inner[n, f] for f in range(FIELDS)]
+        wall_block(g, own_ref, height_ref, inv_ref, stack.at[n], acc_ref, part_ref.at[n])
+
+
+def outer_kernel(
+    fh, fl, znear, zfar, ynear, yfar, pair_ref, ends_ref, acc_in, own_ref, height_ref, inv_ref,
+    sums_ref, part_ref, hh, hl, halo_inner, eh, el, stack, acc_ref,
+):
+    rows, cells = fh.shape[1:]
+    gz_odd = lax.axis_index("gz") % 2 == 1
+    gy_odd = lax.axis_index("gy") % 2 == 1
+    acc_ref[...] = acc_in[...]
     edge_fields(jnp.where(gz_odd, znear[...], zfar[...]), jnp.where(gz_odd, zfar[...], znear[...]), eh, el)
-    for n in range(blocks + 1):
-        if n < blocks:
-            g = [inner[n, f] for f in range(FIELDS)]
-        else:
-            g = smooth_ends(fh, fl, eh, el, ends_ref)
-        wall_block(g, mask, height, inv, stack.at[n], acc_ref, part_ref.at[n])
+    g = smooth_ends(fh, fl, eh, el, ends_ref)
+    wall_block(g, own_ref, height_ref, inv_ref, stack, acc_ref, part_ref)
     for t in range(cells // LANES):
         at = slice(t * LANES, (t + 1) * LANES)
 
@@ -349,10 +374,11 @@
             near, far = ynear[:, span], yfar[:, span]
             raw.append(jnp.concatenate([jnp.where(gy_odd, near, far), jnp.where(gy_odd, far, near)], axis=0))
         store_fields(raw[:3], raw[3:], put_high, put_low)
-    for n in range(blocks):
+    for n in range(halo_inner.shape[0]):
         g = smooth_pair(n, hh, hl, pair_ref)
         for f in range(FIELDS):
             halo_inner[n, f] = g[f]
+    inv = inv_ref[...]
     for k in range(2):
         plane_sums = jnp.sum(acc_ref[k] * (inv * inv), axis=1, keepdims=True)
         sums_ref[k : k + 1, :] = to_row(plane_sums, lax.broadcasted_iota(jnp.int32, (rows, LANES), 0))
@@ -384,7 +410,7 @@
         store_fields(raw[:3], raw[3:], put_high, put_low)
 
 
-def last_kernel(near_ref, far_ref, sums_in, part, mask_ref, total_ref, hh, hl, halo_inner, ends_ref, out_ref, eh, el, stack):
+def last_kernel(near_ref, far_ref, sums_in, part_inner, part_ends, mask_ref, total_ref, hh, hl, halo_inner, ends_ref, out_ref, eh, el, stack):
     rows = out_ref.shape[2]
     width = 2 * LANES
     gy_odd = lax.axis_index("gy") % 2 == 1
@@ -413,7 +439,9 @@
     for n in range(blocks + 1):
         if n < blocks:
             g = [halo_inner[n, f] for f in range(FIELDS)]
+            part = part_inner.at[n]
         else:
+            part = part_ends
             g = smooth_ends(hh, hl, eh, el, ends_ref)
         for f in range(FIELDS):
             hi, lo = split2(g[f] * height)
@@ -425,7 +453,7 @@
             for c in range(2):
                 at = slice(c * LANES, (c + 1) * LANES)
                 values = [
-                    part[n, f, rr, at] + merged[rr, f * width + c * LANES : f * width + (c + 1) * LANES]
+                    part[f, rr, at] + merged[rr, f * width + c * LANES : f * width + (c + 1) * LANES]
                     for f in range(FIELDS)
                 ]
                 sums[i] = list(contract(values, scale[i], *sums[i]))
@@ -437,7 +465,7 @@
         out_ref[:, k : k + 1, :] = jnp.broadcast_to(total[None, :, :rows], (out_ref.shape[0], 1, rows))
 
 
-def call(kernel, out_shape, scratch, limit, *operands):
+def call(kernel, out_shape, scratch, limit, *operands, aliases=None):
     vmem = pl.BlockSpec(memory_space=pltpu.VMEM)
     return pl.pallas_call(
         kernel,
@@ -445,6 +473,7 @@
         out_specs=jax.tree.map(lambda _: vmem, out_shape),
         out_shape=out_shape,
         scratch_shapes=scratch,
+        input_output_aliases=aliases or {},
         compiler_params=pltpu.CompilerParams(vmem_limit_bytes=limit),
         cost_estimate=pl.CostEstimate(flops=4 * 10**9, bytes_accessed=2**20, transcendentals=0),
     )(*operands)
@@ -458,33 +487,65 @@
     shape = jax.ShapeDtypeStruct
     heights = cell_height.reshape(1, rows)
     near, far, wall_near, wall_far, velocity, strain, pair, both_ends = first_call(velocity, strain)
-    zfar = lax.ppermute(far, "gz", far_pairs("gz", True))
-    znear = lax.ppermute(near, "gz", near_pairs("gz"))
-    yfar = lax.ppermute(wall_far, "gy", far_pairs("gy", False))
-    ynear = lax.ppermute(wall_near, "gy", near_pairs("gy"))
-    fh, fl, inner = call(
-        inner_kernel,
-        [
-            shape((FIELDS, rows, cells), BF16),
-            shape((WIDE, rows, cells), BF16),
-            shape((blocks, FIELDS, rows, width), F32),
-        ],
+    own_work = [
+        shape((FIELDS, rows, cells), BF16),
+        shape((WIDE, rows, cells), BF16),
+        shape((blocks, FIELDS, rows, width), F32),
+    ]
+    messages = (near, far, wall_near, wall_far)
+    fh, fl, inner, near, far, wall_near, wall_far = call(
+        early_kernel,
+        own_work + [shape(x.shape, x.dtype) for x in messages],
         [],
         LARGE_VMEM,
         velocity,
         strain,
         pair,
+        *messages,
+        aliases={3 + i: 3 + i for i in range(4)},
+    )
+    znear = lax.ppermute(near, "gz", near_pairs("gz"))
+    zfar = lax.ppermute(far, "gz", far_pairs("gz", True))
+    yfar = lax.ppermute(wall_far, "gy", far_pairs("gy", False))
+    ynear = lax.ppermute(wall_near, "gy", near_pairs("gy"))
+    fh, fl, inner = call(
+        late_kernel,
+        own_work,
+        [],
+        LARGE_VMEM,
+        velocity,
+        strain,
+        pair,
+        fh,
+        fl,
+        inner,
+        aliases={3 + i: i for i in range(3)},
+    )
+    acc, part_inner, own, height, inv, mask, totals = call(
+        wall_kernel,
+        [
+            shape((2, rows, LANES), F32),
+            shape((blocks, FIELDS, ends, width), F32),
+            shape((rows, width), BF16),
+            shape((rows, LANES), F32),
+            shape((rows, LANES), F32),
+            shape((ends, LANES), F32),
+            shape((ends, LANES), F32),
+        ],
+        [pltpu.VMEM((blocks, 2 * rows, FIELDS * width), BF16)],
+        LARGE_VMEM,
+        heights,
+        stencil_reach,
+        inner,
     )
     near, far = corner_call(heights, znear, zfar)
     corner_far = lax.ppermute(far, "gy", far_pairs("gy", False))
     corner_near = lax.ppermute(near, "gy", near_pairs("gy"))
-    sums, part, mask, totals, hh, hl, halo_inner = call(
+    sums, part_ends, hh, hl, halo_inner = call(
         outer_kernel,
         [
             shape((2, LANES), F32),
-            shape((blocks + 1, FIELDS, ends, width), F32),
-            shape((ends, LANES), F32),
-            shape((ends, LANES), F32),
+            shape((FIELDS, ends, width), F32),
             shape((FIELDS, ends, cells), BF16),
             shape((WIDE, ends, cells), BF16),
             shape((blocks, FIELDS, ends, width), F32),
@@ -492,21 +553,22 @@
         [
             pltpu.VMEM((FIELDS, rows, LANES), BF16),
             pltpu.VMEM((WIDE, rows, LANES), BF16),
-            pltpu.VMEM((blocks + 1, 2 * rows, FIELDS * width), BF16),
+            pltpu.VMEM((2 * rows, FIELDS * width), BF16),
             pltpu.VMEM((2, rows, LANES), F32),
         ],
         LARGE_VMEM,
-        heights,
-        stencil_reach,
         fh,
         fl,
-        inner,
         znear,
         zfar,
         ynear,
         yfar,
         pair,
         both_ends,
+        acc,
+        own,
+        height,
+        inv,
     )
     sums = call(
         last_kernel,
@@ -520,7 +582,8 @@
         corner_near,
         corner_far,
         sums,
-        part,
+        part_inner,
+        part_ends,
         mask,
         totals,
         hh,

time: 33.7 us -> 34.8 us (1.033)
  blocking collectives: 8.99 us -> 11.6 us
  starting transfers between devices: 15 us -> 12.8 us
  local copies, waits for them, and re-layouts: 0.01 us -> 0.65 us
    all_to_all x1, blocking collectives: 8.99 us -> 11.6 us  [local(): sums = jnp.sum(lax.all_to_all(sums, 'gz', 0, 0), axis=0)]
    ppermute x1, starting transfers between devices: 4.69 us -> 2.45 us  [local(): zfar = lax.ppermute(far, 'gz', far_pairs('gz', True))]
    unnamed x4, local copies, waits for them, and re-layouts: 0.01 us -> 0.65 us
    pallas_call x3 -> x5, Pallas kernels: 7.06 us -> 7.19 us  [call(): pl.pallas_call(kernel, in_specs=[vmem] * len(operands), out_specs=jax.tre...]
  transfers between devices with their start and end apart: 6 -> 6, of which waited for: 0 -> 0; matrix products, arithmetic and copies ran while one was open for 0% -> 0% of each run, Pallas kernels for 18% -> 11%
where the time goes in v8:
time: 34.8 us; the launch traced here: 34.6 us
  starting transfers between devices  12.8 us (37%)
  blocking collectives  11.6 us (33%)
  Pallas kernels  8.91 us (26%)
  local copies, waits for them, and re-layouts  0.65 us (2%)
  other arithmetic  0.55 us (2%)
    all_to_all x1, blocking collectives, local(): sums = jnp.sum(lax.all_to_all(sums, 'gz', 0, 0), axis=0)  11.6 us
    pallas_call x5, Pallas kernels, call(): pl.pallas_call(kernel, in_specs=[vmem] * len(operands), out_specs=jax.tre...  7.19 us
    ppermute x1, starting transfers between devices, local(): corner_far = lax.ppermute(far, 'gy', far_pairs('gy', False))  3.49 us
    ppermute x1, starting transfers between devices, local(): yfar = lax.ppermute(wall_far, 'gy', far_pairs('gy', False))  3 us
    ppermute x1, starting transfers between devices, local(): znear = lax.ppermute(near, 'gz', near_pairs('gz'))  2.55 us
    ppermute x1, starting transfers between devices, local(): zfar = lax.ppermute(far, 'gz', far_pairs('gz', True))  2.45 us
    pallas_call x1, Pallas kernels, first_call(): pl.pallas_call(first_kernel, in_specs=[hbm] * 2, out_specs=[vmem] * 8, ou...  1.64 us
    ppermute x1, starting transfers between devices, local(): ynear = lax.ppermute(wall_near, 'gy', near_pairs('gy'))  1.24 us
  transfers between devices with their start and end apart: 6, of which 0 were waited for; matrix products, arithmetic and copies ran while one was open for 0% of the time, Pallas kernels for 11%

profile of v8, /device:TPU:1, one launch (start us, length us, event | category | flops | bytes accessed | tf_op | source)
XLA Modules:
  0.0 34.6 jit_solution(1147891969980499082)
XLA Ops:
  0.0 1.6 %shard_map.46 = (f32[96,128]{1,0:T(8,128)S(1)}, f32[96,128]{1,0:T(8,128)S(1)}, f32[8,6912]{1,0:T(8,128)S(1)}, f32[8,6912]{1,0:T(8,128)S(1)}, f32[3,96,768]{2,1,0...) custom-call(f32[3,96,768]{2,1,0:T(8,128)} %v_ref.1, ...), custom_call_target="tpu_custom_call" | custom-call | tf_op jit(solution)/shard_map/pallas_call | solution.py:114
  1.7 2.3 %shard_map.47 = (bf16[21,96,768]{2,1,0:T(8,128)(2,1)S(1)}, bf16[15,96,768]{2,1,0:T(8,128)(2,1)S(1)}, f32[2,21,96,256]{3,2,1,0:T(8,128)S(1)}, f32[96,128]{1,0:T(8...) custom-call(f32[3,96,768]{2,1,0:T(8,128)S(1)} %get-tuple-element.37., ...), custom_call_target="tpu_custom_call", output_to_operand_aliasing={{3}: (3, {}), {4}: (4, {}), {5}: (5, {}), {6}: (6, {})} | custom-call | flops 4000000000 | bytes 1048576 | tf_op jit(solution)/shard_map/pallas_call | solution.py:470
  3.9 2.5 %collective-permute-start = (f32[96,128]{1,0:T(8,128)S(1)}, f32[96,128]{1,0:T(8,128)S(1)}, u32[]{:S(2)}, u32[]{:S(2)}) collective-permute-start(f32[96,128]{1,0:T(8,128)S(1)} %get-tuple-element.44), channel_id=1, source_target_pairs={{0,1},{1,0},{2,3},{3,2},{4,5},{5,4},{6,7},{7,6},{8,9},{9,8},{10,11... | collective-permute-start | bytes 147464 | tf_op jit(solution)/shard_map/ppermute | solution.py:507
  6.5 2.4 %collective-permute-start.1 = (f32[96,128]{1,0:T(8,128)S(1)}, f32[96,128]{1,0:T(8,128)S(1)}, u32[]{:S(2)}, u32[]{:S(2)}) collective-permute-start(f32[96,128]{1,0:T(8,128)S(1)} %get-tuple-element.45), channel_id=1, source_target_pairs={{1,2},{2,1},{3,4},{4,3},{5,6},{6,5},{7,8},{8,7},{9,10},{10,9},{11,... | collective-permute-start | bytes 147464 | tf_op jit(solution)/shard_map/ppermute | solution.py:508
  8.9 1.2 %collective-permute-start.4 = (f32[8,6912]{1,0:T(8,128)S(1)}, f32[8,6912]{1,0:T(8,128)S(1)}, u32[]{:S(2)}, u32[]{:S(2)}) collective-permute-start(f32[8,6912]{1,0:T(8,128)S(1)} %get-tuple-element.53), channel_id=1, source_target_pairs={{0,16},{16,0},{32,48},{48,32},{64,80},{80,64},{96,112},{112,96},{1... | collective-permute-start | bytes 663560 | tf_op jit(solution)/shard_map/ppermute | solution.py:510
  10.2 3.0 %collective-permute-start.5 = (f32[8,6912]{1,0:T(8,128)S(1)}, f32[8,6912]{1,0:T(8,128)S(1)}, u32[]{:S(2)}, u32[]{:S(2)}) collective-permute-start(f32[8,6912]{1,0:T(8,128)S(1)} %get-tuple-element.54), channel_id=1, source_target_pairs={{16,32},{32,16},{48,64},{64,48},{80,96},{96,80},{17,33},{33,17},{4... | collective-permute-start | bytes 663560 | tf_op jit(solution)/shard_map/ppermute | solution.py:509
  13.2 0.0 copy-start
  13.2 0.0 copy-start.1
  13.2 0.6 %copy-done = f32[96]{0:T(128)S(1)} copy-done((f32[96]{0:T(128)S(1)}, f32[96]{0:T(128)}, u32[]{:S(2)}) %copy-start) | copy-done | bytes 408
  13.8 0.0 copy-done.1
  13.9 1.5 %shard_map.50 = (f32[2,96,128]{2,1,0:T(8,128)S(1)}, f32[2,21,16,256]{3,2,1,0:T(8,128)S(1)}, bf16[96,256]{1,0:T(8,128)(2,1)S(1)}, f32[96,128]{1,0:T(8,128)S(1)}, ...) custom-call(f32[1,96]{1,0:T(1,128)S(1)} %bitcast.3, s32[2,96]{1,0:T(2,128)S(1)} %copy-done.1, ...), custom_call_target="tpu_custom_call" | custom-call | flops 4000000000 | bytes 1048576 | tf_op jit(solution)/shard_map/pallas_call | solution.py:470
  15.4 0.0 collective-permute-done.znear
  15.4 0.0 collective-permute-done.1.zfar
  15.4 0.1 shard_map.48
  15.5 0.0 collective-permute-start.2
  15.5 3.5 %collective-permute-start.3 = (f32[8,256]{1,0:T(8,128)S(1)}, f32[8,256]{1,0:T(8,128)S(1)}, u32[]{:S(2)}, u32[]{:S(2)}) collective-permute-start(f32[8,256]{1,0:T(8,128)S(1)} %get-tuple-element.47), channel_id=1, source_target_pairs={{16,32},{32,16},{48,64},{64,48},{80,96},{96,80},{17,33},{33,17},{4... | collective-permute-start | bytes 24584 | tf_op jit(solution)/shard_map/ppermute | solution.py:542
  19.0 0.0 collective-permute-done.4.ynear
  19.0 0.0 collective-permute-done.5.yfar
  19.0 2.4 %shard_map.51 = (f32[2,128]{1,0:T(2,128)S(1)}, f32[21,16,256]{2,1,0:T(8,128)S(1)}, bf16[21,16,768]{2,1,0:T(8,128)(2,1)S(1)}, bf16[15,16,768]{2,1,0:T(8,128)(2,1)S(1)}, f32[2,21,16,256]{3,2,1,0:T(8,128)S(1)}) custom-call(bf16[21,96,768]{2,1,0:T(8,128)(2,1)S(1)} %get-tuple-element.51.fh, bf16[15,96,768]{2,1,0:T(8,128)(2,1)S(1)} %get-tuple-element.52.fl, ...), custom_call_target="tpu_custom_call" | custom-call | flops 4000000000 | bytes 1048576 | tf_op jit(solution)/shard_map/pallas_call | solution.py:470
  21.4 0.0 collective-permute-done.2.near_ref
  21.4 0.0 collective-permute-done.3.far_ref
  21.4 1.0 %shard_map.52 = f32[16,2,96]{2,1,0:T(2,128)S(1)} custom-call(f32[8,256]{1,0:T(8,128)S(1)} %collective-permute-done.2.near_ref, f32[8,256]{1,0:T(8,128)S(1)} %collective-permute-done.3.far_ref, f32[2,128]{1,0:T(2,128)S(1)} %get-tuple-element.61.sums_in, f32[2,21,16,256]{3,2,1,0:T(8,128)S(1)} %get-tuple-element.62.part_inner, ...), custom_call_target="tpu_custom_call" | custom-call | flops 4000000000 | bytes 1048576 | tf_op jit(solution)/shard_map/pallas_call | solution.py:470
  22.5 11.6 %all_to_all.5 = f32[16,2,96]{2,1,0:T(2,128)S(1)} all-to-all(f32[16,2,96]{2,1,0:T(2,128)S(1)} %shard_map.52), channel_id=1, replica_groups=mesh['gy'=8,'gz'=16] {'gz'}, dimensions={0} | all-to-all | bytes 24576 | tf_op jit(solution)/shard_map/all_to_all | solution.py:594
  34.1 0.5 %fusion = f32[96]{0:T(128)} fusion(f32[2,96]{1,0:T(2,128)S(1)} %reduce_sum.9), kind=kLoop, calls=%fused_computation.1 | loop fusion | flops 384 | bytes 1152 | tf_op jit(solution)/shard_map/div | solution.py:596
  (2 shorter events, 0.1 us)
Async XLA Ops:
  3.9 11.5 %collective-permute-start = (f32[96,128]{1,0:T(8,128)S(1)}, f32[96,128]{1,0:T(8,128)S(1)}, u32[]{:S(2)}, u32[]{:S(2)}) collective-permute-start(f32[96,128]{1,0:T(8,128)S(1)} %get-tuple-element.44), channel_id=1, source_target_pairs={{0,1},{1,0},{2,3},{3,2},{4,5},{5,4},{6,7},{7,6},{8,9},{9,8},{10,11... | collective-permute-start | bytes 147464 | tf_op jit(solution)/shard_map/ppermute | solution.py:507
  6.5 8.9 %collective-permute-start.1 = (f32[96,128]{1,0:T(8,128)S(1)}, f32[96,128]{1,0:T(8,128)S(1)}, u32[]{:S(2)}, u32[]{:S(2)}) collective-permute-start(f32[96,128]{1,0:T(8,128)S(1)} %get-tuple-element.45), channel_id=1, source_target_pairs={{1,2},{2,1},{3,4},{4,3},{5,6},{6,5},{7,8},{8,7},{9,10},{10,9},{11,... | collective-permute-start | bytes 147464 | tf_op jit(solution)/shard_map/ppermute | solution.py:508
  8.9 10.1 %collective-permute-start.4 = (f32[8,6912]{1,0:T(8,128)S(1)}, f32[8,6912]{1,0:T(8,128)S(1)}, u32[]{:S(2)}, u32[]{:S(2)}) collective-permute-start(f32[8,6912]{1,0:T(8,128)S(1)} %get-tuple-element.53), channel_id=1, source_target_pairs={{0,16},{16,0},{32,48},{48,32},{64,80},{80,64},{96,112},{112,96},{1... | collective-permute-start | bytes 663560 | tf_op jit(solution)/shard_map/ppermute | solution.py:510
  10.2 8.9 %collective-permute-start.5 = (f32[8,6912]{1,0:T(8,128)S(1)}, f32[8,6912]{1,0:T(8,128)S(1)}, u32[]{:S(2)}, u32[]{:S(2)}) collective-permute-start(f32[8,6912]{1,0:T(8,128)S(1)} %get-tuple-element.54), channel_id=1, source_target_pairs={{16,32},{32,16},{48,64},{64,48},{80,96},{96,80},{17,33},{33,17},{4... | collective-permute-start | bytes 663560 | tf_op jit(solution)/shard_map/ppermute | solution.py:509
  13.2 0.7 %copy-start = (f32[96]{0:T(128)S(1)}, f32[96]{0:T(128)}, u32[]{:S(2)}) copy-start(f32[96]{0:T(128)} %param.6) | copy-start | bytes 1156
  13.2 0.7 %copy-start.1 = (s32[2,96]{1,0:T(2,128)S(1)}, s32[2,96]{1,0:T(2,128)}, u32[]{:S(2)}) copy-start(s32[2,96]{1,0:T(2,128)} %reach_ref.1) | copy-start | bytes 2308
  15.5 5.9 %collective-permute-start.2 = (f32[8,256]{1,0:T(8,128)S(1)}, f32[8,256]{1,0:T(8,128)S(1)}, u32[]{:S(2)}, u32[]{:S(2)}) collective-permute-start(f32[8,256]{1,0:T(8,128)S(1)} %get-tuple-element.46), channel_id=1, source_target_pairs={{0,16},{16,0},{32,48},{48,32},{64,80},{80,64},{96,112},{112,96},{1... | collective-permute-start | bytes 24584 | tf_op jit(solution)/shard_map/ppermute | solution.py:543
  15.5 5.9 %collective-permute-start.3 = (f32[8,256]{1,0:T(8,128)S(1)}, f32[8,256]{1,0:T(8,128)S(1)}, u32[]{:S(2)}, u32[]{:S(2)}) collective-permute-start(f32[8,256]{1,0:T(8,128)S(1)} %get-tuple-element.47), channel_id=1, source_target_pairs={{16,32},{32,16},{48,64},{64,48},{80,96},{96,80},{17,33},{33,17},{4... | collective-permute-start | bytes 24584 | tf_op jit(solution)/shard_map/ppermute | solution.py:542

commit v9 on v8

--- a/solution.py
+++ b/solution.py
@@ -277,9 +277,7 @@
 
 
 def leaves_early():
-    gz = lax.axis_index("gz")
-    y, z = gz // 4, gz % 4
-    return (z == 0) | ((z == 1) & (y <= 1))
+    return lax.axis_index("gz") == 0
 
 
 def inner_work(v_ref, s_ref, pair_ref, fh, fl, inner):

time: 34.8 us -> 33.8 us (0.971)
  blocking collectives: 11.6 us -> 10.6 us
    ppermute x1, starting transfers between devices: 2.55 us -> 0.3 us  [local(): znear = lax.ppermute(near, 'gz', near_pairs('gz'))]
    ppermute x1, starting transfers between devices: 2.45 us -> 4.69 us  [local(): zfar = lax.ppermute(far, 'gz', far_pairs('gz', True))]
    all_to_all x1, blocking collectives: 11.6 us -> 10.6 us  [local(): sums = jnp.sum(lax.all_to_all(sums, 'gz', 0, 0), axis=0)]
  transfers between devices with their start and end apart: 6 -> 6, of which waited for: 0 -> 0; matrix products, arithmetic and copies ran while one was open for 0% -> 0% of each run, Pallas kernels for 11% -> 12%
where the time goes in v9:
time: 33.8 us; the launch traced here: 33.6 us
  starting transfers between devices  12.7 us (38%)
  blocking collectives  10.6 us (31%)
  Pallas kernels  8.89 us (26%)
  local copies, waits for them, and re-layouts  0.66 us (2%)
  other arithmetic  0.55 us (2%)
    all_to_all x1, blocking collectives, local(): sums = jnp.sum(lax.all_to_all(sums, 'gz', 0, 0), axis=0)  10.6 us
    pallas_call x5, Pallas kernels, call(): pl.pallas_call(kernel, in_specs=[vmem] * len(operands), out_specs=jax.tre...  7.18 us
    ppermute x1, starting transfers between devices, local(): zfar = lax.ppermute(far, 'gz', far_pairs('gz', True))  4.69 us
    ppermute x1, starting transfers between devices, local(): corner_far = lax.ppermute(far, 'gy', far_pairs('gy', False))  3.48 us
    ppermute x1, starting transfers between devices, local(): yfar = lax.ppermute(wall_far, 'gy', far_pairs('gy', False))  3 us
    pallas_call x1, Pallas kernels, first_call(): pl.pallas_call(first_kernel, in_specs=[hbm] * 2, out_specs=[vmem] * 8, ou...  1.64 us
    ppermute x1, starting transfers between devices, local(): ynear = lax.ppermute(wall_near, 'gy', near_pairs('gy'))  1.24 us
  transfers between devices with their start and end apart: 6, of which 0 were waited for; matrix products, arithmetic and copies ran while one was open for 0% of the time, Pallas kernels for 12%

profile of v9, /device:TPU:1, one launch (start us, length us, event | category | flops | bytes accessed | tf_op | source)
XLA Modules:
  0.0 33.6 jit_solution(17951920449774982553)
XLA Ops:
  0.0 1.6 %shard_map.46 = (f32[96,128]{1,0:T(8,128)S(1)}, f32[96,128]{1,0:T(8,128)S(1)}, f32[8,6912]{1,0:T(8,128)S(1)}, f32[8,6912]{1,0:T(8,128)S(1)}, f32[3,96,768]{2,1,0...) custom-call(f32[3,96,768]{2,1,0:T(8,128)} %v_ref.1, ...), custom_call_target="tpu_custom_call" | custom-call | tf_op jit(solution)/shard_map/pallas_call | solution.py:114
  1.7 2.3 %shard_map.47 = (bf16[21,96,768]{2,1,0:T(8,128)(2,1)S(1)}, bf16[15,96,768]{2,1,0:T(8,128)(2,1)S(1)}, f32[2,21,96,256]{3,2,1,0:T(8,128)S(1)}, f32[96,128]{1,0:T(8...) custom-call(f32[3,96,768]{2,1,0:T(8,128)S(1)} %get-tuple-element.37., ...), custom_call_target="tpu_custom_call", output_to_operand_aliasing={{3}: (3, {}), {4}: (4, {}), {5}: (5, {}), {6}: (6, {})} | custom-call | flops 4000000000 | bytes 1048576 | tf_op jit(solution)/shard_map/pallas_call | solution.py:468
  3.9 0.3 collective-permute-start
  4.2 4.7 %collective-permute-start.1 = (f32[96,128]{1,0:T(8,128)S(1)}, f32[96,128]{1,0:T(8,128)S(1)}, u32[]{:S(2)}, u32[]{:S(2)}) collective-permute-start(f32[96,128]{1,0:T(8,128)S(1)} %get-tuple-element.45), channel_id=1, source_target_pairs={{1,2},{2,1},{3,4},{4,3},{5,6},{6,5},{7,8},{8,7},{9,10},{10,9},{11,... | collective-permute-start | bytes 147464 | tf_op jit(solution)/shard_map/ppermute | solution.py:506
  8.9 1.2 %collective-permute-start.4 = (f32[8,6912]{1,0:T(8,128)S(1)}, f32[8,6912]{1,0:T(8,128)S(1)}, u32[]{:S(2)}, u32[]{:S(2)}) collective-permute-start(f32[8,6912]{1,0:T(8,128)S(1)} %get-tuple-element.53), channel_id=1, source_target_pairs={{0,16},{16,0},{32,48},{48,32},{64,80},{80,64},{96,112},{112,96},{1... | collective-permute-start | bytes 663560 | tf_op jit(solution)/shard_map/ppermute | solution.py:508
  10.2 3.0 %collective-permute-start.5 = (f32[8,6912]{1,0:T(8,128)S(1)}, f32[8,6912]{1,0:T(8,128)S(1)}, u32[]{:S(2)}, u32[]{:S(2)}) collective-permute-start(f32[8,6912]{1,0:T(8,128)S(1)} %get-tuple-element.54), channel_id=1, source_target_pairs={{16,32},{32,16},{48,64},{64,48},{80,96},{96,80},{17,33},{33,17},{4... | collective-permute-start | bytes 663560 | tf_op jit(solution)/shard_map/ppermute | solution.py:507
  13.2 0.0 copy-start
  13.2 0.0 copy-start.1
  13.2 0.6 %copy-done = f32[96]{0:T(128)S(1)} copy-done((f32[96]{0:T(128)S(1)}, f32[96]{0:T(128)}, u32[]{:S(2)}) %copy-start) | copy-done | bytes 408
  13.8 0.0 copy-done.1
  13.9 1.5 %shard_map.50 = (f32[2,96,128]{2,1,0:T(8,128)S(1)}, f32[2,21,16,256]{3,2,1,0:T(8,128)S(1)}, bf16[96,256]{1,0:T(8,128)(2,1)S(1)}, f32[96,128]{1,0:T(8,128)S(1)}, ...) custom-call(f32[1,96]{1,0:T(1,128)S(1)} %bitcast.3, s32[2,96]{1,0:T(2,128)S(1)} %copy-done.1, ...), custom_call_target="tpu_custom_call" | custom-call | flops 4000000000 | bytes 1048576 | tf_op jit(solution)/shard_map/pallas_call | solution.py:468
  15.4 0.0 collective-permute-done.znear
  15.4 0.0 collective-permute-done.1.zfar
  15.4 0.1 shard_map.48
  15.5 0.0 collective-permute-start.2
  15.5 3.5 %collective-permute-start.3 = (f32[8,256]{1,0:T(8,128)S(1)}, f32[8,256]{1,0:T(8,128)S(1)}, u32[]{:S(2)}, u32[]{:S(2)}) collective-permute-start(f32[8,256]{1,0:T(8,128)S(1)} %get-tuple-element.47), channel_id=1, source_target_pairs={{16,32},{32,16},{48,64},{64,48},{80,96},{96,80},{17,33},{33,17},{4... | collective-permute-start | bytes 24584 | tf_op jit(solution)/shard_map/ppermute | solution.py:540
  19.0 0.0 collective-permute-done.4.ynear
  19.0 0.0 collective-permute-done.5.yfar
  19.0 2.4 %shard_map.51 = (f32[2,128]{1,0:T(2,128)S(1)}, f32[21,16,256]{2,1,0:T(8,128)S(1)}, bf16[21,16,768]{2,1,0:T(8,128)(2,1)S(1)}, bf16[15,16,768]{2,1,0:T(8,128)(2,1)S(1)}, f32[2,21,16,256]{3,2,1,0:T(8,128)S(1)}) custom-call(bf16[21,96,768]{2,1,0:T(8,128)(2,1)S(1)} %get-tuple-element.51.fh, bf16[15,96,768]{2,1,0:T(8,128)(2,1)S(1)} %get-tuple-element.52.fl, ...), custom_call_target="tpu_custom_call" | custom-call | flops 4000000000 | bytes 1048576 | tf_op jit(solution)/shard_map/pallas_call | solution.py:468
  21.4 0.0 collective-permute-done.2.near_ref
  21.4 0.0 collective-permute-done.3.far_ref
  21.4 1.0 %shard_map.52 = f32[16,2,96]{2,1,0:T(2,128)S(1)} custom-call(f32[8,256]{1,0:T(8,128)S(1)} %collective-permute-done.2.near_ref, f32[8,256]{1,0:T(8,128)S(1)} %collective-permute-done.3.far_ref, f32[2,128]{1,0:T(2,128)S(1)} %get-tuple-element.61.sums_in, f32[2,21,16,256]{3,2,1,0:T(8,128)S(1)} %get-tuple-element.62.part_inner, ...), custom_call_target="tpu_custom_call" | custom-call | flops 4000000000 | bytes 1048576 | tf_op jit(solution)/shard_map/pallas_call | solution.py:468
  22.4 10.6 %all_to_all.5 = f32[16,2,96]{2,1,0:T(2,128)S(1)} all-to-all(f32[16,2,96]{2,1,0:T(2,128)S(1)} %shard_map.52), channel_id=1, replica_groups=mesh['gy'=8,'gz'=16] {'gz'}, dimensions={0} | all-to-all | bytes 24576 | tf_op jit(solution)/shard_map/all_to_all | solution.py:592
  33.1 0.5 %fusion = f32[96]{0:T(128)} fusion(f32[2,96]{1,0:T(2,128)S(1)} %reduce_sum.9), kind=kLoop, calls=%fused_computation.1 | loop fusion | flops 384 | bytes 1152 | tf_op jit(solution)/shard_map/div | solution.py:594
  (2 shorter events, 0.0 us)
Async XLA Ops:
  3.9 11.5 %collective-permute-start = (f32[96,128]{1,0:T(8,128)S(1)}, f32[96,128]{1,0:T(8,128)S(1)}, u32[]{:S(2)}, u32[]{:S(2)}) collective-permute-start(f32[96,128]{1,0:T(8,128)S(1)} %get-tuple-element.44), channel_id=1, source_target_pairs={{0,1},{1,0},{2,3},{3,2},{4,5},{5,4},{6,7},{7,6},{8,9},{9,8},{10,11... | collective-permute-start | bytes 147464 | tf_op jit(solution)/shard_map/ppermute | solution.py:505
  4.2 11.2 %collective-permute-start.1 = (f32[96,128]{1,0:T(8,128)S(1)}, f32[96,128]{1,0:T(8,128)S(1)}, u32[]{:S(2)}, u32[]{:S(2)}) collective-permute-start(f32[96,128]{1,0:T(8,128)S(1)} %get-tuple-element.45), channel_id=1, source_target_pairs={{1,2},{2,1},{3,4},{4,3},{5,6},{6,5},{7,8},{8,7},{9,10},{10,9},{11,... | collective-permute-start | bytes 147464 | tf_op jit(solution)/shard_map/ppermute | solution.py:506
  8.9 10.1 %collective-permute-start.4 = (f32[8,6912]{1,0:T(8,128)S(1)}, f32[8,6912]{1,0:T(8,128)S(1)}, u32[]{:S(2)}, u32[]{:S(2)}) collective-permute-start(f32[8,6912]{1,0:T(8,128)S(1)} %get-tuple-element.53), channel_id=1, source_target_pairs={{0,16},{16,0},{32,48},{48,32},{64,80},{80,64},{96,112},{112,96},{1... | collective-permute-start | bytes 663560 | tf_op jit(solution)/shard_map/ppermute | solution.py:508
  10.2 8.9 %collective-permute-start.5 = (f32[8,6912]{1,0:T(8,128)S(1)}, f32[8,6912]{1,0:T(8,128)S(1)}, u32[]{:S(2)}, u32[]{:S(2)}) collective-permute-start(f32[8,6912]{1,0:T(8,128)S(1)} %get-tuple-element.54), channel_id=1, source_target_pairs={{16,32},{32,16},{48,64},{64,48},{80,96},{96,80},{17,33},{33,17},{4... | collective-permute-start | bytes 663560 | tf_op jit(solution)/shard_map/ppermute | solution.py:507
  13.2 0.7 %copy-start = (f32[96]{0:T(128)S(1)}, f32[96]{0:T(128)}, u32[]{:S(2)}) copy-start(f32[96]{0:T(128)} %param.6) | copy-start | bytes 1156
  13.2 0.7 %copy-start.1 = (s32[2,96]{1,0:T(2,128)S(1)}, s32[2,96]{1,0:T(2,128)}, u32[]{:S(2)}) copy-start(s32[2,96]{1,0:T(2,128)} %reach_ref.1) | copy-start | bytes 2308
  15.5 5.9 %collective-permute-start.2 = (f32[8,256]{1,0:T(8,128)S(1)}, f32[8,256]{1,0:T(8,128)S(1)}, u32[]{:S(2)}, u32[]{:S(2)}) collective-permute-start(f32[8,256]{1,0:T(8,128)S(1)} %get-tuple-element.46), channel_id=1, source_target_pairs={{0,16},{16,0},{32,48},{48,32},{64,80},{80,64},{96,112},{112,96},{1... | collective-permute-start | bytes 24584 | tf_op jit(solution)/shard_map/ppermute | solution.py:541
  15.5 5.9 %collective-permute-start.3 = (f32[8,256]{1,0:T(8,128)S(1)}, f32[8,256]{1,0:T(8,128)S(1)}, u32[]{:S(2)}, u32[]{:S(2)}) collective-permute-start(f32[8,256]{1,0:T(8,128)S(1)} %get-tuple-element.47), channel_id=1, source_target_pairs={{16,32},{32,16},{48,64},{64,48},{80,96},{96,80},{17,33},{33,17},{4... | collective-permute-start | bytes 24584 | tf_op jit(solution)/shard_map/ppermute | solution.py:540

commit v10 on v9

--- a/solution.py
+++ b/solution.py
@@ -124,7 +124,7 @@
     )(velocity, strain)
 
 
-def corner_kernel(h_ref, znear, zfar, near_ref, far_ref):
+def corner_kernel(h_ref, zfar, znear, near_ref, far_ref):
     rows = znear.shape[0]
     gz_odd = lax.axis_index("gz") % 2 == 1
     gy_odd = lax.axis_index("gy") % 2 == 1
@@ -145,7 +145,7 @@
     far_ref[:, LANES:] = jnp.where(gy_odd, high_right, low_right)
 
 
-def corner_call(heights, znear, zfar):
+def corner_call(heights, zfar, znear):
     vmem = pl.BlockSpec(memory_space=pltpu.VMEM)
     return pl.pallas_call(
         corner_kernel,
@@ -153,7 +153,7 @@
         out_specs=[vmem] * 2,
         out_shape=[jax.ShapeDtypeStruct((HMAX, 2 * LANES), F32)] * 2,
         compiler_params=pltpu.CompilerParams(vmem_limit_bytes=SMALL_VMEM),
-    )(heights, znear, zfar)
+    )(heights, zfar, znear)
 
 
 def split2(x):
@@ -347,7 +347,7 @@
 
 
 def outer_kernel(
-    fh, fl, znear, zfar, ynear, yfar, pair_ref, ends_ref, acc_in, own_ref, height_ref, inv_ref,
+    fh, fl, zfar, znear, ynear, yfar, pair_ref, ends_ref, acc_in, own_ref, height_ref, inv_ref,
     sums_ref, part_ref, hh, hl, halo_inner, eh, el, stack, acc_ref,
 ):
     rows, cells = fh.shape[1:]
@@ -536,7 +536,7 @@
         stencil_reach,
         inner,
     )
-    near, far = corner_call(heights, znear, zfar)
+    near, far = corner_call(heights, zfar, znear)
     corner_far = lax.ppermute(far, "gy", far_pairs("gy", False))
     corner_near = lax.ppermute(near, "gy", near_pairs("gy"))
     sums, part_ends, hh, hl, halo_inner = call(
@@ -557,8 +557,8 @@
         LARGE_VMEM,
         fh,
         fl,
+        zfar,
         znear,
-        zfar,
         ynear,
         yfar,
         pair,

time: 33.8 us -> 34.3 us (1.015)
  blocking collectives: 10.6 us -> 11.5 us
    all_to_all x1, blocking collectives: 10.6 us -> 11.5 us  [local(): sums = jnp.sum(lax.all_to_all(sums, 'gz', 0, 0), axis=0)]
where the time goes in v10:
time: 34.3 us; the launch traced here: 34.1 us
  starting transfers between devices  12.4 us (36%)
  blocking collectives  11.5 us (34%)
  Pallas kernels  8.89 us (26%)
  local copies, waits for them, and re-layouts  0.66 us (2%)
  other arithmetic  0.55 us (2%)
    all_to_all x1, blocking collectives, local(): sums = jnp.sum(lax.all_to_all(sums, 'gz', 0, 0), axis=0)  11.5 us
    pallas_call x5, Pallas kernels, call(): pl.pallas_call(kernel, in_specs=[vmem] * len(operands), out_specs=jax.tre...  7.17 us
    ppermute x1, starting transfers between devices, local(): zfar = lax.ppermute(far, 'gz', far_pairs('gz', True))  4.87 us
    ppermute x1, starting transfers between devices, local(): corner_far = lax.ppermute(far, 'gy', far_pairs('gy', False))  3.49 us
    ppermute x1, starting transfers between devices, local(): yfar = lax.ppermute(wall_far, 'gy', far_pairs('gy', False))  3 us
    pallas_call x1, Pallas kernels, first_call(): pl.pallas_call(first_kernel, in_specs=[hbm] * 2, out_specs=[vmem] * 8, ou...  1.64 us
    ppermute x1, starting transfers between devices, local(): ynear = lax.ppermute(wall_near, 'gy', near_pairs('gy'))  0.96 us
  transfers between devices with their start and end apart: 6, of which 0 were waited for; matrix products, arithmetic and copies ran while one was open for 0% of the time, Pallas kernels for 12%

profile of v10, /device:TPU:1, one launch (start us, length us, event | category | flops | bytes accessed | tf_op | source)
XLA Modules:
  0.0 34.1 jit_solution(17231321845142336168)
XLA Ops:
  0.0 1.6 %shard_map.46 = (f32[96,128]{1,0:T(8,128)S(1)}, f32[96,128]{1,0:T(8,128)S(1)}, f32[8,6912]{1,0:T(8,128)S(1)}, f32[8,6912]{1,0:T(8,128)S(1)}, f32[3,96,768]{2,1,0...) custom-call(f32[3,96,768]{2,1,0:T(8,128)} %v_ref.1, ...), custom_call_target="tpu_custom_call" | custom-call | tf_op jit(solution)/shard_map/pallas_call | solution.py:114
  1.7 2.3 %shard_map.47 = (bf16[21,96,768]{2,1,0:T(8,128)(2,1)S(1)}, bf16[15,96,768]{2,1,0:T(8,128)(2,1)S(1)}, f32[2,21,96,256]{3,2,1,0:T(8,128)S(1)}, f32[96,128]{1,0:T(8...) custom-call(f32[3,96,768]{2,1,0:T(8,128)S(1)} %get-tuple-element.37., ...), custom_call_target="tpu_custom_call", output_to_operand_aliasing={{3}: (3, {}), {4}: (4, {}), {5}: (5, {}), {6}: (6, {})} | custom-call | flops 4000000000 | bytes 1048576 | tf_op jit(solution)/shard_map/pallas_call | solution.py:468
  3.9 4.9 %collective-permute-start = (f32[96,128]{1,0:T(8,128)S(1)}, f32[96,128]{1,0:T(8,128)S(1)}, u32[]{:S(2)}, u32[]{:S(2)}) collective-permute-start(f32[96,128]{1,0:T(8,128)S(1)} %get-tuple-element.44), channel_id=1, source_target_pairs={{1,2},{2,1},{3,4},{4,3},{5,6},{6,5},{7,8},{8,7},{9,10},{10,9},{11,... | collective-permute-start | bytes 147464 | tf_op jit(solution)/shard_map/ppermute | solution.py:506
  8.8 0.0 collective-permute-start.1
  8.8 1.0 %collective-permute-start.4 = (f32[8,6912]{1,0:T(8,128)S(1)}, f32[8,6912]{1,0:T(8,128)S(1)}, u32[]{:S(2)}, u32[]{:S(2)}) collective-permute-start(f32[8,6912]{1,0:T(8,128)S(1)} %get-tuple-element.53), channel_id=1, source_target_pairs={{0,16},{16,0},{32,48},{48,32},{64,80},{80,64},{96,112},{112,96},{1... | collective-permute-start | bytes 663560 | tf_op jit(solution)/shard_map/ppermute | solution.py:508
  9.8 3.0 %collective-permute-start.5 = (f32[8,6912]{1,0:T(8,128)S(1)}, f32[8,6912]{1,0:T(8,128)S(1)}, u32[]{:S(2)}, u32[]{:S(2)}) collective-permute-start(f32[8,6912]{1,0:T(8,128)S(1)} %get-tuple-element.54), channel_id=1, source_target_pairs={{16,32},{32,16},{48,64},{64,48},{80,96},{96,80},{17,33},{33,17},{4... | collective-permute-start | bytes 663560 | tf_op jit(solution)/shard_map/ppermute | solution.py:507
  12.8 0.0 copy-start
  12.8 0.0 copy-start.1
  12.8 0.6 %copy-done = f32[96]{0:T(128)S(1)} copy-done((f32[96]{0:T(128)S(1)}, f32[96]{0:T(128)}, u32[]{:S(2)}) %copy-start) | copy-done | bytes 408
  13.4 0.0 copy-done.1
  13.5 1.5 %shard_map.50 = (f32[2,96,128]{2,1,0:T(8,128)S(1)}, f32[2,21,16,256]{3,2,1,0:T(8,128)S(1)}, bf16[96,256]{1,0:T(8,128)(2,1)S(1)}, f32[96,128]{1,0:T(8,128)S(1)}, ...) custom-call(f32[1,96]{1,0:T(1,128)S(1)} %bitcast.3, s32[2,96]{1,0:T(2,128)S(1)} %copy-done.1, ...), custom_call_target="tpu_custom_call" | custom-call | flops 4000000000 | bytes 1048576 | tf_op jit(solution)/shard_map/pallas_call | solution.py:468
  15.0 0.0 collective-permute-done.zfar
  15.0 0.0 collective-permute-done.1.znear
  15.0 0.1 shard_map.48
  15.1 0.0 collective-permute-start.2
  15.1 3.5 %collective-permute-start.3 = (f32[8,256]{1,0:T(8,128)S(1)}, f32[8,256]{1,0:T(8,128)S(1)}, u32[]{:S(2)}, u32[]{:S(2)}) collective-permute-start(f32[8,256]{1,0:T(8,128)S(1)} %get-tuple-element.47), channel_id=1, source_target_pairs={{16,32},{32,16},{48,64},{64,48},{80,96},{96,80},{17,33},{33,17},{4... | collective-permute-start | bytes 24584 | tf_op jit(solution)/shard_map/ppermute | solution.py:540
  18.6 0.0 collective-permute-done.4.ynear
  18.6 0.0 collective-permute-done.5.yfar
  18.6 2.4 %shard_map.51 = (f32[2,128]{1,0:T(2,128)S(1)}, f32[21,16,256]{2,1,0:T(8,128)S(1)}, bf16[21,16,768]{2,1,0:T(8,128)(2,1)S(1)}, bf16[15,16,768]{2,1,0:T(8,128)(2,1)S(1)}, f32[2,21,16,256]{3,2,1,0:T(8,128)S(1)}) custom-call(bf16[21,96,768]{2,1,0:T(8,128)(2,1)S(1)} %get-tuple-element.51.fh, bf16[15,96,768]{2,1,0:T(8,128)(2,1)S(1)} %get-tuple-element.52.fl, ...), custom_call_target="tpu_custom_call" | custom-call | flops 4000000000 | bytes 1048576 | tf_op jit(solution)/shard_map/pallas_call | solution.py:468
  21.0 0.0 collective-permute-done.2.near_ref
  21.0 0.0 collective-permute-done.3.far_ref
  21.0 1.0 %shard_map.52 = f32[16,2,96]{2,1,0:T(2,128)S(1)} custom-call(f32[8,256]{1,0:T(8,128)S(1)} %collective-permute-done.2.near_ref, f32[8,256]{1,0:T(8,128)S(1)} %collective-permute-done.3.far_ref, f32[2,128]{1,0:T(2,128)S(1)} %get-tuple-element.61.sums_in, f32[2,21,16,256]{3,2,1,0:T(8,128)S(1)} %get-tuple-element.62.part_inner, ...), custom_call_target="tpu_custom_call" | custom-call | flops 4000000000 | bytes 1048576 | tf_op jit(solution)/shard_map/pallas_call | solution.py:468
  22.1 11.5 %all_to_all.5 = f32[16,2,96]{2,1,0:T(2,128)S(1)} all-to-all(f32[16,2,96]{2,1,0:T(2,128)S(1)} %shard_map.52), channel_id=1, replica_groups=mesh['gy'=8,'gz'=16] {'gz'}, dimensions={0} | all-to-all | bytes 24576 | tf_op jit(solution)/shard_map/all_to_all | solution.py:592
  33.6 0.5 %fusion = f32[96]{0:T(128)} fusion(f32[2,96]{1,0:T(2,128)S(1)} %reduce_sum.9), kind=kLoop, calls=%fused_computation.1 | loop fusion | flops 384 | bytes 1152 | tf_op jit(solution)/shard_map/div | solution.py:594
  (2 shorter events, 0.0 us)
Async XLA Ops:
  3.9 11.1 %collective-permute-start = (f32[96,128]{1,0:T(8,128)S(1)}, f32[96,128]{1,0:T(8,128)S(1)}, u32[]{:S(2)}, u32[]{:S(2)}) collective-permute-start(f32[96,128]{1,0:T(8,128)S(1)} %get-tuple-element.44), channel_id=1, source_target_pairs={{1,2},{2,1},{3,4},{4,3},{5,6},{6,5},{7,8},{8,7},{9,10},{10,9},{11,... | collective-permute-start | bytes 147464 | tf_op jit(solution)/shard_map/ppermute | solution.py:506
  8.8 6.2 %collective-permute-start.1 = (f32[96,128]{1,0:T(8,128)S(1)}, f32[96,128]{1,0:T(8,128)S(1)}, u32[]{:S(2)}, u32[]{:S(2)}) collective-permute-start(f32[96,128]{1,0:T(8,128)S(1)} %get-tuple-element.45), channel_id=1, source_target_pairs={{0,1},{1,0},{2,3},{3,2},{4,5},{5,4},{6,7},{7,6},{8,9},{9,8},{10,11... | collective-permute-start | bytes 147464 | tf_op jit(solution)/shard_map/ppermute | solution.py:505
  8.8 9.8 %collective-permute-start.4 = (f32[8,6912]{1,0:T(8,128)S(1)}, f32[8,6912]{1,0:T(8,128)S(1)}, u32[]{:S(2)}, u32[]{:S(2)}) collective-permute-start(f32[8,6912]{1,0:T(8,128)S(1)} %get-tuple-element.53), channel_id=1, source_target_pairs={{0,16},{16,0},{32,48},{48,32},{64,80},{80,64},{96,112},{112,96},{1... | collective-permute-start | bytes 663560 | tf_op jit(solution)/shard_map/ppermute | solution.py:508
  9.8 8.9 %collective-permute-start.5 = (f32[8,6912]{1,0:T(8,128)S(1)}, f32[8,6912]{1,0:T(8,128)S(1)}, u32[]{:S(2)}, u32[]{:S(2)}) collective-permute-start(f32[8,6912]{1,0:T(8,128)S(1)} %get-tuple-element.54), channel_id=1, source_target_pairs={{16,32},{32,16},{48,64},{64,48},{80,96},{96,80},{17,33},{33,17},{4... | collective-permute-start | bytes 663560 | tf_op jit(solution)/shard_map/ppermute | solution.py:507
  12.8 0.7 %copy-start = (f32[96]{0:T(128)S(1)}, f32[96]{0:T(128)}, u32[]{:S(2)}) copy-start(f32[96]{0:T(128)} %param.6) | copy-start | bytes 1156
  12.8 0.7 %copy-start.1 = (s32[2,96]{1,0:T(2,128)S(1)}, s32[2,96]{1,0:T(2,128)}, u32[]{:S(2)}) copy-start(s32[2,96]{1,0:T(2,128)} %reach_ref.1) | copy-start | bytes 2308
  15.1 5.9 %collective-permute-start.2 = (f32[8,256]{1,0:T(8,128)S(1)}, f32[8,256]{1,0:T(8,128)S(1)}, u32[]{:S(2)}, u32[]{:S(2)}) collective-permute-start(f32[8,256]{1,0:T(8,128)S(1)} %get-tuple-element.46), channel_id=1, source_target_pairs={{0,16},{16,0},{32,48},{48,32},{64,80},{80,64},{96,112},{112,96},{1... | collective-permute-start | bytes 24584 | tf_op jit(solution)/shard_map/ppermute | solution.py:541
  15.1 5.9 %collective-permute-start.3 = (f32[8,256]{1,0:T(8,128)S(1)}, f32[8,256]{1,0:T(8,128)S(1)}, u32[]{:S(2)}, u32[]{:S(2)}) collective-permute-start(f32[8,256]{1,0:T(8,128)S(1)} %get-tuple-element.47), channel_id=1, source_target_pairs={{16,32},{32,16},{48,64},{64,48},{80,96},{96,80},{17,33},{33,17},{4... | collective-permute-start | bytes 24584 | tf_op jit(solution)/shard_map/ppermute | solution.py:540

commit v11 on v9

--- a/solution.py
+++ b/solution.py
@@ -355,8 +355,7 @@
     gy_odd = lax.axis_index("gy") % 2 == 1
     acc_ref[...] = acc_in[...]
     edge_fields(jnp.where(gz_odd, znear[...], zfar[...]), jnp.where(gz_odd, zfar[...], znear[...]), eh, el)
-    g = smooth_ends(fh, fl, eh, el, ends_ref)
-    wall_block(g, own_ref, height_ref, inv_ref, stack, acc_ref, part_ref)
+    g_ends = smooth_ends(fh, fl, eh, el, ends_ref)
     for t in range(cells // LANES):
         at = slice(t * LANES, (t + 1) * LANES)
 
@@ -376,6 +375,7 @@
         g = smooth_pair(n, hh, hl, pair_ref)
         for f in range(FIELDS):
             halo_inner[n, f] = g[f]
+    wall_block(g_ends, own_ref, height_ref, inv_ref, stack, acc_ref, part_ref)
     inv = inv_ref[...]
     for k in range(2):
         plane_sums = jnp.sum(acc_ref[k] * (inv * inv), axis=1, keepdims=True)
@@ -434,13 +434,14 @@
     zero = jnp.zeros((HMAX, LANES), F32)
     sums = [[zero, zero], [zero, zero]]
     blocks = halo_inner.shape[0]
+    g_ends = smooth_ends(hh, hl, eh, el, ends_ref)
     for n in range(blocks + 1):
         if n < blocks:
             g = [halo_inner[n, f] for f in range(FIELDS)]
             part = part_inner.at[n]
         else:
             part = part_ends
-            g = smooth_ends(hh, hl, eh, el, ends_ref)
+            g = g_ends
         for f in range(FIELDS):
             hi, lo = split2(g[f] * height)
             stack[n, 0:both_rows, f * width : (f + 1) * width] = hi

time: 33.8 us -> 33.3 us (0.985)
  Pallas kernels: 8.89 us -> 8.38 us
    pallas_call x5, Pallas kernels: 7.18 us -> 6.66 us  [call(): pl.pallas_call(kernel, in_specs=[vmem] * len(operands), out_specs=jax.tre...]
  transfers between devices with their start and end apart: 6 -> 6, of which waited for: 0 -> 0; matrix products, arithmetic and copies ran while one was open for 0% -> 0% of each run, Pallas kernels for 12% -> 11%
where the time goes in v11:
time: 33.3 us; the launch traced here: 33.1 us
  starting transfers between devices  12.7 us (38%)
  blocking collectives  10.6 us (32%)
  Pallas kernels  8.38 us (25%)
  local copies, waits for them, and re-layouts  0.66 us (2%)
  other arithmetic  0.55 us (2%)
    all_to_all x1, blocking collectives, local(): sums = jnp.sum(lax.all_to_all(sums, 'gz', 0, 0), axis=0)  10.6 us
    pallas_call x5, Pallas kernels, call(): pl.pallas_call(kernel, in_specs=[vmem] * len(operands), out_specs=jax.tre...  6.66 us
    ppermute x1, starting transfers between devices, local(): zfar = lax.ppermute(far, 'gz', far_pairs('gz', True))  4.69 us
    ppermute x1, starting transfers between devices, local(): corner_far = lax.ppermute(far, 'gy', far_pairs('gy', False))  3.48 us
    ppermute x1, starting transfers between devices, local(): yfar = lax.ppermute(wall_far, 'gy', far_pairs('gy', False))  3 us
    pallas_call x1, Pallas kernels, first_call(): pl.pallas_call(first_kernel, in_specs=[hbm] * 2, out_specs=[vmem] * 8, ou...  1.64 us
    ppermute x1, starting transfers between devices, local(): ynear = lax.ppermute(wall_near, 'gy', near_pairs('gy'))  1.24 us
  transfers between devices with their start and end apart: 6, of which 0 were waited for; matrix products, arithmetic and copies ran while one was open for 0% of the time, Pallas kernels for 11%

profile of v11, /device:TPU:1, one launch (start us, length us, event | category | flops | bytes accessed | tf_op | source)
XLA Modules:
  0.0 33.1 jit_solution(13187428063322069093)
XLA Ops:
  0.0 1.6 %shard_map.46 = (f32[96,128]{1,0:T(8,128)S(1)}, f32[96,128]{1,0:T(8,128)S(1)}, f32[8,6912]{1,0:T(8,128)S(1)}, f32[8,6912]{1,0:T(8,128)S(1)}, f32[3,96,768]{2,1,0...) custom-call(f32[3,96,768]{2,1,0:T(8,128)} %v_ref.1, ...), custom_call_target="tpu_custom_call" | custom-call | tf_op jit(solution)/shard_map/pallas_call | solution.py:114
  1.7 2.3 %shard_map.47 = (bf16[21,96,768]{2,1,0:T(8,128)(2,1)S(1)}, bf16[15,96,768]{2,1,0:T(8,128)(2,1)S(1)}, f32[2,21,96,256]{3,2,1,0:T(8,128)S(1)}, f32[96,128]{1,0:T(8...) custom-call(f32[3,96,768]{2,1,0:T(8,128)S(1)} %get-tuple-element.37., ...), custom_call_target="tpu_custom_call", output_to_operand_aliasing={{3}: (3, {}), {4}: (4, {}), {5}: (5, {}), {6}: (6, {})} | custom-call | flops 4000000000 | bytes 1048576 | tf_op jit(solution)/shard_map/pallas_call | solution.py:469
  3.9 0.3 collective-permute-start
  4.2 4.7 %collective-permute-start.1 = (f32[96,128]{1,0:T(8,128)S(1)}, f32[96,128]{1,0:T(8,128)S(1)}, u32[]{:S(2)}, u32[]{:S(2)}) collective-permute-start(f32[96,128]{1,0:T(8,128)S(1)} %get-tuple-element.45), channel_id=1, source_target_pairs={{1,2},{2,1},{3,4},{4,3},{5,6},{6,5},{7,8},{8,7},{9,10},{10,9},{11,... | collective-permute-start | bytes 147464 | tf_op jit(solution)/shard_map/ppermute | solution.py:507
  8.9 1.2 %collective-permute-start.4 = (f32[8,6912]{1,0:T(8,128)S(1)}, f32[8,6912]{1,0:T(8,128)S(1)}, u32[]{:S(2)}, u32[]{:S(2)}) collective-permute-start(f32[8,6912]{1,0:T(8,128)S(1)} %get-tuple-element.53), channel_id=1, source_target_pairs={{0,16},{16,0},{32,48},{48,32},{64,80},{80,64},{96,112},{112,96},{1... | collective-permute-start | bytes 663560 | tf_op jit(solution)/shard_map/ppermute | solution.py:509
  10.2 3.0 %collective-permute-start.5 = (f32[8,6912]{1,0:T(8,128)S(1)}, f32[8,6912]{1,0:T(8,128)S(1)}, u32[]{:S(2)}, u32[]{:S(2)}) collective-permute-start(f32[8,6912]{1,0:T(8,128)S(1)} %get-tuple-element.54), channel_id=1, source_target_pairs={{16,32},{32,16},{48,64},{64,48},{80,96},{96,80},{17,33},{33,17},{4... | collective-permute-start | bytes 663560 | tf_op jit(solution)/shard_map/ppermute | solution.py:508
  13.2 0.0 copy-start
  13.2 0.0 copy-start.1
  13.2 0.6 %copy-done = f32[96]{0:T(128)S(1)} copy-done((f32[96]{0:T(128)S(1)}, f32[96]{0:T(128)}, u32[]{:S(2)}) %copy-start) | copy-done | bytes 408
  13.8 0.0 copy-done.1
  13.9 1.5 %shard_map.50 = (f32[2,96,128]{2,1,0:T(8,128)S(1)}, f32[2,21,16,256]{3,2,1,0:T(8,128)S(1)}, bf16[96,256]{1,0:T(8,128)(2,1)S(1)}, f32[96,128]{1,0:T(8,128)S(1)}, ...) custom-call(f32[1,96]{1,0:T(1,128)S(1)} %bitcast.3, s32[2,96]{1,0:T(2,128)S(1)} %copy-done.1, ...), custom_call_target="tpu_custom_call" | custom-call | flops 4000000000 | bytes 1048576 | tf_op jit(solution)/shard_map/pallas_call | solution.py:469
  15.4 0.0 collective-permute-done.znear
  15.4 0.0 collective-permute-done.1.zfar
  15.4 0.1 shard_map.48
  15.5 0.0 collective-permute-start.2
  15.5 3.5 %collective-permute-start.3 = (f32[8,256]{1,0:T(8,128)S(1)}, f32[8,256]{1,0:T(8,128)S(1)}, u32[]{:S(2)}, u32[]{:S(2)}) collective-permute-start(f32[8,256]{1,0:T(8,128)S(1)} %get-tuple-element.47), channel_id=1, source_target_pairs={{16,32},{32,16},{48,64},{64,48},{80,96},{96,80},{17,33},{33,17},{4... | collective-permute-start | bytes 24584 | tf_op jit(solution)/shard_map/ppermute | solution.py:541
  19.0 0.0 collective-permute-done.4.ynear
  19.0 0.0 collective-permute-done.5.yfar
  19.0 2.1 %shard_map.51 = (f32[2,128]{1,0:T(2,128)S(1)}, f32[21,16,256]{2,1,0:T(8,128)S(1)}, bf16[21,16,768]{2,1,0:T(8,128)(2,1)S(1)}, bf16[15,16,768]{2,1,0:T(8,128)(2,1)S(1)}, f32[2,21,16,256]{3,2,1,0:T(8,128)S(1)}) custom-call(bf16[21,96,768]{2,1,0:T(8,128)(2,1)S(1)} %get-tuple-element.51.fh, bf16[15,96,768]{2,1,0:T(8,128)(2,1)S(1)} %get-tuple-element.52.fl, ...), custom_call_target="tpu_custom_call" | custom-call | flops 4000000000 | bytes 1048576 | tf_op jit(solution)/shard_map/pallas_call | solution.py:469
  21.2 0.0 collective-permute-done.2.near_ref
  21.2 0.0 collective-permute-done.3.far_ref
  21.2 0.8 %shard_map.52 = f32[16,2,96]{2,1,0:T(2,128)S(1)} custom-call(f32[8,256]{1,0:T(8,128)S(1)} %collective-permute-done.2.near_ref, f32[8,256]{1,0:T(8,128)S(1)} %collective-permute-done.3.far_ref, f32[2,128]{1,0:T(2,128)S(1)} %get-tuple-element.61.sums_in, f32[2,21,16,256]{3,2,1,0:T(8,128)S(1)} %get-tuple-element.62.part_inner, ...), custom_call_target="tpu_custom_call" | custom-call | flops 4000000000 | bytes 1048576 | tf_op jit(solution)/shard_map/pallas_call | solution.py:469
  21.9 10.6 %all_to_all.5 = f32[16,2,96]{2,1,0:T(2,128)S(1)} all-to-all(f32[16,2,96]{2,1,0:T(2,128)S(1)} %shard_map.52), channel_id=1, replica_groups=mesh['gy'=8,'gz'=16] {'gz'}, dimensions={0} | all-to-all | bytes 24576 | tf_op jit(solution)/shard_map/all_to_all | solution.py:593
  32.5 0.5 %fusion = f32[96]{0:T(128)} fusion(f32[2,96]{1,0:T(2,128)S(1)} %reduce_sum.9), kind=kLoop, calls=%fused_computation.1 | loop fusion | flops 384 | bytes 1152 | tf_op jit(solution)/shard_map/div | solution.py:595
  (2 shorter events, 0.0 us)
Async XLA Ops:
  3.9 11.5 %collective-permute-start = (f32[96,128]{1,0:T(8,128)S(1)}, f32[96,128]{1,0:T(8,128)S(1)}, u32[]{:S(2)}, u32[]{:S(2)}) collective-permute-start(f32[96,128]{1,0:T(8,128)S(1)} %get-tuple-element.44), channel_id=1, source_target_pairs={{0,1},{1,0},{2,3},{3,2},{4,5},{5,4},{6,7},{7,6},{8,9},{9,8},{10,11... | collective-permute-start | bytes 147464 | tf_op jit(solution)/shard_map/ppermute | solution.py:506
  4.2 11.2 %collective-permute-start.1 = (f32[96,128]{1,0:T(8,128)S(1)}, f32[96,128]{1,0:T(8,128)S(1)}, u32[]{:S(2)}, u32[]{:S(2)}) collective-permute-start(f32[96,128]{1,0:T(8,128)S(1)} %get-tuple-element.45), channel_id=1, source_target_pairs={{1,2},{2,1},{3,4},{4,3},{5,6},{6,5},{7,8},{8,7},{9,10},{10,9},{11,... | collective-permute-start | bytes 147464 | tf_op jit(solution)/shard_map/ppermute | solution.py:507
  8.9 10.1 %collective-permute-start.4 = (f32[8,6912]{1,0:T(8,128)S(1)}, f32[8,6912]{1,0:T(8,128)S(1)}, u32[]{:S(2)}, u32[]{:S(2)}) collective-permute-start(f32[8,6912]{1,0:T(8,128)S(1)} %get-tuple-element.53), channel_id=1, source_target_pairs={{0,16},{16,0},{32,48},{48,32},{64,80},{80,64},{96,112},{112,96},{1... | collective-permute-start | bytes 663560 | tf_op jit(solution)/shard_map/ppermute | solution.py:509
  10.2 8.9 %collective-permute-start.5 = (f32[8,6912]{1,0:T(8,128)S(1)}, f32[8,6912]{1,0:T(8,128)S(1)}, u32[]{:S(2)}, u32[]{:S(2)}) collective-permute-start(f32[8,6912]{1,0:T(8,128)S(1)} %get-tuple-element.54), channel_id=1, source_target_pairs={{16,32},{32,16},{48,64},{64,48},{80,96},{96,80},{17,33},{33,17},{4... | collective-permute-start | bytes 663560 | tf_op jit(solution)/shard_map/ppermute | solution.py:508
  13.2 0.7 %copy-start = (f32[96]{0:T(128)S(1)}, f32[96]{0:T(128)}, u32[]{:S(2)}) copy-start(f32[96]{0:T(128)} %param.6) | copy-start | bytes 1156
  13.2 0.7 %copy-start.1 = (s32[2,96]{1,0:T(2,128)S(1)}, s32[2,96]{1,0:T(2,128)}, u32[]{:S(2)}) copy-start(s32[2,96]{1,0:T(2,128)} %reach_ref.1) | copy-start | bytes 2308
  15.5 5.7 %collective-permute-start.2 = (f32[8,256]{1,0:T(8,128)S(1)}, f32[8,256]{1,0:T(8,128)S(1)}, u32[]{:S(2)}, u32[]{:S(2)}) collective-permute-start(f32[8,256]{1,0:T(8,128)S(1)} %get-tuple-element.46), channel_id=1, source_target_pairs={{0,16},{16,0},{32,48},{48,32},{64,80},{80,64},{96,112},{112,96},{1... | collective-permute-start | bytes 24584 | tf_op jit(solution)/shard_map/ppermute | solution.py:542
  15.5 5.7 %collective-permute-start.3 = (f32[8,256]{1,0:T(8,128)S(1)}, f32[8,256]{1,0:T(8,128)S(1)}, u32[]{:S(2)}, u32[]{:S(2)}) collective-permute-start(f32[8,256]{1,0:T(8,128)S(1)} %get-tuple-element.47), channel_id=1, source_target_pairs={{16,32},{32,16},{48,64},{64,48},{80,96},{96,80},{17,33},{33,17},{4... | collective-permute-start | bytes 24584 | tf_op jit(solution)/shard_map/ppermute | solution.py:541

commit v12 on v11

--- a/solution.py
+++ b/solution.py
@@ -347,7 +347,7 @@
 
 
 def outer_kernel(
-    fh, fl, znear, zfar, ynear, yfar, pair_ref, ends_ref, acc_in, own_ref, height_ref, inv_ref,
+    fh, fl, znear, zfar, yfar, ynear, pair_ref, ends_ref, acc_in, own_ref, height_ref, inv_ref,
     sums_ref, part_ref, hh, hl, halo_inner, eh, el, stack, acc_ref,
 ):
     rows, cells = fh.shape[1:]
@@ -408,7 +408,7 @@
         store_fields(raw[:3], raw[3:], put_high, put_low)
 
 
-def last_kernel(near_ref, far_ref, sums_in, part_inner, part_ends, mask_ref, total_ref, hh, hl, halo_inner, ends_ref, out_ref, eh, el, stack):
+def last_kernel(far_ref, near_ref, sums_in, part_inner, part_ends, mask_ref, total_ref, hh, hl, halo_inner, ends_ref, out_ref, eh, el, stack):
     rows = out_ref.shape[2]
     width = 2 * LANES
     gy_odd = lax.axis_index("gy") % 2 == 1
@@ -560,8 +560,8 @@
         fl,
         znear,
         zfar,
+        yfar,
         ynear,
-        yfar,
         pair,
         both_ends,
         acc,
@@ -578,8 +578,8 @@
             pltpu.VMEM((blocks + 1, 2 * ends, FIELDS * width), BF16),
         ],
         LARGE_VMEM,
+        corner_far,
         corner_near,
-        corner_far,
         sums,
         part_inner,
         part_ends,

time: 33.3 us -> 33.9 us (1.018)
  the two profiles are of different devices: /device:TPU:1 before, /device:TPU:0 now
where the time goes in v12:
time: 33.9 us; the launch traced here: 33.7 us
  starting transfers between devices  12 us (35%)
  blocking collectives  12 us (35%)
  Pallas kernels  8.35 us (25%)
  local copies, waits for them, and re-layouts  0.69 us (2%)
  other arithmetic  0.55 us (2%)
    all_to_all x1, blocking collectives, local(): sums = jnp.sum(lax.all_to_all(sums, 'gz', 0, 0), axis=0)  12 us
    pallas_call x5, Pallas kernels, call(): pl.pallas_call(kernel, in_specs=[vmem] * len(operands), out_specs=jax.tre...  6.64 us
    ppermute x1, starting transfers between devices, local(): zfar = lax.ppermute(far, 'gz', far_pairs('gz', True))  4.71 us
    ppermute x1, starting transfers between devices, local(): corner_near = lax.ppermute(near, 'gy', near_pairs('gy'))  2.94 us
    ppermute x1, starting transfers between devices, local(): ynear = lax.ppermute(wall_near, 'gy', near_pairs('gy'))  2.92 us
    pallas_call x1, Pallas kernels, first_call(): pl.pallas_call(first_kernel, in_specs=[hbm] * 2, out_specs=[vmem] * 8, ou...  1.64 us
    unnamed x4, local copies, waits for them, and re-layouts  0.69 us
  transfers between devices with their start and end apart: 6, of which 0 were waited for; matrix products, arithmetic and copies ran while one was open for 0% of the time, Pallas kernels for 11%

profile of v12, /device:TPU:0, one launch (start us, length us, event | category | flops | bytes accessed | tf_op | source)
XLA Modules:
  0.0 33.7 jit_solution(6913766766182083958)
XLA Ops:
  0.0 1.6 %shard_map.46 = (f32[96,128]{1,0:T(8,128)S(1)}, f32[96,128]{1,0:T(8,128)S(1)}, f32[8,6912]{1,0:T(8,128)S(1)}, f32[8,6912]{1,0:T(8,128)S(1)}, f32[3,96,768]{2,1,0...) custom-call(f32[3,96,768]{2,1,0:T(8,128)} %v_ref.1, ...), custom_call_target="tpu_custom_call" | custom-call | tf_op jit(solution)/shard_map/pallas_call | solution.py:114
  1.7 2.3 %shard_map.47 = (bf16[21,96,768]{2,1,0:T(8,128)(2,1)S(1)}, bf16[15,96,768]{2,1,0:T(8,128)(2,1)S(1)}, f32[2,21,96,256]{3,2,1,0:T(8,128)S(1)}, f32[96,128]{1,0:T(8...) custom-call(f32[3,96,768]{2,1,0:T(8,128)S(1)} %get-tuple-element.37., ...), custom_call_target="tpu_custom_call", output_to_operand_aliasing={{3}: (3, {}), {4}: (4, {}), {5}: (5, {}), {6}: (6, {})} | custom-call | flops 4000000000 | bytes 1048576 | tf_op jit(solution)/shard_map/pallas_call | solution.py:469
  3.9 0.1 collective-permute-start
  4.0 4.7 %collective-permute-start.1 = (f32[96,128]{1,0:T(8,128)S(1)}, f32[96,128]{1,0:T(8,128)S(1)}, u32[]{:S(2)}, u32[]{:S(2)}) collective-permute-start(f32[96,128]{1,0:T(8,128)S(1)} %get-tuple-element.45), channel_id=1, source_target_pairs={{1,2},{2,1},{3,4},{4,3},{5,6},{6,5},{7,8},{8,7},{9,10},{10,9},{11,... | collective-permute-start | bytes 147464 | tf_op jit(solution)/shard_map/ppermute | solution.py:507
  8.7 0.7 %collective-permute-start.4 = (f32[8,6912]{1,0:T(8,128)S(1)}, f32[8,6912]{1,0:T(8,128)S(1)}, u32[]{:S(2)}, u32[]{:S(2)}) collective-permute-start(f32[8,6912]{1,0:T(8,128)S(1)} %get-tuple-element.53), channel_id=1, source_target_pairs={{16,32},{32,16},{48,64},{64,48},{80,96},{96,80},{17,33},{33,17},{4... | collective-permute-start | bytes 663560 | tf_op jit(solution)/shard_map/ppermute | solution.py:508
  9.4 2.9 %collective-permute-start.5 = (f32[8,6912]{1,0:T(8,128)S(1)}, f32[8,6912]{1,0:T(8,128)S(1)}, u32[]{:S(2)}, u32[]{:S(2)}) collective-permute-start(f32[8,6912]{1,0:T(8,128)S(1)} %get-tuple-element.54), channel_id=1, source_target_pairs={{0,16},{16,0},{32,48},{48,32},{64,80},{80,64},{96,112},{112,96},{1... | collective-permute-start | bytes 663560 | tf_op jit(solution)/shard_map/ppermute | solution.py:509
  12.3 0.0 copy-start
  12.3 0.0 copy-start.1
  12.3 0.7 %copy-done = f32[96]{0:T(128)S(1)} copy-done((f32[96]{0:T(128)S(1)}, f32[96]{0:T(128)}, u32[]{:S(2)}) %copy-start) | copy-done | bytes 408
  13.0 0.0 copy-done.1
  13.0 1.5 %shard_map.50 = (f32[2,96,128]{2,1,0:T(8,128)S(1)}, f32[2,21,16,256]{3,2,1,0:T(8,128)S(1)}, bf16[96,256]{1,0:T(8,128)(2,1)S(1)}, f32[96,128]{1,0:T(8,128)S(1)}, ...) custom-call(f32[1,96]{1,0:T(1,128)S(1)} %bitcast.3, s32[2,96]{1,0:T(2,128)S(1)} %copy-done.1, ...), custom_call_target="tpu_custom_call" | custom-call | flops 4000000000 | bytes 1048576 | tf_op jit(solution)/shard_map/pallas_call | solution.py:469
  14.5 0.0 collective-permute-done.znear
  14.5 0.0 collective-permute-done.1.zfar
  14.5 0.1 shard_map.48
  14.6 0.7 %collective-permute-start.2 = (f32[8,256]{1,0:T(8,128)S(1)}, f32[8,256]{1,0:T(8,128)S(1)}, u32[]{:S(2)}, u32[]{:S(2)}) collective-permute-start(f32[8,256]{1,0:T(8,128)S(1)} %get-tuple-element.46), channel_id=1, source_target_pairs={{16,32},{32,16},{48,64},{64,48},{80,96},{96,80},{17,33},{33,17},{4... | collective-permute-start | bytes 24584 | tf_op jit(solution)/shard_map/ppermute | solution.py:541
  15.3 2.9 %collective-permute-start.3 = (f32[8,256]{1,0:T(8,128)S(1)}, f32[8,256]{1,0:T(8,128)S(1)}, u32[]{:S(2)}, u32[]{:S(2)}) collective-permute-start(f32[8,256]{1,0:T(8,128)S(1)} %get-tuple-element.47), channel_id=1, source_target_pairs={{0,16},{16,0},{32,48},{48,32},{64,80},{80,64},{96,112},{112,96},{1... | collective-permute-start | bytes 24584 | tf_op jit(solution)/shard_map/ppermute | solution.py:542
  18.2 0.0 collective-permute-done.4.yfar
  18.2 0.0 collective-permute-done.5.ynear
  18.2 2.1 %shard_map.51 = (f32[2,128]{1,0:T(2,128)S(1)}, f32[21,16,256]{2,1,0:T(8,128)S(1)}, bf16[21,16,768]{2,1,0:T(8,128)(2,1)S(1)}, bf16[15,16,768]{2,1,0:T(8,128)(2,1)S(1)}, f32[2,21,16,256]{3,2,1,0:T(8,128)S(1)}) custom-call(bf16[21,96,768]{2,1,0:T(8,128)(2,1)S(1)} %get-tuple-element.51.fh, bf16[15,96,768]{2,1,0:T(8,128)(2,1)S(1)} %get-tuple-element.52.fl, ...), custom_call_target="tpu_custom_call" | custom-call | flops 4000000000 | bytes 1048576 | tf_op jit(solution)/shard_map/pallas_call | solution.py:469
  20.3 0.0 collective-permute-done.2.far_ref
  20.4 0.0 collective-permute-done.3.near_ref
  20.4 0.8 %shard_map.52 = f32[16,2,96]{2,1,0:T(2,128)S(1)} custom-call(f32[8,256]{1,0:T(8,128)S(1)} %collective-permute-done.2.far_ref, f32[8,256]{1,0:T(8,128)S(1)} %collective-permute-done.3.near_ref, f32[2,128]{1,0:T(2,128)S(1)} %get-tuple-element.61.sums_in, f32[2,21,16,256]{3,2,1,0:T(8,128)S(1)} %get-tuple-element.62.part_inner, ...), custom_call_target="tpu_custom_call" | custom-call | flops 4000000000 | bytes 1048576 | tf_op jit(solution)/shard_map/pallas_call | solution.py:469
  21.1 12.0 %all_to_all.5 = f32[16,2,96]{2,1,0:T(2,128)S(1)} all-to-all(f32[16,2,96]{2,1,0:T(2,128)S(1)} %shard_map.52), channel_id=1, replica_groups=mesh['gy'=8,'gz'=16] {'gz'}, dimensions={0} | all-to-all | bytes 24576 | tf_op jit(solution)/shard_map/all_to_all | solution.py:593
  33.1 0.5 %fusion = f32[96]{0:T(128)} fusion(f32[2,96]{1,0:T(2,128)S(1)} %reduce_sum.9), kind=kLoop, calls=%fused_computation.1 | loop fusion | flops 384 | bytes 1152 | tf_op jit(solution)/shard_map/div | solution.py:595
  (2 shorter events, 0.0 us)
Async XLA Ops:
  3.9 10.6 %collective-permute-start = (f32[96,128]{1,0:T(8,128)S(1)}, f32[96,128]{1,0:T(8,128)S(1)}, u32[]{:S(2)}, u32[]{:S(2)}) collective-permute-start(f32[96,128]{1,0:T(8,128)S(1)} %get-tuple-element.44), channel_id=1, source_target_pairs={{0,1},{1,0},{2,3},{3,2},{4,5},{5,4},{6,7},{7,6},{8,9},{9,8},{10,11... | collective-permute-start | bytes 147464 | tf_op jit(solution)/shard_map/ppermute | solution.py:506
  4.0 10.5 %collective-permute-start.1 = (f32[96,128]{1,0:T(8,128)S(1)}, f32[96,128]{1,0:T(8,128)S(1)}, u32[]{:S(2)}, u32[]{:S(2)}) collective-permute-start(f32[96,128]{1,0:T(8,128)S(1)} %get-tuple-element.45), channel_id=1, source_target_pairs={{1,2},{2,1},{3,4},{4,3},{5,6},{6,5},{7,8},{8,7},{9,10},{10,9},{11,... | collective-permute-start | bytes 147464 | tf_op jit(solution)/shard_map/ppermute | solution.py:507
  8.7 9.5 %collective-permute-start.4 = (f32[8,6912]{1,0:T(8,128)S(1)}, f32[8,6912]{1,0:T(8,128)S(1)}, u32[]{:S(2)}, u32[]{:S(2)}) collective-permute-start(f32[8,6912]{1,0:T(8,128)S(1)} %get-tuple-element.53), channel_id=1, source_target_pairs={{16,32},{32,16},{48,64},{64,48},{80,96},{96,80},{17,33},{33,17},{4... | collective-permute-start | bytes 663560 | tf_op jit(solution)/shard_map/ppermute | solution.py:508
  9.4 8.8 %collective-permute-start.5 = (f32[8,6912]{1,0:T(8,128)S(1)}, f32[8,6912]{1,0:T(8,128)S(1)}, u32[]{:S(2)}, u32[]{:S(2)}) collective-permute-start(f32[8,6912]{1,0:T(8,128)S(1)} %get-tuple-element.54), channel_id=1, source_target_pairs={{0,16},{16,0},{32,48},{48,32},{64,80},{80,64},{96,112},{112,96},{1... | collective-permute-start | bytes 663560 | tf_op jit(solution)/shard_map/ppermute | solution.py:509
  12.3 0.7 %copy-start = (f32[96]{0:T(128)S(1)}, f32[96]{0:T(128)}, u32[]{:S(2)}) copy-start(f32[96]{0:T(128)} %param.6) | copy-start | bytes 1156
  12.3 0.7 %copy-start.1 = (s32[2,96]{1,0:T(2,128)S(1)}, s32[2,96]{1,0:T(2,128)}, u32[]{:S(2)}) copy-start(s32[2,96]{1,0:T(2,128)} %reach_ref.1) | copy-start | bytes 2308
  14.6 5.7 %collective-permute-start.2 = (f32[8,256]{1,0:T(8,128)S(1)}, f32[8,256]{1,0:T(8,128)S(1)}, u32[]{:S(2)}, u32[]{:S(2)}) collective-permute-start(f32[8,256]{1,0:T(8,128)S(1)} %get-tuple-element.46), channel_id=1, source_target_pairs={{16,32},{32,16},{48,64},{64,48},{80,96},{96,80},{17,33},{33,17},{4... | collective-permute-start | bytes 24584 | tf_op jit(solution)/shard_map/ppermute | solution.py:541
  15.3 5.1 %collective-permute-start.3 = (f32[8,256]{1,0:T(8,128)S(1)}, f32[8,256]{1,0:T(8,128)S(1)}, u32[]{:S(2)}, u32[]{:S(2)}) collective-permute-start(f32[8,256]{1,0:T(8,128)S(1)} %get-tuple-element.47), channel_id=1, source_target_pairs={{0,16},{16,0},{32,48},{48,32},{64,80},{80,64},{96,112},{112,96},{1... | collective-permute-start | bytes 24584 | tf_op jit(solution)/shard_map/ppermute | solution.py:542

commit v13 on v11

--- a/solution.py
+++ b/solution.py
@@ -276,11 +276,16 @@
         acc_ref[1, r : r + HMAX, :] = den
 
 
-def leaves_early():
+def fields_early():
+    gz = lax.axis_index("gz")
+    return (gz == 0) | ((gz >= 8) & (gz % 4 < 2))
+
+
+def filters_early():
     return lax.axis_index("gz") == 0
 
 
-def inner_work(v_ref, s_ref, pair_ref, fh, fl, inner):
+def own_fields(v_ref, s_ref, fh, fl):
     rows, cells = v_ref.shape[1:]
     for t in range(cells // LANES):
         at = slice(t * LANES, (t + 1) * LANES)
@@ -296,6 +301,9 @@
             store_fields(
                 [v_ref[f, rr, at] for f in range(3)], [s_ref[f, rr, at] for f in range(6)], put_high, put_low
             )
+
+
+def own_filters(pair_ref, fh, fl, inner):
     for n in range(inner.shape[0]):
         g = smooth_pair(n, fh, fl, pair_ref)
         for f in range(FIELDS):
@@ -303,15 +311,23 @@
 
 
 def early_kernel(v_ref, s_ref, pair_ref, a, b, c, d, fh, fl, inner, *same):
-    @pl.when(leaves_early())
+    @pl.when(fields_early())
     def _():
-        inner_work(v_ref, s_ref, pair_ref, fh, fl, inner)
+        own_fields(v_ref, s_ref, fh, fl)
+
+    @pl.when(filters_early())
+    def _():
+        own_filters(pair_ref, fh, fl, inner)
 
 
 def late_kernel(v_ref, s_ref, pair_ref, a, b, c, fh, fl, inner):
-    @pl.when(jnp.logical_not(leaves_early()))
+    @pl.when(jnp.logical_not(fields_early()))
     def _():
-        inner_work(v_ref, s_ref, pair_ref, fh, fl, inner)
+        own_fields(v_ref, s_ref, fh, fl)
+
+    @pl.when(jnp.logical_not(filters_early()))
+    def _():
+        own_filters(pair_ref, fh, fl, inner)
 
 
 def wall_kernel(

time: 33.3 us -> 34.9 us (1.048)
  blocking collectives: 10.6 us -> 12.2 us
  Pallas kernels: 8.38 us -> 8.93 us
  starting transfers between devices: 12.7 us -> 12.2 us
    all_to_all x1, blocking collectives: 10.6 us -> 12.2 us  [local(): sums = jnp.sum(lax.all_to_all(sums, 'gz', 0, 0), axis=0)]
    pallas_call x5, Pallas kernels: 6.66 us -> 7.21 us  [call(): pl.pallas_call(kernel, in_specs=[vmem] * len(operands), out_specs=jax.tre...]
where the time goes in v13:
time: 34.9 us; the launch traced here: 34.7 us
  starting transfers between devices  12.2 us (35%)
  blocking collectives  12.2 us (35%)
  Pallas kernels  8.93 us (26%)
  local copies, waits for them, and re-layouts  0.65 us (2%)
  other arithmetic  0.55 us (2%)
    all_to_all x1, blocking collectives, local(): sums = jnp.sum(lax.all_to_all(sums, 'gz', 0, 0), axis=0)  12.2 us
    pallas_call x5, Pallas kernels, call(): pl.pallas_call(kernel, in_specs=[vmem] * len(operands), out_specs=jax.tre...  7.21 us
    ppermute x1, starting transfers between devices, local(): zfar = lax.ppermute(far, 'gz', far_pairs('gz', True))  4.36 us
    ppermute x1, starting transfers between devices, local(): corner_far = lax.ppermute(far, 'gy', far_pairs('gy', False))  3.49 us
    ppermute x1, starting transfers between devices, local(): yfar = lax.ppermute(wall_far, 'gy', far_pairs('gy', False))  3 us
    pallas_call x1, Pallas kernels, first_call(): pl.pallas_call(first_kernel, in_specs=[hbm] * 2, out_specs=[vmem] * 8, ou...  1.64 us
    ppermute x1, starting transfers between devices, local(): ynear = lax.ppermute(wall_near, 'gy', near_pairs('gy'))  1.24 us
  transfers between devices with their start and end apart: 6, of which 0 were waited for; matrix products, arithmetic and copies ran while one was open for 0% of the time, Pallas kernels for 11%

profile of v13, /device:TPU:1, one launch (start us, length us, event | category | flops | bytes accessed | tf_op | source)
XLA Modules:
  0.0 34.7 jit_solution(6983619089135786358)
XLA Ops:
  0.0 1.6 %shard_map.46 = (f32[96,128]{1,0:T(8,128)S(1)}, f32[96,128]{1,0:T(8,128)S(1)}, f32[8,6912]{1,0:T(8,128)S(1)}, f32[8,6912]{1,0:T(8,128)S(1)}, f32[3,96,768]{2,1,0...) custom-call(f32[3,96,768]{2,1,0:T(8,128)} %v_ref.1, ...), custom_call_target="tpu_custom_call" | custom-call | tf_op jit(solution)/shard_map/pallas_call | solution.py:114
  1.7 2.8 %shard_map.47 = (bf16[21,96,768]{2,1,0:T(8,128)(2,1)S(1)}, bf16[15,96,768]{2,1,0:T(8,128)(2,1)S(1)}, f32[2,21,96,256]{3,2,1,0:T(8,128)S(1)}, f32[96,128]{1,0:T(8...) custom-call(f32[3,96,768]{2,1,0:T(8,128)S(1)} %get-tuple-element.37., ...), custom_call_target="tpu_custom_call", output_to_operand_aliasing={{3}: (3, {}), {4}: (4, {}), {5}: (5, {}), {6}: (6, {})} | custom-call | flops 4000000000 | bytes 1048576 | tf_op jit(solution)/shard_map/pallas_call | solution.py:485
  4.5 0.1 collective-permute-start
  4.6 4.4 %collective-permute-start.1 = (f32[96,128]{1,0:T(8,128)S(1)}, f32[96,128]{1,0:T(8,128)S(1)}, u32[]{:S(2)}, u32[]{:S(2)}) collective-permute-start(f32[96,128]{1,0:T(8,128)S(1)} %get-tuple-element.45), channel_id=1, source_target_pairs={{1,2},{2,1},{3,4},{4,3},{5,6},{6,5},{7,8},{8,7},{9,10},{10,9},{11,... | collective-permute-start | bytes 147464 | tf_op jit(solution)/shard_map/ppermute | solution.py:523
  8.9 1.2 %collective-permute-start.4 = (f32[8,6912]{1,0:T(8,128)S(1)}, f32[8,6912]{1,0:T(8,128)S(1)}, u32[]{:S(2)}, u32[]{:S(2)}) collective-permute-start(f32[8,6912]{1,0:T(8,128)S(1)} %get-tuple-element.53), channel_id=1, source_target_pairs={{0,16},{16,0},{32,48},{48,32},{64,80},{80,64},{96,112},{112,96},{1... | collective-permute-start | bytes 663560 | tf_op jit(solution)/shard_map/ppermute | solution.py:525
  10.2 3.0 %collective-permute-start.5 = (f32[8,6912]{1,0:T(8,128)S(1)}, f32[8,6912]{1,0:T(8,128)S(1)}, u32[]{:S(2)}, u32[]{:S(2)}) collective-permute-start(f32[8,6912]{1,0:T(8,128)S(1)} %get-tuple-element.54), channel_id=1, source_target_pairs={{16,32},{32,16},{48,64},{64,48},{80,96},{96,80},{17,33},{33,17},{4... | collective-permute-start | bytes 663560 | tf_op jit(solution)/shard_map/ppermute | solution.py:524
  13.2 0.0 copy-start
  13.2 0.0 copy-start.1
  13.2 0.6 %copy-done = f32[96]{0:T(128)S(1)} copy-done((f32[96]{0:T(128)S(1)}, f32[96]{0:T(128)}, u32[]{:S(2)}) %copy-start) | copy-done | bytes 408
  13.8 0.0 copy-done.1
  13.9 1.5 %shard_map.50 = (f32[2,96,128]{2,1,0:T(8,128)S(1)}, f32[2,21,16,256]{3,2,1,0:T(8,128)S(1)}, bf16[96,256]{1,0:T(8,128)(2,1)S(1)}, f32[96,128]{1,0:T(8,128)S(1)}, ...) custom-call(f32[1,96]{1,0:T(1,128)S(1)} %bitcast.3, s32[2,96]{1,0:T(2,128)S(1)} %copy-done.1, ...), custom_call_target="tpu_custom_call" | custom-call | flops 4000000000 | bytes 1048576 | tf_op jit(solution)/shard_map/pallas_call | solution.py:485
  15.4 0.0 collective-permute-done.znear
  15.4 0.0 collective-permute-done.1.zfar
  15.4 0.1 shard_map.48
  15.5 0.0 collective-permute-start.2
  15.5 3.5 %collective-permute-start.3 = (f32[8,256]{1,0:T(8,128)S(1)}, f32[8,256]{1,0:T(8,128)S(1)}, u32[]{:S(2)}, u32[]{:S(2)}) collective-permute-start(f32[8,256]{1,0:T(8,128)S(1)} %get-tuple-element.47), channel_id=1, source_target_pairs={{16,32},{32,16},{48,64},{64,48},{80,96},{96,80},{17,33},{33,17},{4... | collective-permute-start | bytes 24584 | tf_op jit(solution)/shard_map/ppermute | solution.py:557
  19.0 0.0 collective-permute-done.4.ynear
  19.0 0.0 collective-permute-done.5.yfar
  19.0 2.1 %shard_map.51 = (f32[2,128]{1,0:T(2,128)S(1)}, f32[21,16,256]{2,1,0:T(8,128)S(1)}, bf16[21,16,768]{2,1,0:T(8,128)(2,1)S(1)}, bf16[15,16,768]{2,1,0:T(8,128)(2,1)S(1)}, f32[2,21,16,256]{3,2,1,0:T(8,128)S(1)}) custom-call(bf16[21,96,768]{2,1,0:T(8,128)(2,1)S(1)} %get-tuple-element.51.fh, bf16[15,96,768]{2,1,0:T(8,128)(2,1)S(1)} %get-tuple-element.52.fl, ...), custom_call_target="tpu_custom_call" | custom-call | flops 4000000000 | bytes 1048576 | tf_op jit(solution)/shard_map/pallas_call | solution.py:485
  21.2 0.0 collective-permute-done.2.near_ref
  21.2 0.0 collective-permute-done.3.far_ref
  21.2 0.8 %shard_map.52 = f32[16,2,96]{2,1,0:T(2,128)S(1)} custom-call(f32[8,256]{1,0:T(8,128)S(1)} %collective-permute-done.2.near_ref, f32[8,256]{1,0:T(8,128)S(1)} %collective-permute-done.3.far_ref, f32[2,128]{1,0:T(2,128)S(1)} %get-tuple-element.61.sums_in, f32[2,21,16,256]{3,2,1,0:T(8,128)S(1)} %get-tuple-element.62.part_inner, ...), custom_call_target="tpu_custom_call" | custom-call | flops 4000000000 | bytes 1048576 | tf_op jit(solution)/shard_map/pallas_call | solution.py:485
  22.0 12.2 %all_to_all.5 = f32[16,2,96]{2,1,0:T(2,128)S(1)} all-to-all(f32[16,2,96]{2,1,0:T(2,128)S(1)} %shard_map.52), channel_id=1, replica_groups=mesh['gy'=8,'gz'=16] {'gz'}, dimensions={0} | all-to-all | bytes 24576 | tf_op jit(solution)/shard_map/all_to_all | solution.py:609
  34.2 0.5 %fusion = f32[96]{0:T(128)} fusion(f32[2,96]{1,0:T(2,128)S(1)} %reduce_sum.9), kind=kLoop, calls=%fused_computation.1 | loop fusion | flops 384 | bytes 1152 | tf_op jit(solution)/shard_map/div | solution.py:611
  (2 shorter events, 0.1 us)
Async XLA Ops:
  4.5 10.9 %collective-permute-start = (f32[96,128]{1,0:T(8,128)S(1)}, f32[96,128]{1,0:T(8,128)S(1)}, u32[]{:S(2)}, u32[]{:S(2)}) collective-permute-start(f32[96,128]{1,0:T(8,128)S(1)} %get-tuple-element.44), channel_id=1, source_target_pairs={{0,1},{1,0},{2,3},{3,2},{4,5},{5,4},{6,7},{7,6},{8,9},{9,8},{10,11... | collective-permute-start | bytes 147464 | tf_op jit(solution)/shard_map/ppermute | solution.py:522
  4.6 10.8 %collective-permute-start.1 = (f32[96,128]{1,0:T(8,128)S(1)}, f32[96,128]{1,0:T(8,128)S(1)}, u32[]{:S(2)}, u32[]{:S(2)}) collective-permute-start(f32[96,128]{1,0:T(8,128)S(1)} %get-tuple-element.45), channel_id=1, source_target_pairs={{1,2},{2,1},{3,4},{4,3},{5,6},{6,5},{7,8},{8,7},{9,10},{10,9},{11,... | collective-permute-start | bytes 147464 | tf_op jit(solution)/shard_map/ppermute | solution.py:523
  8.9 10.1 %collective-permute-start.4 = (f32[8,6912]{1,0:T(8,128)S(1)}, f32[8,6912]{1,0:T(8,128)S(1)}, u32[]{:S(2)}, u32[]{:S(2)}) collective-permute-start(f32[8,6912]{1,0:T(8,128)S(1)} %get-tuple-element.53), channel_id=1, source_target_pairs={{0,16},{16,0},{32,48},{48,32},{64,80},{80,64},{96,112},{112,96},{1... | collective-permute-start | bytes 663560 | tf_op jit(solution)/shard_map/ppermute | solution.py:525
  10.2 8.9 %collective-permute-start.5 = (f32[8,6912]{1,0:T(8,128)S(1)}, f32[8,6912]{1,0:T(8,128)S(1)}, u32[]{:S(2)}, u32[]{:S(2)}) collective-permute-start(f32[8,6912]{1,0:T(8,128)S(1)} %get-tuple-element.54), channel_id=1, source_target_pairs={{16,32},{32,16},{48,64},{64,48},{80,96},{96,80},{17,33},{33,17},{4... | collective-permute-start | bytes 663560 | tf_op jit(solution)/shard_map/ppermute | solution.py:524
  13.2 0.7 %copy-start = (f32[96]{0:T(128)S(1)}, f32[96]{0:T(128)}, u32[]{:S(2)}) copy-start(f32[96]{0:T(128)} %param.6) | copy-start | bytes 1156
  13.2 0.7 %copy-start.1 = (s32[2,96]{1,0:T(2,128)S(1)}, s32[2,96]{1,0:T(2,128)}, u32[]{:S(2)}) copy-start(s32[2,96]{1,0:T(2,128)} %reach_ref.1) | copy-start | bytes 2308
  15.5 5.7 %collective-permute-start.2 = (f32[8,256]{1,0:T(8,128)S(1)}, f32[8,256]{1,0:T(8,128)S(1)}, u32[]{:S(2)}, u32[]{:S(2)}) collective-permute-start(f32[8,256]{1,0:T(8,128)S(1)} %get-tuple-element.46), channel_id=1, source_target_pairs={{0,16},{16,0},{32,48},{48,32},{64,80},{80,64},{96,112},{112,96},{1... | collective-permute-start | bytes 24584 | tf_op jit(solution)/shard_map/ppermute | solution.py:558
  15.5 5.7 %collective-permute-start.3 = (f32[8,256]{1,0:T(8,128)S(1)}, f32[8,256]{1,0:T(8,128)S(1)}, u32[]{:S(2)}, u32[]{:S(2)}) collective-permute-start(f32[8,256]{1,0:T(8,128)S(1)} %get-tuple-element.47), channel_id=1, source_target_pairs={{16,32},{32,16},{48,64},{64,48},{80,96},{96,80},{17,33},{33,17},{4... | collective-permute-start | bytes 24584 | tf_op jit(solution)/shard_map/ppermute | solution.py:557

commit v14 on v13

--- a/solution.py
+++ b/solution.py
@@ -278,7 +278,7 @@
 
 def fields_early():
     gz = lax.axis_index("gz")
-    return (gz == 0) | ((gz >= 8) & (gz % 4 < 2))
+    return (gz == 0) | (gz == 9)
 
 
 def filters_early():
@@ -424,7 +424,7 @@
         store_fields(raw[:3], raw[3:], put_high, put_low)
 
 
-def last_kernel(near_ref, far_ref, sums_in, part_inner, part_ends, mask_ref, total_ref, hh, hl, halo_inner, ends_ref, out_ref, eh, el, stack):
+def last_kernel(far_ref, near_ref, sums_in, part_inner, part_ends, mask_ref, total_ref, hh, hl, halo_inner, ends_ref, out_ref, eh, el, stack):
     rows = out_ref.shape[2]
     width = 2 * LANES
     gy_odd = lax.axis_index("gy") % 2 == 1
@@ -594,8 +594,8 @@
             pltpu.VMEM((blocks + 1, 2 * ends, FIELDS * width), BF16),
         ],
         LARGE_VMEM,
+        corner_far,
         corner_near,
-        corner_far,
         sums,
         part_inner,
         part_ends,

time: 34.9 us -> 33.4 us (0.957)
  blocking collectives: 12.2 us -> 11.1 us
  starting transfers between devices: 12.2 us -> 11.3 us
    all_to_all x1, blocking collectives: 12.2 us -> 11.1 us  [local(): sums = jnp.sum(lax.all_to_all(sums, 'gz', 0, 0), axis=0)]
    ppermute x1, starting transfers between devices: 3.49 us -> 2.54 us  [local(): corner_far = lax.ppermute(far, 'gy', far_pairs('gy', False))]
  transfers between devices with their start and end apart: 6 -> 6, of which waited for: 0 -> 1; matrix products, arithmetic and copies ran while one was open for 0% -> 0% of each run, Pallas kernels for 11% -> 11%
where the time goes in v14:
time: 33.4 us; the launch traced here: 32.9 us
  starting transfers between devices  11.3 us (34%)
  blocking collectives  11.1 us (33%)
  Pallas kernels  8.92 us (27%)
  local copies, waits for them, and re-layouts  0.65 us (2%)
  other arithmetic  0.55 us (2%)
    all_to_all x1, blocking collectives, local(): sums = jnp.sum(lax.all_to_all(sums, 'gz', 0, 0), axis=0)  11.1 us
    pallas_call x5, Pallas kernels, call(): pl.pallas_call(kernel, in_specs=[vmem] * len(operands), out_specs=jax.tre...  7.2 us
    ppermute x1, starting transfers between devices, local(): zfar = lax.ppermute(far, 'gz', far_pairs('gz', True))  4.36 us
    ppermute x1, starting transfers between devices, local(): yfar = lax.ppermute(wall_far, 'gy', far_pairs('gy', False))  3 us
    ppermute x1, starting transfers between devices, local(): corner_far = lax.ppermute(far, 'gy', far_pairs('gy', False))  2.54 us
    pallas_call x1, Pallas kernels, first_call(): pl.pallas_call(first_kernel, in_specs=[hbm] * 2, out_specs=[vmem] * 8, ou...  1.64 us
    ppermute x1, starting transfers between devices, local(): ynear = lax.ppermute(wall_near, 'gy', near_pairs('gy'))  1.24 us
  transfers between devices with their start and end apart: 6, of which 1 were waited for; matrix products, arithmetic and copies ran while one was open for 0% of the time, Pallas kernels for 11%

profile of v14, /device:TPU:1, one launch (start us, length us, event | category | flops | bytes accessed | tf_op | source)
XLA Modules:
  0.0 32.9 jit_solution(17608846203443056984)
XLA Ops:
  0.0 1.6 %shard_map.46 = (f32[96,128]{1,0:T(8,128)S(1)}, f32[96,128]{1,0:T(8,128)S(1)}, f32[8,6912]{1,0:T(8,128)S(1)}, f32[8,6912]{1,0:T(8,128)S(1)}, f32[3,96,768]{2,1,0...) custom-call(f32[3,96,768]{2,1,0:T(8,128)} %v_ref.1, ...), custom_call_target="tpu_custom_call" | custom-call | tf_op jit(solution)/shard_map/pallas_call | solution.py:114
  1.7 2.8 %shard_map.47 = (bf16[21,96,768]{2,1,0:T(8,128)(2,1)S(1)}, bf16[15,96,768]{2,1,0:T(8,128)(2,1)S(1)}, f32[2,21,96,256]{3,2,1,0:T(8,128)S(1)}, f32[96,128]{1,0:T(8...) custom-call(f32[3,96,768]{2,1,0:T(8,128)S(1)} %get-tuple-element.37., ...), custom_call_target="tpu_custom_call", output_to_operand_aliasing={{3}: (3, {}), {4}: (4, {}), {5}: (5, {}), {6}: (6, {})} | custom-call | flops 4000000000 | bytes 1048576 | tf_op jit(solution)/shard_map/pallas_call | solution.py:485
  4.5 0.1 collective-permute-start
  4.6 4.4 %collective-permute-start.1 = (f32[96,128]{1,0:T(8,128)S(1)}, f32[96,128]{1,0:T(8,128)S(1)}, u32[]{:S(2)}, u32[]{:S(2)}) collective-permute-start(f32[96,128]{1,0:T(8,128)S(1)} %get-tuple-element.45), channel_id=1, source_target_pairs={{1,2},{2,1},{3,4},{4,3},{5,6},{6,5},{7,8},{8,7},{9,10},{10,9},{11,... | collective-permute-start | bytes 147464 | tf_op jit(solution)/shard_map/ppermute | solution.py:523
  8.9 1.2 %collective-permute-start.4 = (f32[8,6912]{1,0:T(8,128)S(1)}, f32[8,6912]{1,0:T(8,128)S(1)}, u32[]{:S(2)}, u32[]{:S(2)}) collective-permute-start(f32[8,6912]{1,0:T(8,128)S(1)} %get-tuple-element.53), channel_id=1, source_target_pairs={{0,16},{16,0},{32,48},{48,32},{64,80},{80,64},{96,112},{112,96},{1... | collective-permute-start | bytes 663560 | tf_op jit(solution)/shard_map/ppermute | solution.py:525
  10.2 3.0 %collective-permute-start.5 = (f32[8,6912]{1,0:T(8,128)S(1)}, f32[8,6912]{1,0:T(8,128)S(1)}, u32[]{:S(2)}, u32[]{:S(2)}) collective-permute-start(f32[8,6912]{1,0:T(8,128)S(1)} %get-tuple-element.54), channel_id=1, source_target_pairs={{16,32},{32,16},{48,64},{64,48},{80,96},{96,80},{17,33},{33,17},{4... | collective-permute-start | bytes 663560 | tf_op jit(solution)/shard_map/ppermute | solution.py:524
  13.2 0.0 copy-start
  13.2 0.0 copy-start.1
  13.2 0.6 %copy-done = f32[96]{0:T(128)S(1)} copy-done((f32[96]{0:T(128)S(1)}, f32[96]{0:T(128)}, u32[]{:S(2)}) %copy-start) | copy-done | bytes 408
  13.8 0.0 copy-done.1
  13.9 1.5 %shard_map.50 = (f32[2,96,128]{2,1,0:T(8,128)S(1)}, f32[2,21,16,256]{3,2,1,0:T(8,128)S(1)}, bf16[96,256]{1,0:T(8,128)(2,1)S(1)}, f32[96,128]{1,0:T(8,128)S(1)}, ...) custom-call(f32[1,96]{1,0:T(1,128)S(1)} %bitcast.3, s32[2,96]{1,0:T(2,128)S(1)} %copy-done.1, ...), custom_call_target="tpu_custom_call" | custom-call | flops 4000000000 | bytes 1048576 | tf_op jit(solution)/shard_map/pallas_call | solution.py:485
  15.4 0.0 collective-permute-done.znear
  15.4 0.0 collective-permute-done.1.zfar
  15.4 0.1 shard_map.48
  15.5 2.5 %collective-permute-start.2 = (f32[8,256]{1,0:T(8,128)S(1)}, f32[8,256]{1,0:T(8,128)S(1)}, u32[]{:S(2)}, u32[]{:S(2)}) collective-permute-start(f32[8,256]{1,0:T(8,128)S(1)} %get-tuple-element.46), channel_id=1, source_target_pairs={{16,32},{32,16},{48,64},{64,48},{80,96},{96,80},{17,33},{33,17},{4... | collective-permute-start | bytes 24584 | tf_op jit(solution)/shard_map/ppermute | solution.py:557
  18.0 0.1 collective-permute-start.3
  18.1 0.0 collective-permute-done.4.ynear
  18.1 0.0 collective-permute-done.5.yfar
  18.1 2.1 %shard_map.51 = (f32[2,128]{1,0:T(2,128)S(1)}, f32[21,16,256]{2,1,0:T(8,128)S(1)}, bf16[21,16,768]{2,1,0:T(8,128)(2,1)S(1)}, bf16[15,16,768]{2,1,0:T(8,128)(2,1)S(1)}, f32[2,21,16,256]{3,2,1,0:T(8,128)S(1)}) custom-call(bf16[21,96,768]{2,1,0:T(8,128)(2,1)S(1)} %get-tuple-element.51.fh, bf16[15,96,768]{2,1,0:T(8,128)(2,1)S(1)} %get-tuple-element.52.fl, ...), custom_call_target="tpu_custom_call" | custom-call | flops 4000000000 | bytes 1048576 | tf_op jit(solution)/shard_map/pallas_call | solution.py:485
  20.3 0.2 collective-permute-done.2.far_ref
  20.4 0.0 collective-permute-done.3.near_ref
  20.4 0.8 %shard_map.52 = f32[16,2,96]{2,1,0:T(2,128)S(1)} custom-call(f32[8,256]{1,0:T(8,128)S(1)} %collective-permute-done.2.far_ref, f32[8,256]{1,0:T(8,128)S(1)} %collective-permute-done.3.near_ref, f32[2,128]{1,0:T(2,128)S(1)} %get-tuple-element.61.sums_in, f32[2,21,16,256]{3,2,1,0:T(8,128)S(1)} %get-tuple-element.62.part_inner, ...), custom_call_target="tpu_custom_call" | custom-call | flops 4000000000 | bytes 1048576 | tf_op jit(solution)/shard_map/pallas_call | solution.py:485
  21.2 11.1 %all_to_all.5 = f32[16,2,96]{2,1,0:T(2,128)S(1)} all-to-all(f32[16,2,96]{2,1,0:T(2,128)S(1)} %shard_map.52), channel_id=1, replica_groups=mesh['gy'=8,'gz'=16] {'gz'}, dimensions={0} | all-to-all | bytes 24576 | tf_op jit(solution)/shard_map/all_to_all | solution.py:609
  32.3 0.5 %fusion = f32[96]{0:T(128)} fusion(f32[2,96]{1,0:T(2,128)S(1)} %reduce_sum.9), kind=kLoop, calls=%fused_computation.1 | loop fusion | flops 384 | bytes 1152 | tf_op jit(solution)/shard_map/div | solution.py:611
  (2 shorter events, 0.0 us)
Async XLA Ops:
  4.5 10.9 %collective-permute-start = (f32[96,128]{1,0:T(8,128)S(1)}, f32[96,128]{1,0:T(8,128)S(1)}, u32[]{:S(2)}, u32[]{:S(2)}) collective-permute-start(f32[96,128]{1,0:T(8,128)S(1)} %get-tuple-element.44), channel_id=1, source_target_pairs={{0,1},{1,0},{2,3},{3,2},{4,5},{5,4},{6,7},{7,6},{8,9},{9,8},{10,11... | collective-permute-start | bytes 147464 | tf_op jit(solution)/shard_map/ppermute | solution.py:522
  4.6 10.8 %collective-permute-start.1 = (f32[96,128]{1,0:T(8,128)S(1)}, f32[96,128]{1,0:T(8,128)S(1)}, u32[]{:S(2)}, u32[]{:S(2)}) collective-permute-start(f32[96,128]{1,0:T(8,128)S(1)} %get-tuple-element.45), channel_id=1, source_target_pairs={{1,2},{2,1},{3,4},{4,3},{5,6},{6,5},{7,8},{8,7},{9,10},{10,9},{11,... | collective-permute-start | bytes 147464 | tf_op jit(solution)/shard_map/ppermute | solution.py:523
  8.9 9.2 %collective-permute-start.4 = (f32[8,6912]{1,0:T(8,128)S(1)}, f32[8,6912]{1,0:T(8,128)S(1)}, u32[]{:S(2)}, u32[]{:S(2)}) collective-permute-start(f32[8,6912]{1,0:T(8,128)S(1)} %get-tuple-element.53), channel_id=1, source_target_pairs={{0,16},{16,0},{32,48},{48,32},{64,80},{80,64},{96,112},{112,96},{1... | collective-permute-start | bytes 663560 | tf_op jit(solution)/shard_map/ppermute | solution.py:525
  10.2 8.0 %collective-permute-start.5 = (f32[8,6912]{1,0:T(8,128)S(1)}, f32[8,6912]{1,0:T(8,128)S(1)}, u32[]{:S(2)}, u32[]{:S(2)}) collective-permute-start(f32[8,6912]{1,0:T(8,128)S(1)} %get-tuple-element.54), channel_id=1, source_target_pairs={{16,32},{32,16},{48,64},{64,48},{80,96},{96,80},{17,33},{33,17},{4... | collective-permute-start | bytes 663560 | tf_op jit(solution)/shard_map/ppermute | solution.py:524
  13.2 0.7 %copy-start = (f32[96]{0:T(128)S(1)}, f32[96]{0:T(128)}, u32[]{:S(2)}) copy-start(f32[96]{0:T(128)} %param.6) | copy-start | bytes 1156
  13.2 0.7 %copy-start.1 = (s32[2,96]{1,0:T(2,128)S(1)}, s32[2,96]{1,0:T(2,128)}, u32[]{:S(2)}) copy-start(s32[2,96]{1,0:T(2,128)} %reach_ref.1) | copy-start | bytes 2308
  15.5 5.0 %collective-permute-start.2 = (f32[8,256]{1,0:T(8,128)S(1)}, f32[8,256]{1,0:T(8,128)S(1)}, u32[]{:S(2)}, u32[]{:S(2)}) collective-permute-start(f32[8,256]{1,0:T(8,128)S(1)} %get-tuple-element.46), channel_id=1, source_target_pairs={{16,32},{32,16},{48,64},{64,48},{80,96},{96,80},{17,33},{33,17},{4... | collective-permute-start | bytes 24584 | tf_op jit(solution)/shard_map/ppermute | solution.py:557
  18.0 2.4 %collective-permute-start.3 = (f32[8,256]{1,0:T(8,128)S(1)}, f32[8,256]{1,0:T(8,128)S(1)}, u32[]{:S(2)}, u32[]{:S(2)}) collective-permute-start(f32[8,256]{1,0:T(8,128)S(1)} %get-tuple-element.47), channel_id=1, source_target_pairs={{0,16},{16,0},{32,48},{48,32},{64,80},{80,64},{96,112},{112,96},{1... | collective-permute-start | bytes 24584 | tf_op jit(solution)/shard_map/ppermute | solution.py:558

commit v15 on v12

--- a/solution.py
+++ b/solution.py
@@ -347,7 +347,7 @@
 
 
 def outer_kernel(
-    fh, fl, znear, zfar, yfar, ynear, pair_ref, ends_ref, acc_in, own_ref, height_ref, inv_ref,
+    fh, fl, znear, zfar, ynear, yfar, pair_ref, ends_ref, acc_in, own_ref, height_ref, inv_ref,
     sums_ref, part_ref, hh, hl, halo_inner, eh, el, stack, acc_ref,
 ):
     rows, cells = fh.shape[1:]
@@ -560,8 +560,8 @@
         fl,
         znear,
         zfar,
+        ynear,
         yfar,
-        ynear,
         pair,
         both_ends,
         acc,

time: 33.9 us -> 32.9 us (0.971)
  the two profiles are of different devices: /device:TPU:0 before, /device:TPU:1 now
where the time goes in v15:
time: 32.9 us; the launch traced here: 32.3 us
  starting transfers between devices  11.9 us (36%)
  blocking collectives  10.6 us (32%)
  Pallas kernels  8.37 us (25%)
  local copies, waits for them, and re-layouts  0.66 us (2%)
  other arithmetic  0.55 us (2%)
    all_to_all x1, blocking collectives, local(): sums = jnp.sum(lax.all_to_all(sums, 'gz', 0, 0), axis=0)  10.6 us
    pallas_call x5, Pallas kernels, call(): pl.pallas_call(kernel, in_specs=[vmem] * len(operands), out_specs=jax.tre...  6.65 us
    ppermute x1, starting transfers between devices, local(): zfar = lax.ppermute(far, 'gz', far_pairs('gz', True))  4.69 us
    ppermute x1, starting transfers between devices, local(): yfar = lax.ppermute(wall_far, 'gy', far_pairs('gy', False))  3 us
    ppermute x1, starting transfers between devices, local(): corner_far = lax.ppermute(far, 'gy', far_pairs('gy', False))  2.54 us
    pallas_call x1, Pallas kernels, first_call(): pl.pallas_call(first_kernel, in_specs=[hbm] * 2, out_specs=[vmem] * 8, ou...  1.64 us
    ppermute x1, starting transfers between devices, local(): ynear = lax.ppermute(wall_near, 'gy', near_pairs('gy'))  1.24 us
    unnamed x4, local copies, waits for them, and re-layouts  0.66 us
  transfers between devices with their start and end apart: 6, of which 1 were waited for; matrix products, arithmetic and copies ran while one was open for 0% of the time, Pallas kernels for 12%

profile of v15, /device:TPU:1, one launch (start us, length us, event | category | flops | bytes accessed | tf_op | source)
XLA Modules:
  0.0 32.3 jit_solution(7805488627531541528)
XLA Ops:
  0.0 1.6 %shard_map.46 = (f32[96,128]{1,0:T(8,128)S(1)}, f32[96,128]{1,0:T(8,128)S(1)}, f32[8,6912]{1,0:T(8,128)S(1)}, f32[8,6912]{1,0:T(8,128)S(1)}, f32[3,96,768]{2,1,0...) custom-call(f32[3,96,768]{2,1,0:T(8,128)} %v_ref.1, ...), custom_call_target="tpu_custom_call" | custom-call | tf_op jit(solution)/shard_map/pallas_call | solution.py:114
  1.7 2.3 %shard_map.47 = (bf16[21,96,768]{2,1,0:T(8,128)(2,1)S(1)}, bf16[15,96,768]{2,1,0:T(8,128)(2,1)S(1)}, f32[2,21,96,256]{3,2,1,0:T(8,128)S(1)}, f32[96,128]{1,0:T(8...) custom-call(f32[3,96,768]{2,1,0:T(8,128)S(1)} %get-tuple-element.37., ...), custom_call_target="tpu_custom_call", output_to_operand_aliasing={{3}: (3, {}), {4}: (4, {}), {5}: (5, {}), {6}: (6, {})} | custom-call | flops 4000000000 | bytes 1048576 | tf_op jit(solution)/shard_map/pallas_call | solution.py:469
  3.9 0.3 collective-permute-start
  4.2 4.7 %collective-permute-start.1 = (f32[96,128]{1,0:T(8,128)S(1)}, f32[96,128]{1,0:T(8,128)S(1)}, u32[]{:S(2)}, u32[]{:S(2)}) collective-permute-start(f32[96,128]{1,0:T(8,128)S(1)} %get-tuple-element.45), channel_id=1, source_target_pairs={{1,2},{2,1},{3,4},{4,3},{5,6},{6,5},{7,8},{8,7},{9,10},{10,9},{11,... | collective-permute-start | bytes 147464 | tf_op jit(solution)/shard_map/ppermute | solution.py:507
  8.9 1.2 %collective-permute-start.4 = (f32[8,6912]{1,0:T(8,128)S(1)}, f32[8,6912]{1,0:T(8,128)S(1)}, u32[]{:S(2)}, u32[]{:S(2)}) collective-permute-start(f32[8,6912]{1,0:T(8,128)S(1)} %get-tuple-element.53), channel_id=1, source_target_pairs={{0,16},{16,0},{32,48},{48,32},{64,80},{80,64},{96,112},{112,96},{1... | collective-permute-start | bytes 663560 | tf_op jit(solution)/shard_map/ppermute | solution.py:509
  10.2 3.0 %collective-permute-start.5 = (f32[8,6912]{1,0:T(8,128)S(1)}, f32[8,6912]{1,0:T(8,128)S(1)}, u32[]{:S(2)}, u32[]{:S(2)}) collective-permute-start(f32[8,6912]{1,0:T(8,128)S(1)} %get-tuple-element.54), channel_id=1, source_target_pairs={{16,32},{32,16},{48,64},{64,48},{80,96},{96,80},{17,33},{33,17},{4... | collective-permute-start | bytes 663560 | tf_op jit(solution)/shard_map/ppermute | solution.py:508
  13.2 0.0 copy-start
  13.2 0.0 copy-start.1
  13.2 0.6 %copy-done = f32[96]{0:T(128)S(1)} copy-done((f32[96]{0:T(128)S(1)}, f32[96]{0:T(128)}, u32[]{:S(2)}) %copy-start) | copy-done | bytes 408
  13.8 0.0 copy-done.1
  13.9 1.5 %shard_map.50 = (f32[2,96,128]{2,1,0:T(8,128)S(1)}, f32[2,21,16,256]{3,2,1,0:T(8,128)S(1)}, bf16[96,256]{1,0:T(8,128)(2,1)S(1)}, f32[96,128]{1,0:T(8,128)S(1)}, ...) custom-call(f32[1,96]{1,0:T(1,128)S(1)} %bitcast.3, s32[2,96]{1,0:T(2,128)S(1)} %copy-done.1, ...), custom_call_target="tpu_custom_call" | custom-call | flops 4000000000 | bytes 1048576 | tf_op jit(solution)/shard_map/pallas_call | solution.py:469
  15.4 0.0 collective-permute-done.znear
  15.4 0.0 collective-permute-done.1.zfar
  15.4 0.1 shard_map.48
  15.5 2.5 %collective-permute-start.2 = (f32[8,256]{1,0:T(8,128)S(1)}, f32[8,256]{1,0:T(8,128)S(1)}, u32[]{:S(2)}, u32[]{:S(2)}) collective-permute-start(f32[8,256]{1,0:T(8,128)S(1)} %get-tuple-element.46), channel_id=1, source_target_pairs={{16,32},{32,16},{48,64},{64,48},{80,96},{96,80},{17,33},{33,17},{4... | collective-permute-start | bytes 24584 | tf_op jit(solution)/shard_map/ppermute | solution.py:541
  18.0 0.1 collective-permute-start.3
  18.1 0.0 collective-permute-done.4.ynear
  18.1 0.0 collective-permute-done.5.yfar
  18.1 2.1 %shard_map.51 = (f32[2,128]{1,0:T(2,128)S(1)}, f32[21,16,256]{2,1,0:T(8,128)S(1)}, bf16[21,16,768]{2,1,0:T(8,128)(2,1)S(1)}, bf16[15,16,768]{2,1,0:T(8,128)(2,1)S(1)}, f32[2,21,16,256]{3,2,1,0:T(8,128)S(1)}) custom-call(bf16[21,96,768]{2,1,0:T(8,128)(2,1)S(1)} %get-tuple-element.51.fh, bf16[15,96,768]{2,1,0:T(8,128)(2,1)S(1)} %get-tuple-element.52.fl, ...), custom_call_target="tpu_custom_call" | custom-call | flops 4000000000 | bytes 1048576 | tf_op jit(solution)/shard_map/pallas_call | solution.py:469
  20.3 0.2 collective-permute-done.2.far_ref
  20.4 0.0 collective-permute-done.3.near_ref
  20.4 0.7 %shard_map.52 = f32[16,2,96]{2,1,0:T(2,128)S(1)} custom-call(f32[8,256]{1,0:T(8,128)S(1)} %collective-permute-done.2.far_ref, f32[8,256]{1,0:T(8,128)S(1)} %collective-permute-done.3.near_ref, f32[2,128]{1,0:T(2,128)S(1)} %get-tuple-element.61.sums_in, f32[2,21,16,256]{3,2,1,0:T(8,128)S(1)} %get-tuple-element.62.part_inner, ...), custom_call_target="tpu_custom_call" | custom-call | flops 4000000000 | bytes 1048576 | tf_op jit(solution)/shard_map/pallas_call | solution.py:469
  21.2 10.6 %all_to_all.5 = f32[16,2,96]{2,1,0:T(2,128)S(1)} all-to-all(f32[16,2,96]{2,1,0:T(2,128)S(1)} %shard_map.52), channel_id=1, replica_groups=mesh['gy'=8,'gz'=16] {'gz'}, dimensions={0} | all-to-all | bytes 24576 | tf_op jit(solution)/shard_map/all_to_all | solution.py:593
  31.8 0.5 %fusion = f32[96]{0:T(128)} fusion(f32[2,96]{1,0:T(2,128)S(1)} %reduce_sum.9), kind=kLoop, calls=%fused_computation.1 | loop fusion | flops 384 | bytes 1152 | tf_op jit(solution)/shard_map/div | solution.py:595
  (2 shorter events, 0.0 us)
Async XLA Ops:
  3.9 11.5 %collective-permute-start = (f32[96,128]{1,0:T(8,128)S(1)}, f32[96,128]{1,0:T(8,128)S(1)}, u32[]{:S(2)}, u32[]{:S(2)}) collective-permute-start(f32[96,128]{1,0:T(8,128)S(1)} %get-tuple-element.44), channel_id=1, source_target_pairs={{0,1},{1,0},{2,3},{3,2},{4,5},{5,4},{6,7},{7,6},{8,9},{9,8},{10,11... | collective-permute-start | bytes 147464 | tf_op jit(solution)/shard_map/ppermute | solution.py:506
  4.2 11.2 %collective-permute-start.1 = (f32[96,128]{1,0:T(8,128)S(1)}, f32[96,128]{1,0:T(8,128)S(1)}, u32[]{:S(2)}, u32[]{:S(2)}) collective-permute-start(f32[96,128]{1,0:T(8,128)S(1)} %get-tuple-element.45), channel_id=1, source_target_pairs={{1,2},{2,1},{3,4},{4,3},{5,6},{6,5},{7,8},{8,7},{9,10},{10,9},{11,... | collective-permute-start | bytes 147464 | tf_op jit(solution)/shard_map/ppermute | solution.py:507
  8.9 9.2 %collective-permute-start.4 = (f32[8,6912]{1,0:T(8,128)S(1)}, f32[8,6912]{1,0:T(8,128)S(1)}, u32[]{:S(2)}, u32[]{:S(2)}) collective-permute-start(f32[8,6912]{1,0:T(8,128)S(1)} %get-tuple-element.53), channel_id=1, source_target_pairs={{0,16},{16,0},{32,48},{48,32},{64,80},{80,64},{96,112},{112,96},{1... | collective-permute-start | bytes 663560 | tf_op jit(solution)/shard_map/ppermute | solution.py:509
  10.2 8.0 %collective-permute-start.5 = (f32[8,6912]{1,0:T(8,128)S(1)}, f32[8,6912]{1,0:T(8,128)S(1)}, u32[]{:S(2)}, u32[]{:S(2)}) collective-permute-start(f32[8,6912]{1,0:T(8,128)S(1)} %get-tuple-element.54), channel_id=1, source_target_pairs={{16,32},{32,16},{48,64},{64,48},{80,96},{96,80},{17,33},{33,17},{4... | collective-permute-start | bytes 663560 | tf_op jit(solution)/shard_map/ppermute | solution.py:508
  13.2 0.7 %copy-start = (f32[96]{0:T(128)S(1)}, f32[96]{0:T(128)}, u32[]{:S(2)}) copy-start(f32[96]{0:T(128)} %param.6) | copy-start | bytes 1156
  13.2 0.7 %copy-start.1 = (s32[2,96]{1,0:T(2,128)S(1)}, s32[2,96]{1,0:T(2,128)}, u32[]{:S(2)}) copy-start(s32[2,96]{1,0:T(2,128)} %reach_ref.1) | copy-start | bytes 2308
  15.5 5.0 %collective-permute-start.2 = (f32[8,256]{1,0:T(8,128)S(1)}, f32[8,256]{1,0:T(8,128)S(1)}, u32[]{:S(2)}, u32[]{:S(2)}) collective-permute-start(f32[8,256]{1,0:T(8,128)S(1)} %get-tuple-element.46), channel_id=1, source_target_pairs={{16,32},{32,16},{48,64},{64,48},{80,96},{96,80},{17,33},{33,17},{4... | collective-permute-start | bytes 24584 | tf_op jit(solution)/shard_map/ppermute | solution.py:541
  18.0 2.4 %collective-permute-start.3 = (f32[8,256]{1,0:T(8,128)S(1)}, f32[8,256]{1,0:T(8,128)S(1)}, u32[]{:S(2)}, u32[]{:S(2)}) collective-permute-start(f32[8,256]{1,0:T(8,128)S(1)} %get-tuple-element.47), channel_id=1, source_target_pairs={{0,16},{16,0},{32,48},{48,32},{64,80},{80,64},{96,112},{112,96},{1... | collective-permute-start | bytes 24584 | tf_op jit(solution)/shard_map/ppermute | solution.py:542
